TPU v7x, 256 devices: a whole 4x4x8 slice. The times are simulated.
256 devices in a mesh: row: 16 (over y, z_lo), col: 16 (over x, z_hi, core).
Axes of the slice: x: 4, y: 4, z: 8 (z_hi: 2, z_lo: 4; z = z_hi * 4 + z_lo), core: 2. Of those that a mesh axis runs over, the one named last changes fastest.
Arguments:
- tokens: bfloat16 [2048, 4096], P('row', 'col'), may hold values from -6 to 6
- cotangent: bfloat16 [2048, 4096], P('row', 'col'), may hold values from -6 to 6
- gate_weight: bfloat16 [4096, 14336], P('row', 'col'), may hold values from -0.125 to 0.125
- up_weight: bfloat16 [4096, 14336], P('row', 'col'), may hold values from -0.125 to 0.125
- down_weight: bfloat16 [14336, 4096], P('col', 'row'), may hold values from -0.0625 to 0.0625
- gate_mask: int32 [32, 112], P(None, 'col'), may hold values from 0 to 1, as said below
- up_mask: int32 [32, 112], P(None, 'col'), may hold values from 0 to 1, as said below
- down_mask: int32 [112, 32], P('col'), may hold values from 0 to 1, as said below
Outputs:
- output: bfloat16 [2048, 4096], P('row', 'col')
- input_grad: bfloat16 [2048, 4096], P('row', 'col')
- gate_grad: bfloat16 [4096, 14336], P('row', 'col')
- up_grad: bfloat16 [4096, 14336], P('row', 'col')
- down_grad: bfloat16 [14336, 4096], P('col', 'row')
Inputs may be any that keep to these rules, and one draw needn't show every extreme that they name: `gate_mask`: blocks of 2 x 7 aligned with the tiles of one device hold between 5 and 7 ones each, and some tile holds exactly 7. `up_mask`: blocks of 2 x 7 aligned with the tiles of one device hold between 5 and 7 ones each, and some tile holds exactly 7. `down_mask`: blocks of 7 x 2 aligned with the tiles of one device hold between 5 and 7 ones each, and some tile holds exactly 7.
All inputs are finite; a program needn't handle non-finite values.
Results may differ from a plain program's by a relative error of at most 0.017.
Values may be sent and summed in bfloat16 or wider, within the bound.
No kernel may reach another device: no remote copies, remote signals or barrier semaphores. Data moves between devices by JAX's collectives and lax.ppermute only.
A program may use at most 128 MiB of HBM per device.

v0:
```python
import jax
import jax.numpy as jnp
from jax import lax
from jax.sharding import PartitionSpec as P

BLK = 128


def tile_picks(tiles, capacity):
    tile_count = tiles.shape[0]
    flat = tiles.reshape(tile_count, -1)
    order = jnp.argsort(1 - flat, axis=1, stable=True)[:, :capacity]
    scale = jnp.take_along_axis(flat, order, axis=1)
    return (order, scale)


def compact(weight, rows_blk, cols_blk, own_order, own_scale):
    block_size = weight.shape[0] // rows_blk
    cells = rows_blk * cols_blk
    tile_blocks = weight.reshape(rows_blk, block_size, cols_blk, block_size).transpose(0, 2, 1, 3)
    tile_blocks = tile_blocks.reshape(cells, block_size, block_size)
    select = (own_order[:, None] == jnp.arange(cells, dtype=jnp.int32)[None, :]).astype(
        weight.dtype
    )
    select = select * own_scale[:, None].astype(weight.dtype)
    chosen = jnp.einsum("pn,nbc->pbc", select, tile_blocks, preferred_element_type=jnp.float32)
    return chosen.astype(weight.dtype)


def panel_product(
    pattern, panel_blocks, source_idx, source_count, target_idx, target_count, operand_blocks
):
    source_pick = (
        source_idx[:, None] == jnp.arange(source_count, dtype=jnp.int32)[None, :]
    ).astype(operand_blocks.dtype)
    selected = jnp.einsum(
        "tmb,nm->tnb", operand_blocks, source_pick, preferred_element_type=jnp.float32
    ).astype(operand_blocks.dtype)
    product = jnp.einsum(pattern, selected, panel_blocks, preferred_element_type=jnp.float32)
    target_pick = (
        target_idx[:, None] == jnp.arange(target_count, dtype=jnp.int32)[None, :]
    ).astype(jnp.float32)
    return jnp.einsum("ntc,nk->tkc", product, target_pick, precision=lax.Precision.HIGHEST)


def tile_grad(left_all, right_all, rows_blk, cols_blk, order, scale, block_size):
    token_count = left_all.shape[0]
    cells = rows_blk * cols_blk
    left_blocks = left_all.reshape(token_count, rows_blk, block_size)
    right_blocks = right_all.reshape(token_count, cols_blk, block_size)
    left_pick = (
        (order // cols_blk)[:, None] == jnp.arange(rows_blk, dtype=jnp.int32)[None, :]
    ).astype(left_all.dtype)
    right_pick = (
        (order % cols_blk)[:, None] == jnp.arange(cols_blk, dtype=jnp.int32)[None, :]
    ).astype(right_all.dtype)
    left_sel = jnp.einsum(
        "trb,pr->tpb", left_blocks, left_pick, preferred_element_type=jnp.float32
    ).astype(left_all.dtype)
    right_sel = jnp.einsum(
        "trb,pr->tpb", right_blocks, right_pick, preferred_element_type=jnp.float32
    ).astype(right_all.dtype)
    grads = jnp.einsum("tnp,tnq->npq", left_sel, right_sel, preferred_element_type=jnp.float32)
    grads = grads * scale.astype(jnp.float32)[:, None, None]
    place = (order[:, None] == jnp.arange(cells, dtype=jnp.int32)[None, :]).astype(jnp.float32)
    dense = jnp.einsum("pn,paq->naq", place, grads, precision=lax.Precision.HIGHEST)
    dense = dense.reshape(rows_blk, cols_blk, block_size, block_size).transpose(0, 2, 1, 3)
    return dense.reshape(rows_blk * block_size, cols_blk * block_size).astype(jnp.bfloat16)


def body(tokens, cotangent, gate_weight, up_weight, down_weight, gate_mask, up_mask, down_mask):
    block_size = BLK
    rows_blk = gate_weight.shape[0] // block_size
    cols_blk = gate_weight.shape[1] // block_size
    row_count = lax.axis_size("row")
    row_index = lax.axis_index("row")
    capacity = rows_blk * cols_blk // 2
    tok_rows = tokens.shape[0]
    local_width = gate_weight.shape[1]
    full_tokens, full_cotangent = (
        lax.all_gather(tokens, "col", axis=1, tiled=True),
        lax.all_gather(cotangent, "col", axis=1, tiled=True),
    )
    model_width = full_tokens.shape[1]
    width_blocks = model_width // block_size
    gate_order, gate_scale = tile_picks(gate_mask.reshape(row_count, rows_blk, cols_blk), capacity)
    up_order, up_scale = tile_picks(up_mask.reshape(row_count, rows_blk, cols_blk), capacity)
    down_tiles = down_mask.reshape(cols_blk, row_count, rows_blk).transpose(1, 0, 2)
    down_order, down_scale = tile_picks(down_tiles, capacity)

    def own(values):
        return lax.dynamic_index_in_dim(values, row_index, 0, keepdims=False)

    gate_blocks = compact(gate_weight, rows_blk, cols_blk, own(gate_order), own(gate_scale))
    up_blocks = compact(up_weight, rows_blk, cols_blk, own(up_order), own(up_scale))
    down_blocks = compact(down_weight, cols_blk, rows_blk, own(down_order), own(down_scale))
    gate_panel, up_panel, down_panel = (
        lax.all_gather(gate_blocks, "row", axis=0, tiled=True),
        lax.all_gather(up_blocks, "row", axis=0, tiled=True),
        lax.all_gather(down_blocks, "row", axis=0, tiled=True),
    )
    slot_source = jnp.arange(row_count * capacity, dtype=jnp.int32) // capacity
    gate_flat = gate_order.reshape(-1)
    up_flat = up_order.reshape(-1)
    down_flat = down_order.reshape(-1)
    gate_drow = slot_source * rows_blk + gate_flat // cols_blk
    gate_ccol = gate_flat % cols_blk
    up_drow = slot_source * rows_blk + up_flat // cols_blk
    up_ccol = up_flat % cols_blk
    down_frow = down_flat // rows_blk
    down_dcol = slot_source * rows_blk + down_flat % rows_blk
    token_blocks = full_tokens.reshape(tok_rows, width_blocks, block_size)
    gate = panel_product(
        "tnb,nbc->ntc", gate_panel, gate_drow, width_blocks, gate_ccol, cols_blk, token_blocks
    ).reshape(tok_rows, local_width)
    up = panel_product(
        "tnb,nbc->ntc", up_panel, up_drow, width_blocks, up_ccol, cols_blk, token_blocks
    ).reshape(tok_rows, local_width)
    sig = jax.nn.sigmoid(gate)
    silu_gate = gate * sig
    hidden = (silu_gate * up).astype(jnp.bfloat16)
    hidden_blocks = hidden.reshape(tok_rows, cols_blk, block_size)
    out_term = panel_product(
        "tnb,nbc->ntc", down_panel, down_frow, cols_blk, down_dcol, width_blocks, hidden_blocks
    ).reshape(tok_rows, model_width)
    output = lax.psum_scatter(out_term.astype(jnp.bfloat16), "col", scatter_dimension=1, tiled=True)
    tokens_all, cot_all = (
        lax.all_to_all(full_tokens, "row", split_axis=1, concat_axis=0, tiled=True),
        lax.all_to_all(full_cotangent, "row", split_axis=1, concat_axis=0, tiled=True),
    )
    cot_blocks = full_cotangent.reshape(tok_rows, width_blocks, block_size)
    hidden_grad = panel_product(
        "tnc,nbc->ntb", down_panel, down_dcol, width_blocks, down_frow, cols_blk, cot_blocks
    ).reshape(tok_rows, local_width)
    gate_act_grad = (hidden_grad * up * sig * (1.0 + gate * (1.0 - sig))).astype(jnp.bfloat16)
    up_act_grad = (hidden_grad * silu_gate).astype(jnp.bfloat16)
    gate_act_blocks = gate_act_grad.reshape(tok_rows, cols_blk, block_size)
    up_act_blocks = up_act_grad.reshape(tok_rows, cols_blk, block_size)
    grad_term = panel_product(
        "tnc,nbc->ntb", gate_panel, gate_ccol, cols_blk, gate_drow, width_blocks, gate_act_blocks
    )
    grad_term = grad_term + panel_product(
        "tnc,nbc->ntb", up_panel, up_ccol, cols_blk, up_drow, width_blocks, up_act_blocks
    )
    input_grad = lax.psum_scatter(
        grad_term.reshape(tok_rows, model_width).astype(jnp.bfloat16),
        "col",
        scatter_dimension=1,
        tiled=True,
    )
    hidden_all, gate_act_all, up_act_all = (
        lax.all_gather(hidden, "row", axis=0, tiled=True),
        lax.all_gather(gate_act_grad, "row", axis=0, tiled=True),
        lax.all_gather(up_act_grad, "row", axis=0, tiled=True),
    )
    gate_grad = tile_grad(
        tokens_all, gate_act_all, rows_blk, cols_blk, own(gate_order), own(gate_scale), block_size
    )
    up_grad = tile_grad(
        tokens_all, up_act_all, rows_blk, cols_blk, own(up_order), own(up_scale), block_size
    )
    down_grad = tile_grad(
        hidden_all, cot_all, cols_blk, rows_blk, own(down_order), own(down_scale), block_size
    )
    return (output, input_grad, gate_grad, up_grad, down_grad)


def solution(mesh):
    return jax.shard_map(
        body,
        mesh=mesh,
        in_specs=(
            P("row", "col"),
            P("row", "col"),
            P("row", "col"),
            P("row", "col"),
            P("col", "row"),
            P(None, "col"),
            P(None, "col"),
            P("col", None),
        ),
        out_specs=(
            P("row", "col"),
            P("row", "col"),
            P("row", "col"),
            P("row", "col"),
            P("col", "row"),
        ),
        check_vma=False,
    )
```

profile of v0, /device:TPU:34, one launch (start us, length us, event | category | flops | bytes accessed | tf_op | source)
XLA Modules:
  0.0 941.0 jit_solution(3454512349592678602)
XLA Ops:
  10.5 1.7 gather_fusion.2
  13.6 1.7 gather_fusion.1
  18.4 1.7 gather_fusion
  28.8 39.2 %all-gather.9.cloned.1.call-done = bf16[128,4096]{1,0:T(8,128)(2,1)} async-done(((bf16[128,256]{1,0:T(8,128)(2,1)}), bf16[128,4096]{1,0:T(8,128)(2,1)}) %all-gather.9.cloned.1.call-update) | async-done | bytes 1048592 | tf_op jit(solution)/shard_map/all_gather | solution.py:81
  68.0 1.4 copy.226
  69.4 52.7 %all-gather.17.cloned.1.call-done = bf16[128,4096]{1,0:T(8,128)(2,1)} async-done(((bf16[128,256]{1,0:T(8,128)(2,1)}), bf16[128,4096]{1,0:T(8,128)(2,1)}) %all-gather.17.cloned.1.call-update) | async-done | bytes 1048592 | tf_op jit(solution)/shard_map/all_gather | solution.py:82
  122.2 1.5 copy.228
  123.6 3.0 convert_bitcast_fusion.10
  126.7 3.0 convert_bitcast_fusion.11
  129.7 2.9 convert_bitcast_fusion.8
  132.6 82.8 %all-gather.13.cloned.1.call-done = bf16[112,128,128]{2,1,0:T(8,128)(2,1)} async-done(((bf16[7,128,128]{2,1,0:T(8,128)(2,1)}), bf16[112,128,128]{2,1,0:T(8,128)(2,1)}) %all-gather.13.cloned.1.call-update) | async-done | bytes 3670032 | tf_op jit(solution)/shard_map/all_gather | solution.py:99
  215.4 4.3 fusion.29
  219.8 6.6 fusion.41
  226.8 83.7 %all-gather.11.cloned.1.call-done = bf16[112,128,128]{2,1,0:T(8,128)(2,1)} async-done(((bf16[7,128,128]{2,1,0:T(8,128)(2,1)}), bf16[112,128,128]{2,1,0:T(8,128)(2,1)}) %all-gather.11.cloned.1.call-update) | async-done | bytes 3670032 | tf_op jit(solution)/shard_map/all_gather | solution.py:98
  310.5 4.3 fusion.31
  314.8 6.6 fusion.38
  321.6 83.9 %all-gather.15.cloned.1.call-done = bf16[112,128,128]{2,1,0:T(8,128)(2,1)} async-done(((bf16[7,128,128]{2,1,0:T(8,128)(2,1)}), bf16[112,128,128]{2,1,0:T(8,128)(2,1)}) %all-gather.15.cloned.1.call-update) | async-done | bytes 3670032 | tf_op jit(solution)/shard_map/all_gather | solution.py:100
  405.5 5.8 fusion.25
  411.4 7.0 fusion.44
  419.3 2.2 fusion.76
  424.4 7.5 all-to-all-start
  431.9 2.3 copy.206
  434.1 31.7 %all-to-all-done = bf16[128,16,256]{0,2,1:T(8,128)(2,1)S(1)} async-done(((bf16[128,16,256]{0,2,1:T(8,128)(2,1)}), bf16[128,16,256]{0,2,1:T(8,128)(2,1)S(1)}, u32[]{:S(2)}, u32[]{:S(2)}) %all-to-all-start) | async-done | bytes 1048608 | tf_op jit(solution)/shard_map/all_to_all | solution.py:128
  465.8 16.7 %all-to-all-start.1 = ((bf16[128,16,256]{0,2,1:T(8,128)(2,1)}), bf16[128,16,256]{0,2,1:T(8,128)(2,1)}, u32[]{:S(2)}, u32[]{:S(2)}) async-start(bf16[128,16,256]{0,2,1:T(8,128)(2,1)} %bitcast.220), calls=%async_computation.3 | async-start | bytes 2097152 | tf_op jit(solution)/shard_map/all_to_all | solution.py:129
  485.7 33.2 %all-to-all-done.1 = bf16[128,16,256]{0,2,1:T(8,128)(2,1)} async-done(((bf16[128,16,256]{0,2,1:T(8,128)(2,1)}), bf16[128,16,256]{0,2,1:T(8,128)(2,1)}, u32[]{:S(2)}, u32[]{:S(2)}) %all-to-all-start.1) | async-done | bytes 1048608 | tf_op jit(solution)/shard_map/all_to_all | solution.py:129
  518.9 2.3 copy.220
  521.2 2.2 reshape.480
  523.4 3.5 convert_bitcast_fusion.5
  526.9 3.5 convert_bitcast_fusion.3
  530.5 3.6 convert_bitcast_fusion
  536.5 6.8 fusion.35
  544.7 3.1 convert_bitcast_fusion.6
  548.1 5.8 fusion.21
  555.1 6.8 fusion
  561.9 2.7 fusion.23
  564.6 7.3 add_convert_fusion
  573.4 6.7 copy.192
  580.0 84.4 %all-gather.21.cloned.1.call-done = bf16[2048,896]{0,1:T(8,128)(2,1)} async-done(((bf16[128,896]{0,1:T(8,128)(2,1)}), bf16[2048,896]{0,1:T(8,128)(2,1)}) %all-gather.21.cloned.1.call-update) | async-done | bytes 3670032 | tf_op jit(solution)/shard_map/all_gather | solution.py:154
  664.4 6.5 copy.199
  670.9 3.6 convert_bitcast_fusion.4
  676.7 2.3 fusion.47
  679.0 2.3 fusion.52
  685.7 85.2 %all-gather.23.cloned.1.call-done = bf16[2048,896]{0,1:T(8,128)(2,1)} async-done(((bf16[128,896]{0,1:T(8,128)(2,1)}), bf16[2048,896]{0,1:T(8,128)(2,1)}) %all-gather.23.cloned.1.call-update) | async-done | bytes 3670032 | tf_op jit(solution)/shard_map/all_gather | solution.py:152
  771.0 6.7 copy.205
  777.7 3.6 convert_bitcast_fusion.1
  781.3 2.3 fusion.57
  786.0 66.9 %reduce-scatter.3.cloned.1.call-done = bf16[128,256]{1,0:T(8,128)(2,1)} async-done(((bf16[128,4096]{1,0:T(8,128)(2,1)}), bf16[128,256]{1,0:T(8,128)(2,1)}) %reduce-scatter.3.cloned.1.call-update) | async-done | bytes 65552 | tf_op jit(solution)/shard_map/reduce_scatter | solution.py:126
  852.8 81.1 %reduce-scatter.5.cloned.1.call-done = bf16[128,256]{1,0:T(8,128)(2,1)} async-done(((bf16[128,4096]{1,0:T(8,128)(2,1)}), bf16[128,256]{1,0:T(8,128)(2,1)}) %reduce-scatter.5.cloned.1.call-update) | async-done | bytes 65552 | tf_op jit(solution)/shard_map/reduce_scatter | solution.py:145
  (180 shorter events, 39.4 us)
Async XLA Ops:
  7.2 60.8 %all-gather.9.cloned.1.call-start = ((), (), s32[]{:S(2)}) async-start(), calls=%async_computation.4 | async-start | bytes 1114112 | tf_op jit(solution)/shard_map/all_gather | solution.py:81
  7.9 114.3 %all-gather.17.cloned.1.call-start = ((), (), s32[]{:S(2)}) async-start(), calls=%async_computation.9 | async-start | bytes 1114112 | tf_op jit(solution)/shard_map/all_gather | solution.py:82
  8.7 206.8 %all-gather.13.cloned.1.call-start = ((), (), s32[]{:S(2)}) async-start(), calls=%async_computation.6 | async-start | bytes 3899392 | tf_op jit(solution)/shard_map/all_gather | solution.py:99
  10.5 1.9 copy-start.23
  13.6 1.9 copy-start.9
  13.6 3.7 copy-start.24
  18.4 3.6 copy-start.10
  20.1 5.0 copy-start.8
  20.6 1.4 copy-start.11
  21.9 288.5 %all-gather.11.cloned.1.call-start = ((), (), s32[]{:S(2)}) async-start(), calls=%async_computation.5 | async-start | bytes 3899392 | tf_op jit(solution)/shard_map/all_gather | solution.py:98
  24.0 44.0 %copy-start.13 = (s32[7]{0:T(128)}, s32[7]{0:T(128)S(1)}, u32[]{:S(2)}) copy-start(s32[7]{0:T(128)S(1)} %dynamic-slice_reduce_fusion.2) | copy-start | bytes 88
  25.1 380.4 %all-gather.15.cloned.1.call-start = ((), (), s32[]{:S(2)}) async-start(), calls=%async_computation.7 | async-start | bytes 3899392 | tf_op jit(solution)/shard_map/all_gather | solution.py:100
  26.7 546.7 %all-gather.19.cloned.1.call-start = ((), (), s32[]{:S(2)}) async-start(), calls=%async_computation.11 | async-start | bytes 3899392 | tf_op jit(solution)/shard_map/all_gather | solution.py:153
  28.7 101.0 %copy-start.25 = (s32[112]{0:T(128)}, s32[112]{0:T(128)S(1)}, u32[]{:S(2)}) copy-start(s32[112]{0:T(128)S(1)} %get-tuple-element.46) | copy-start | bytes 1348
  28.8 97.9 %copy-start.15 = (s32[112]{0:T(128)}, s32[112]{0:T(128)S(1)}, u32[]{:S(2)}) copy-start(s32[112]{0:T(128)S(1)} %get-tuple-element.51) | copy-start | bytes 1348
  28.8 97.9 %copy-start.21 = (s32[112]{0:T(128)}, s32[112]{0:T(128)S(1)}, u32[]{:S(2)}) copy-start(s32[112]{0:T(128)S(1)} %get-tuple-element.52) | copy-start | bytes 1348
  28.8 191.0 %copy-start.17 = (s32[112]{0:T(128)}, s32[112]{0:T(128)S(1)}, u32[]{:S(2)}) copy-start(s32[112]{0:T(128)S(1)} %get-tuple-element.50) | copy-start | bytes 1348
  28.8 286.0 %copy-start.19 = (s32[112]{0:T(128)}, s32[112]{0:T(128)S(1)}, u32[]{:S(2)}) copy-start(s32[112]{0:T(128)S(1)} %get-tuple-element.53) | copy-start | bytes 1348
  405.5 5.8 copy-start.27
  411.4 11.7 %copy-start.6 = (bf16[128,4096]{1,0:T(8,128)(2,1)S(1)}, bf16[128,4096]{1,0:T(8,128)(2,1)}, u32[]{:S(2)}) copy-start(bf16[128,4096]{1,0:T(8,128)(2,1)} %all-gather.9.cloned.1.call-done) | copy-start | bytes 3145732
  421.5 242.9 %all-gather.21.cloned.1.call-start = ((), (), s32[]{:S(2)}) async-start(), calls=%async_computation.12 | async-start | bytes 3899392 | tf_op jit(solution)/shard_map/all_gather | solution.py:154
  422.3 348.7 %all-gather.23.cloned.1.call-start = ((), (), s32[]{:S(2)}) async-start(), calls=%async_computation.13 | async-start | bytes 3899392 | tf_op jit(solution)/shard_map/all_gather | solution.py:152
  423.0 59.9 %copy-start.14 = (s32[7]{0:T(128)S(1)}, s32[7]{0:T(128)}, u32[]{:S(2)}) copy-start(s32[7]{0:T(128)} %copy-done.13) | copy-start | bytes 88
  423.0 60.0 %copy-start.12 = (s32[7]{0:T(128)S(1)}, s32[7]{0:T(128)}, u32[]{:S(2)}) copy-start(s32[7]{0:T(128)} %copy-done.11) | copy-start | bytes 88
  424.4 41.4 %all-to-all-start = ((bf16[128,16,256]{0,2,1:T(8,128)(2,1)}), bf16[128,16,256]{0,2,1:T(8,128)(2,1)S(1)}, u32[]{:S(2)}, u32[]{:S(2)}) async-start(bf16[128,16,256]{0,2,1:T(8,128)(2,1)} %bitcast.221), calls=%async_computation.2 | async-start | bytes 2097152 | tf_op jit(solution)/shard_map/all_to_all | solution.py:128
  465.8 53.1 %all-to-all-start.1 = ((bf16[128,16,256]{0,2,1:T(8,128)(2,1)}), bf16[128,16,256]{0,2,1:T(8,128)(2,1)}, u32[]{:S(2)}, u32[]{:S(2)}) async-start(bf16[128,16,256]{0,2,1:T(8,128)(2,1)} %bitcast.220), calls=%async_computation.3 | async-start | bytes 2097152 | tf_op jit(solution)/shard_map/all_to_all | solution.py:129
  482.5 370.3 %reduce-scatter.3.cloned.1.call-start = ((), (), s32[]{:S(2)}) async-start(), calls=%async_computation.8 | async-start | bytes 1114112 | tf_op jit(solution)/shard_map/reduce_scatter | solution.py:126
  523.4 7.1 copy-start.7
  526.9 7.2 copy-start.28
  530.5 4.8 copy-start.2
  535.3 1.2 copy-start.26
  536.5 8.3 copy-start.18
  547.8 6.1 copy-start.20
  547.8 386.1 %reduce-scatter.5.cloned.1.call-start = ((), (), s32[]{:S(2)}) async-start(), calls=%async_computation.10 | async-start | bytes 1114112 | tf_op jit(solution)/shard_map/reduce_scatter | solution.py:145
  553.9 1.2 copy-start.16
  555.1 6.8 copy-start.1
  561.9 2.7 copy-start.22
  670.9 3.6 copy-start
  674.5 2.2 copy-start.5
  676.7 2.3 copy-start.4
  777.7 3.7 copy-start.3
Sparse Core Ops, SparseCore 0:
  10.5 57.3 all-gather.8
  70.5 51.6 all-gather.16
  124.5 90.8 all-gather.12
  217.7 92.7 all-gather.10
  312.7 92.7 all-gather.14
  421.6 130.6 all-gather.18
  554.6 109.7 all-gather.20
  666.1 104.7 all-gather.22
  775.6 77.1 reduce-scatter.2
  857.9 75.9 reduce-scatter.4
where the time goes:
time: 949 us; the launch traced here: 941 us
  waiting for transfers between devices  728 us (77%)
  matrix products  109 us (11%)
  local copies, waits for them, and re-layouts  57.9 us (6%)
  starting transfers between devices  25 us (3%)
  between operations  15.2 us (2%)
    all_gather x1, waiting for transfers between devices, body(): lax.all_gather(hidden, 'row', axis=0, tiled=True)  85.2 us
    all_gather x1, waiting for transfers between devices, body(): lax.all_gather(up_act_grad, 'row', axis=0, tiled=True)  84.4 us
    all_gather x1, waiting for transfers between devices, body(): lax.all_gather(down_blocks, 'row', axis=0, tiled=True)  83.9 us
    all_gather x1, waiting for transfers between devices, body(): lax.all_gather(gate_blocks, 'row', axis=0, tiled=True)  83.7 us
    all_gather x1, waiting for transfers between devices, body(): lax.all_gather(up_blocks, 'row', axis=0, tiled=True)  82.8 us
    reduce_scatter x1, waiting for transfers between devices, body(): lax.psum_scatter(grad_term.reshape(tok_rows, model_width).astype(jnp.bflo...  81.1 us
    reduce_scatter x1, waiting for transfers between devices, body(): lax.psum_scatter(out_term.astype(jnp.bfloat16), 'col', scatter_dimension=...  66.9 us
    all_gather x1, waiting for transfers between devices, body(): lax.all_gather(cotangent, 'col', axis=1, tiled=True)  52.7 us
  transfers between devices with their start and end apart: 12, of which 11 were waited for; matrix products, arithmetic and copies ran while one was open for 17% of the time, Pallas kernels for 0%

commit v1 on v0

v1 whole, which is shorter than its diff:
```python
import jax
import jax.numpy as jnp
from jax import lax
from jax.experimental import pallas as pl
from jax.experimental.pallas import tpu as pltpu
from jax.sharding import Mesh, PartitionSpec as P

B = 128
VM = pl.BlockSpec(memory_space=pltpu.VMEM)
SM = pl.BlockSpec(memory_space=pltpu.SMEM)
BF = jnp.bfloat16
F32 = jnp.float32


def sds(shape, dtype=BF):
    return jax.ShapeDtypeStruct(shape, dtype)


def call(kernel, specs, args, outs, scratch=(), flops=0, mib=40):
    nbytes = sum(a.size * a.dtype.itemsize for a in list(args) + list(outs))
    return pl.pallas_call(
        kernel,
        out_shape=tuple(outs),
        in_specs=[SM if s else VM for s in specs],
        out_specs=tuple(VM for _ in outs),
        scratch_shapes=list(scratch),
        compiler_params=pltpu.CompilerParams(vmem_limit_bytes=mib * 1024 * 1024),
        cost_estimate=pl.CostEstimate(flops=flops, bytes_accessed=nbytes, transcendentals=0),
    )(*args)


def cells(mask, tile, down):
    slot = jnp.int32(0)
    for cc in range(7):
        for rr in range(2):
            on = mask[cc, 2 * tile + rr] if down else mask[2 * tile + rr, cc]
            yield rr, cc, on == 1, jnp.minimum(slot, 6)
            slot = slot + on
    yield None, None, slot, None


def sub(rr, cc, down):
    a, b = (cc, rr) if down else (rr, cc)
    return pl.ds(a * B, B), pl.ds(b * B, B)


def pack(mask, tile, down, source, out, base):
    for rr, cc, on, slot in cells(mask, tile, down):
        if rr is None:
            for p in range(5, 7):

                @pl.when(on <= p)
                def _(p=p):
                    out[base + p] = jnp.zeros((B, B), out.dtype)

        else:

            @pl.when(on)
            def _(rr=rr, cc=cc, slot=slot):
                out[base + slot] = source[sub(rr, cc, down)].astype(out.dtype)


def unpack(mask, tile, down, block, store):
    for rr, cc, on, slot in cells(mask, tile, down):
        if rr is not None:
            found = block(slot)
            store(rr, cc, jnp.where(on, found, jnp.zeros_like(found)))


def k_pack(pos, gm, um, dm, gw, uw, dw, gu, dn):
    tile = pos[0] * 4 + pos[1]
    pack(gm, tile, False, gw, gu, 0)
    pack(um, tile, False, uw, gu, 7)
    pack(dm, tile, True, dw, dn, 0)


def k_gate_up(pos, gm, um, p0, p1, p2, p3, full, o0, o1, o2, o3, wg, wu, tok, acc):
    y, z = pos[0], pos[1]
    for j, panel in enumerate((p0, p1, p2, p3)):
        zz = jnp.bitwise_xor(z, j)
        for mask, base, dense in ((gm, 0, wg), (um, 7, wu)):

            def store(rr, cc, v, dense=dense, zz=zz):
                rows = pl.ds(pl.multiple_of(zz * 256 + rr * B, B), B)
                dense[rows, pl.ds(cc * B, B)] = v

            unpack(mask, 4 * y + zz, False, lambda s, base=base, panel=panel: panel[base + s], store)
    for x in range(4):
        for q in range(4):
            tok[x * B : (x + 1) * B, q * 256 : (q + 1) * 256] = full[q % 2, x, q // 2, 0]
    for half, dense in enumerate((wg, wu)):
        got = jnp.dot(tok[...], dense[...], preferred_element_type=F32)
        acc[:, :, half * 896 : (half + 1) * 896] = got.reshape(4, B, 896)
    o0[...] = acc[y]
    for j, out in ((1, o1), (2, o2), (3, o3)):
        out[...] = acc[jnp.bitwise_xor(y, j)].astype(BF)


def k_hidden_grad(pos, dm, p0, p1, p2, p3, full, o0, o1, o2, o3, wd, cot, acc):
    y, z = pos[0], pos[1]
    for j, panel in enumerate((p0, p1, p2, p3)):
        zz = jnp.bitwise_xor(z, j)

        def store(rr, cc, v, zz=zz):
            wd[zz, pl.ds(cc * B, B), pl.ds(rr * B, B)] = v

        unpack(dm, 4 * y + zz, True, lambda s, panel=panel: panel[s], store)
    for x in range(4):
        for q in range(4):
            cot[x * B : (x + 1) * B, q * 256 : (q + 1) * 256] = full[q % 2, x, q // 2, 1]
    got = None
    for q in range(4):
        term = lax.dot_general(
            cot[:, q * 256 : (q + 1) * 256],
            wd[q],
            (((1,), (1,)), ((), ())),
            preferred_element_type=F32,
        )
        got = term if got is None else got + term
    acc[...] = got.reshape(4, B, 896)
    o0[...] = acc[y]
    for j, out in ((1, o1), (2, o2), (3, o3)):
        out[...] = acc[jnp.bitwise_xor(y, j)].astype(BF)


def total(own, *others):
    out = own[...]
    for o in others:
        out = out + o[...].astype(F32)
    return out


def k_hidden(a0, a1, a2, a3, hid):
    both = total(a0, a1, a2, a3)
    gate, up = both[:, :896], both[:, 896:]
    hid[...] = (gate * jax.nn.sigmoid(gate) * up).astype(BF)


def k_act(a0, a1, a2, a3, b0, b1, b2, b3, act):
    both = total(a0, a1, a2, a3)
    gate, up = both[:, :896], both[:, 896:]
    grad = total(b0, b1, b2, b3)
    sig = jax.nn.sigmoid(gate)
    act[:, :896] = (grad * up * sig * (1.0 + gate * (1.0 - sig))).astype(BF)
    act[:, 896:] = (grad * (gate * sig)).astype(BF)


def columns(q):
    return pl.ds(pl.multiple_of(q * 256, 256), 256)


TN = (((0,), (0,)), ((), ()))
NT = (((1,), (1,)), ((), ()))


def k_down_grad(pos, dm, h0, h1, h2, h3, cot, d0, d1, d2, d3, hid, acc):
    y, z = pos[0], pos[1]
    for j, h in enumerate((h0, h1, h2, h3)):
        hid[jnp.bitwise_xor(y, j)] = h[...]
    left = hid[...].reshape(512, 896)
    for j, out in ((1, d1), (2, d2), (3, d3), (0, d0)):
        zz = jnp.bitwise_xor(z, j)
        acc[...] = lax.dot_general(left, cot[:, columns(zz)], TN, preferred_element_type=F32)
        pack(dm, 4 * y + zz, True, acc, out, 0)


def k_weight_grad(pos, gm, um, a0, a1, a2, a3, tok, d0, d1, d2, d3, act, acc):
    y, z = pos[0], pos[1]
    for j, a in enumerate((a0, a1, a2, a3)):
        act[jnp.bitwise_xor(y, j)] = a[...]
    right = act[...].reshape(512, 1792)
    for j, out in ((1, d1), (2, d2), (3, d3), (0, d0)):
        zz = jnp.bitwise_xor(z, j)
        got = lax.dot_general(tok[:, columns(zz)], right, TN, preferred_element_type=F32)
        acc[0] = got[:, :896]
        acc[1] = got[:, 896:]
        pack(gm, 4 * y + zz, False, acc.at[0], out, 0)
        pack(um, 4 * y + zz, False, acc.at[1], out, 7)


def k_out(pos, hid, wd, keep, send):
    k = pos[4]
    left = hid[...].reshape(512, 896)
    for out, kk in ((send, 1 - k), (keep, k)):
        for h in range(2):
            got = jnp.dot(left, wd[2 * h + kk], preferred_element_type=F32)
            out[:, h] = got.reshape(4, B, 256).astype(out.dtype)


def k_in(pos, act, wg, wu, keep, send):
    k = pos[4]
    both = act[...].reshape(512, 1792)
    left, right = both[:, :896], both[:, 896:]
    for out, kk in ((send, 1 - k), (keep, k)):
        for h in range(2):
            rows = columns(2 * h + kk)
            got = lax.dot_general(left, wg[rows, :], NT, preferred_element_type=F32)
            got = got + lax.dot_general(right, wu[rows, :], NT, preferred_element_type=F32)
            out[:, h] = got.reshape(4, B, 256).astype(out.dtype)


def k_sum_core(pos, keep, got, o0, o1, o2, o3):
    x = pos[2]
    for j, out in enumerate((o0, o1, o2, o3)):
        at = jnp.bitwise_xor(x, j)
        out[...] = (keep[at] + got[at].astype(F32)).astype(out.dtype)


def k_sum_x(pos, a0, a1, a2, a3, keep, send, acc):
    h = pos[3]
    acc[...] = total(a0, a1, a2, a3)
    keep[...] = acc[h]
    send[...] = acc[1 - h].astype(BF)


def k_sum_pair(a, b, out):
    out[...] = (a[...] + b[...].astype(F32)).astype(BF)


def k_place(pos, mask, a0, a1, a2, a3, out, *, base, down):
    tile = pos[0] * 4 + pos[1]

    def block(s):
        return total(a0.at[base + s], a1.at[base + s], a2.at[base + s], a3.at[base + s])

    def store(rr, cc, v):
        out[sub(rr, cc, down)] = v.astype(BF)

    unpack(mask, tile, down, block, store)


def exchange(value, axis, by, size=4):
    return lax.ppermute(value, axis, [(i, i ^ by) for i in range(size)])


def spread(value, axis):
    return [value] + [exchange(value, axis, j) for j in (1, 2, 3)]


def collect(own, others, axis):
    return [own] + [exchange(v, axis, j) for j, v in zip((1, 2, 3), others)]


def swap(value):
    pairs = [(y * 4 + x, x * 4 + y) for y in range(4) for x in range(4)]
    return lax.ppermute(value, ("y", "x"), pairs)


def scatter_sum(pos, keep, send):
    got = exchange(send, "k", 1, 2)
    part = (2, B, 256)
    s = call(
        k_sum_core, (1, 0, 0), (pos, keep, got),
        (sds(part, F32), sds(part), sds(part), sds(part)),
    )
    own, other = call(
        k_sum_x, (1, 0, 0, 0, 0), (pos, *collect(s[0], s[1:], "x")),
        (sds((B, 256), F32), sds((B, 256))), (pltpu.VMEM(part, F32),),
    )
    (done,) = call(k_sum_pair, (0, 0), (own, exchange(other, "h", 1, 2)), (sds((B, 256)),))
    return swap(done)


def body(tokens, cotangent, gate_weight, up_weight, down_weight, gate_mask, up_mask, down_mask):
    pos = jnp.stack([lax.axis_index(a) for a in ("y", "z", "x", "h", "k")]).astype(jnp.int32)
    masks = (gate_mask, up_mask, down_mask)
    both = swap(jnp.stack([tokens, cotangent]))
    gu, dn = call(
        k_pack, (1, 1, 1, 1, 0, 0, 0),
        (pos, *masks, gate_weight, up_weight, down_weight),
        (sds((14, B, B)), sds((7, B, B))),
    )
    gu_all = spread(gu, "z")
    dn_all = spread(dn, "z")
    full = both
    for axis in ("h", "x", "k"):
        full = lax.all_gather(full, axis, axis=0)
    blk = (B, 1792)
    g = call(
        k_gate_up, (1, 1, 1, 0, 0, 0, 0, 0), (pos, gate_mask, up_mask, *gu_all, full),
        (sds(blk, F32), sds(blk), sds(blk), sds(blk),
         sds((1024, 896)), sds((1024, 896)), sds((512, 1024))),
        (pltpu.VMEM((4, B, 1792), F32),), flops=2 * 512 * 1024 * 1792,
    )
    wg, wu, tok = g[4:]
    g_all = collect(g[0], g[1:4], "y")
    blk = (B, 896)
    d = call(
        k_hidden_grad, (1, 1, 0, 0, 0, 0, 0), (pos, down_mask, *dn_all, full),
        (sds(blk, F32), sds(blk), sds(blk), sds(blk), sds((4, 896, 256)), sds((512, 1024))),
        (pltpu.VMEM((4, B, 896), F32),), flops=2 * 512 * 1024 * 896,
    )
    wd, cot = d[4:]
    d_all = collect(d[0], d[1:4], "y")
    (hidden,) = call(k_hidden, (0,) * 4, g_all, (sds((B, 896)),))
    hid_all = spread(hidden, "y")
    (act,) = call(k_act, (0,) * 8, (*g_all, *d_all), (sds((B, 1792)),))
    act_all = spread(act, "y")
    blk = (7, B, B)
    e = call(
        k_down_grad, (1, 1, 0, 0, 0, 0, 0), (pos, down_mask, *hid_all, cot),
        (sds(blk, F32), sds(blk), sds(blk), sds(blk), sds((4, B, 896))),
        (pltpu.VMEM((896, 256), F32),), flops=2 * 512 * 1024 * 896,
    )
    e_all = collect(e[0], e[1:4], "z")
    half = (4, 2, B, 256)
    keep, send = call(
        k_out, (1, 0, 0), (pos, e[4], wd), (sds(half, F32), sds(half)),
        flops=2 * 512 * 1024 * 896,
    )
    output = scatter_sum(pos, keep, send)
    blk = (14, B, B)
    f = call(
        k_weight_grad, (1, 1, 1, 0, 0, 0, 0, 0), (pos, gate_mask, up_mask, *act_all, tok),
        (sds(blk, F32), sds(blk), sds(blk), sds(blk), sds((4, B, 1792))),
        (pltpu.VMEM((2, 256, 896), F32),), flops=2 * 512 * 1024 * 1792,
    )
    f_all = collect(f[0], f[1:4], "z")
    keep, send = call(
        k_in, (1, 0, 0, 0), (pos, f[4], wg, wu), (sds(half, F32), sds(half)),
        flops=2 * 512 * 1024 * 1792,
    )
    input_grad = scatter_sum(pos, keep, send)

    def place(mask, parts, base, down, shape):
        def kernel(*refs):
            k_place(*refs, base=base, down=down)

        return call(kernel, (1, 1, 0, 0, 0, 0), (pos, mask, *parts), (sds(shape),))[0]

    down_grad = place(down_mask, e_all, 0, True, (896, 256))
    gate_grad = place(gate_mask, f_all, 0, False, (256, 896))
    up_grad = place(up_mask, f_all, 7, False, (256, 896))
    return (output, input_grad, gate_grad, up_grad, down_grad)


def solution(mesh):
    mesh = Mesh(mesh.devices.reshape(4, 4, 4, 2, 2), ("y", "z", "x", "h", "k"))
    row, col = ("y", "z"), ("x", "h", "k")
    return jax.shard_map(
        body,
        mesh=mesh,
        in_specs=(
            P(row, col),
            P(row, col),
            P(row, col),
            P(row, col),
            P(col, row),
            P(None, col),
            P(None, col),
            P(col, None),
        ),
        out_specs=(P(row, col), P(row, col), P(row, col), P(row, col), P(col, row)),
        check_vma=False,
    )
```

time: 949 us -> 297 us (0.31)
  waiting for transfers between devices: 728 us -> 156 us
  matrix products: 109 us -> 0 us
  local copies, waits for them, and re-layouts: 57.9 us -> 3.14 us
  starting transfers between devices: 25 us -> 74.1 us
  Pallas kernels: 0 us -> 30.7 us
  blocking collectives: 0 us -> 12.5 us
    all_gather x8 -> x2, waiting for transfers between devices: 512 us -> 30.3 us  [body(): full = lax.all_gather(full, axis, axis=0)]
    reduce_scatter x2 -> x0, waiting for transfers between devices: 148 us -> none  [the longest x1 81.1 us: body(): lax.psum_scatter(grad_term.reshape(tok_rows, model_width).astype(jnp.bflo...]
    ppermute x0 -> x37, waiting for transfers between devices: none -> 126 us  [the longest x34 121 us: exchange(): return lax.ppermute(value, axis, [(i, i ^ by) for i in range(size)])]
    dot_general x33 -> x0, matrix products: 109 us -> none  [the longest x6 41 us: panel_product(): jnp.einsum('ntc,nk->tkc', product, target_pick, precision=lax.Precision.H...]
    ppermute x0 -> x37, starting transfers between devices: none -> 74 us  [the longest x34 64 us: exchange(): return lax.ppermute(value, axis, [(i, i ^ by) for i in range(size)])]
    all_to_all x2 -> x0, waiting for transfers between devices: 64.9 us -> none  [the longest x1 33.2 us: body(): lax.all_to_all(full_cotangent, 'row', split_axis=1, concat_axis=0, tiled=...]
    pallas_call x0 -> x18, Pallas kernels: none -> 30.7 us  [call(): pl.pallas_call(kernel, out_shape=tuple(outs), in_specs=[SM if s else VM f...]
    reshape x14 -> x0, local copies, waits for them, and re-layouts: 29 us -> none  [the longest x4 17.6 us: tile_grad(): right_blocks = right_all.reshape(token_count, cols_blk, block_size)]
  transfers between devices with their start and end apart: 12 -> 39, of which waited for: 11 -> 19; matrix products, arithmetic and copies ran while one was open for 17% -> 0% of each run, Pallas kernels for 0% -> 11%
where the time goes in v1:
time: 297 us; the launch traced here: 292 us
  waiting for transfers between devices  156 us (53%)
  starting transfers between devices  74.1 us (25%)
  Pallas kernels  30.7 us (10%)
  between operations  14.3 us (5%)
  blocking collectives  12.5 us (4%)
  local copies, waits for them, and re-layouts  3.14 us (1%)
    ppermute x34, waiting for transfers between devices, exchange(): return lax.ppermute(value, axis, [(i, i ^ by) for i in range(size)])  121 us
    ppermute x34, starting transfers between devices, exchange(): return lax.ppermute(value, axis, [(i, i ^ by) for i in range(size)])  64 us
    pallas_call x18, Pallas kernels, call(): pl.pallas_call(kernel, out_shape=tuple(outs), in_specs=[SM if s else VM f...  30.7 us
    all_gather x2, waiting for transfers between devices, body(): full = lax.all_gather(full, axis, axis=0)  30.3 us
    all_gather x1, blocking collectives, body(): full = lax.all_gather(full, axis, axis=0)  12.5 us
    ppermute x3, starting transfers between devices, swap(): return lax.ppermute(value, ('y', 'x'), pairs)  10 us
  transfers between devices with their start and end apart: 39, of which 19 were waited for; matrix products, arithmetic and copies ran while one was open for 0% of the time, Pallas kernels for 11%

profile of v1, /device:TPU:34, one launch (start us, length us, event | category | flops | bytes accessed | tf_op | source)
XLA Modules:
  0.0 292.1 jit_solution(1618775216375793764)
XLA Ops:
  8.3 3.5 %collective-permute-start.3 = (bf16[2,128,256]{2,1,0:T(8,128)(2,1)S(1)}, bf16[2,128,256]{2,1,0:T(8,128)(2,1)S(1)}, u32[]{:S(2)}, u32[]{:S(2)}) collective-permute-start(bf16[2,128,256]{2,1,0:T(8,128)(2,1)S(1)} %pad_maximum_fusion), channel_id=1, source_target_pairs={{0,0},{4,64},{8,128},{12,192},{64,4},{68,68},{72,132},{76,196},{12... | collective-permute-start | bytes 393224 | tf_op jit(solution)/shard_map/ppermute | solution.py:246
  11.7 4.6 %collective-permute-done.3 = bf16[2,128,256]{2,1,0:T(8,128)(2,1)S(1)} collective-permute-done((bf16[2,128,256]{2,1,0:T(8,128)(2,1)S(1)}, bf16[2,128,256]{2,1,0:T(8,128)(2,1)S(1)}, u32[]{:S(2)}, u32[]{:S(2)}) %collective-permute-start.3) | collective-permute-done | bytes 131104 | tf_op jit(solution)/shard_map/ppermute | solution.py:246
  16.3 12.5 %all-gather = bf16[4,128,256]{2,1,0:T(8,128)(2,1)} all-gather(bf16[2,128,256]{2,1,0:T(8,128)(2,1)S(1)} %collective-permute-done.3), channel_id=2, replica_groups=mesh['y'=4,'z'=4,'x'=4,'h'=2,'k'=2] {'h'}, dimensions={0}, use_global_device_ids=true | all-gather | bytes 393216 | tf_op jit(solution)/shard_map/all_gather | solution.py:277
  28.9 30.3 %all-gather.6.cloned.1.call-done = bf16[8,2,128,256]{3,2,1,0:T(8,128)(2,1)} async-done(((bf16[2,2,128,256]{3,2,1,0:T(8,128)(2,1)}), bf16[8,2,128,256]{3,2,1,0:T(8,128)(2,1)}) %all-gather.6.cloned.1.call-update) | async-done | bytes 1048592 | tf_op jit(solution)/shard_map/all_gather | solution.py:277
  59.5 1.6 shard_map.119
  61.1 1.6 collective-permute-start.2
  62.8 1.3 collective-permute-start.1
  65.2 1.5 collective-permute-start.12
  66.7 28.6 %collective-permute-done.2.p3 = bf16[14,128,128]{2,1,0:T(8,128)(2,1)S(1)} collective-permute-done((bf16[14,128,128]{2,1,0:T(8,128)(2,1)S(1)}, bf16[14,128,128]{2,1,0:T(8,128)(2,1)S(1)}, u32[]{:S(2)}, u32[]{:S(2)}) %collective-permute-start.2) | collective-permute-done | bytes 458784 | tf_op jit(solution)/shard_map/ppermute | solution.py:233
  95.3 12.6 %collective-permute-done.1.p2 = bf16[14,128,128]{2,1,0:T(8,128)(2,1)S(1)} collective-permute-done((bf16[14,128,128]{2,1,0:T(8,128)(2,1)S(1)}, bf16[14,128,128]{2,1,0:T(8,128)(2,1)S(1)}, u32[]{:S(2)}, u32[]{:S(2)}) %collective-permute-start.1) | collective-permute-done | bytes 458784 | tf_op jit(solution)/shard_map/ppermute | solution.py:233
  107.9 1.6 copy-done.4
  109.4 4.4 %shard_map.120 = (f32[128,1792]{1,0:T(8,128)S(1)}, bf16[128,1792]{1,0:T(8,128)(2,1)S(1)}, bf16[128,1792]{1,0:T(8,128)(2,1)S(1)}, bf16[128,1792]{1,0:T(8,128)(2,1...) custom-call(s32[5]{0:T(128)S(1)} %stack.32.pos.refs_0_, ...), custom_call_target="tpu_custom_call" | custom-call | flops 1879048192 | bytes 10946324 | tf_op jit(solution)/shard_map/pallas_call | solution.py:21
  113.9 1.6 collective-permute-start.4
  115.4 2.7 collective-permute-start.5
  118.6 3.4 %collective-permute-start.11 = (bf16[7,128,128]{2,1,0:T(8,128)(2,1)S(1)}, bf16[7,128,128]{2,1,0:T(8,128)(2,1)S(1)}, u32[]{:S(2)}, u32[]{:S(2)}) collective-permute-start(bf16[7,128,128]{2,1,0:T(8,128)(2,1)S(1)} %get-tuple-element.51.p0), channel_id=1, source_target_pairs={{0,32},{16,48},{32,0},{48,16},{1,33},{17,49},{33,1},{49,17},{2,34}... | collective-permute-start | bytes 688136 | tf_op jit(solution)/shard_map/ppermute | solution.py:233
  122.0 5.0 %collective-permute-done.11.p2 = bf16[7,128,128]{2,1,0:T(8,128)(2,1)S(1)} collective-permute-done((bf16[7,128,128]{2,1,0:T(8,128)(2,1)S(1)}, bf16[7,128,128]{2,1,0:T(8,128)(2,1)S(1)}, u32[]{:S(2)}, u32[]{:S(2)}) %collective-permute-start.11) | collective-permute-done | bytes 229408 | tf_op jit(solution)/shard_map/ppermute | solution.py:233
  128.1 2.4 shard_map.122
  130.9 3.9 %collective-permute-start.20 = (bf16[128,896]{1,0:T(8,128)(2,1)S(1)}, bf16[128,896]{1,0:T(8,128)(2,1)S(1)}, u32[]{:S(2)}, u32[]{:S(2)}) collective-permute-start(bf16[128,896]{1,0:T(8,128)(2,1)S(1)} %get-tuple-element.65), channel_id=1, source_target_pairs={{0,128},{64,192},{128,0},{192,64},{1,129},{65,193},{129,1},{193,65... | collective-permute-start | bytes 688136 | tf_op jit(solution)/shard_map/ppermute | solution.py:233
  135.3 1.4 collective-permute-done.5.a2
  136.7 3.0 %collective-permute-done.6.a3 = bf16[128,1792]{1,0:T(8,128)(2,1)S(1)} collective-permute-done((bf16[128,1792]{1,0:T(8,128)(2,1)S(1)}, bf16[128,1792]{1,0:T(8,128)(2,1)S(1)}, u32[]{:S(2)}, u32[]{:S(2)}) %collective-permute-start.6) | collective-permute-done | bytes 458784 | tf_op jit(solution)/shard_map/ppermute | solution.py:233
  140.6 3.7 %collective-permute-done.20.b2 = bf16[128,896]{1,0:T(8,128)(2,1)S(1)} collective-permute-done((bf16[128,896]{1,0:T(8,128)(2,1)S(1)}, bf16[128,896]{1,0:T(8,128)(2,1)S(1)}, u32[]{:S(2)}, u32[]{:S(2)}) %collective-permute-start.20) | collective-permute-done | bytes 229408 | tf_op jit(solution)/shard_map/ppermute | solution.py:233
  144.3 3.9 %collective-permute-done.21.b3 = bf16[128,896]{1,0:T(8,128)(2,1)S(1)} collective-permute-done((bf16[128,896]{1,0:T(8,128)(2,1)S(1)}, bf16[128,896]{1,0:T(8,128)(2,1)S(1)}, u32[]{:S(2)}, u32[]{:S(2)}) %collective-permute-start.21) | collective-permute-done | bytes 229408 | tf_op jit(solution)/shard_map/ppermute | solution.py:233
  149.8 3.0 %collective-permute-start.22 = (bf16[128,1792]{1,0:T(8,128)(2,1)S(1)}, bf16[128,1792]{1,0:T(8,128)(2,1)S(1)}, u32[]{:S(2)}, u32[]{:S(2)}) collective-permute-start(bf16[128,1792]{1,0:T(8,128)(2,1)S(1)} %shard_map.128.a0), channel_id=1, source_target_pairs={{0,64},{64,0},{128,192},{192,128},{1,65},{65,1},{129,193},{193,129... | collective-permute-start | bytes 1376264 | tf_op jit(solution)/shard_map/ppermute | solution.py:233
  153.5 8.2 %collective-permute-done.9.h3 = bf16[128,896]{1,0:T(8,128)(2,1)S(1)} collective-permute-done((bf16[128,896]{1,0:T(8,128)(2,1)S(1)}, bf16[128,896]{1,0:T(8,128)(2,1)S(1)}, u32[]{:S(2)}, u32[]{:S(2)}) %collective-permute-start.9) | collective-permute-done | bytes 229408 | tf_op jit(solution)/shard_map/ppermute | solution.py:233
  161.7 16.0 %collective-permute-done.8.h2 = bf16[128,896]{1,0:T(8,128)(2,1)S(1)} collective-permute-done((bf16[128,896]{1,0:T(8,128)(2,1)S(1)}, bf16[128,896]{1,0:T(8,128)(2,1)S(1)}, u32[]{:S(2)}, u32[]{:S(2)}) %collective-permute-start.8) | collective-permute-done | bytes 229408 | tf_op jit(solution)/shard_map/ppermute | solution.py:233
  177.7 2.5 collective-permute-done.7.h1
  180.2 3.7 %shard_map.123 = (f32[7,128,128]{2,1,0:T(8,128)S(1)}, bf16[7,128,128]{2,1,0:T(8,128)(2,1)S(1)}, bf16[7,128,128]{2,1,0:T(8,128)(2,1)S(1)}, bf16[7,128,128]{2,1,0:T(8,128)(2,1)S(1)}, bf16[4,128,896]{2,1,0:T(8,128)(2,1)S(1)}) custom-call(s32[5]{0:T(128)S(1)} %stack.32.pos.refs_0_, s32[7,32]{1,0:T(8,128)S(1)} %copy-done.3, bf16[128,896]{1,0:T(8,128)(2,1)S(1)} %shard_map.121.h0, ...), custom_call_target="tpu_custom_call" | custom-call | flops 939524096 | bytes 4031380 | tf_op jit(solution)/shard_map/pallas_call | solution.py:21
  183.9 1.8 shard_map.124
  185.9 5.2 %shard_map.129 = (f32[14,128,128]{2,1,0:T(8,128)S(1)}, bf16[14,128,128]{2,1,0:T(8,128)(2,1)S(1)}, bf16[14,128,128]{2,1,0:T(8,128)(2,1)S(1)}, bf16[14,128,128]{2,1,0:T(8,128)(2,1)S(1)}, bf16[4,128,1792]{2,1,0:T(8,128)(2,1)S(1)}) custom-call(s32[5]{0:T(128)S(1)} %stack.32.pos.refs_0_, s32[32,7]{1,0:T(8,128)S(1)} %copy.23.gm.refs_1_, ...), custom_call_target="tpu_custom_call" | custom-call | flops 1879048192 | bytes 7014164 | tf_op jit(solution)/shard_map/pallas_call | solution.py:21
  191.1 2.9 shard_map.130
  195.4 1.8 collective-permute-start.14
  197.2 1.6 collective-permute-start.15
  199.6 3.0 %collective-permute-start.26 = (bf16[2,128,256]{2,1,0:T(8,128)(2,1)S(1)}, bf16[2,128,256]{2,1,0:T(8,128)(2,1)S(1)}, u32[]{:S(2)}, u32[]{:S(2)}) collective-permute-start(bf16[2,128,256]{2,1,0:T(8,128)(2,1)S(1)} %get-tuple-element.74), channel_id=1, source_target_pairs={{0,4},{4,0},{8,12},{12,8},{1,5},{5,1},{9,13},{13,9},{2,6},{6,2},{1... | collective-permute-start | bytes 393224 | tf_op jit(solution)/shard_map/ppermute | solution.py:233
  203.1 2.4 collective-permute-start.34
  206.7 2.2 collective-permute-start.31
  208.9 2.0 collective-permute-start.32
  212.4 4.7 %collective-permute-start.17 = (bf16[128,256]{1,0:T(8,128)(2,1)S(1)}, bf16[128,256]{1,0:T(8,128)(2,1)S(1)}, u32[]{:S(2)}, u32[]{:S(2)}) collective-permute-start(bf16[128,256]{1,0:T(8,128)(2,1)S(1)} %get-tuple-element.62), channel_id=1, source_target_pairs={{0,2},{2,0},{1,3},{3,1},{4,6},{6,4},{5,7},{7,5},{8,10},{10,8},{9,1... | collective-permute-start | bytes 196616 | tf_op jit(solution)/shard_map/ppermute | solution.py:233
  217.7 2.0 collective-permute-done.34.refs_3_
  219.7 4.6 %collective-permute-start.29 = (bf16[128,256]{1,0:T(8,128)(2,1)S(1)}, bf16[128,256]{1,0:T(8,128)(2,1)S(1)}, u32[]{:S(2)}, u32[]{:S(2)}) collective-permute-start(bf16[128,256]{1,0:T(8,128)(2,1)S(1)} %get-tuple-element.78), channel_id=1, source_target_pairs={{0,2},{2,0},{1,3},{3,1},{4,6},{6,4},{5,7},{7,5},{8,10},{10,8},{9,1... | collective-permute-start | bytes 196616 | tf_op jit(solution)/shard_map/ppermute | solution.py:233
  224.3 12.6 %collective-permute-done.17.b = bf16[128,256]{1,0:T(8,128)(2,1)S(1)} collective-permute-done((bf16[128,256]{1,0:T(8,128)(2,1)S(1)}, bf16[128,256]{1,0:T(8,128)(2,1)S(1)}, u32[]{:S(2)}, u32[]{:S(2)}) %collective-permute-start.17) | collective-permute-done | bytes 65568 | tf_op jit(solution)/shard_map/ppermute | solution.py:233
  236.9 12.6 %collective-permute-start.35 = (bf16[7,128,128]{2,1,0:T(8,128)(2,1)S(1)}, bf16[7,128,128]{2,1,0:T(8,128)(2,1)S(1)}, u32[]{:S(2)}, u32[]{:S(2)}) collective-permute-start(bf16[7,128,128]{2,1,0:T(8,128)(2,1)S(1)} %get-tuple-element.85), channel_id=1, source_target_pairs={{0,32},{16,48},{32,0},{48,16},{1,33},{17,49},{33,1},{49,17},{2,34}... | collective-permute-start | bytes 688136 | tf_op jit(solution)/shard_map/ppermute | solution.py:233
  249.5 2.5 collective-permute-start.36
  252.1 19.5 %collective-permute-done.35.refs_4_ = bf16[7,128,128]{2,1,0:T(8,128)(2,1)S(1)} collective-permute-done((bf16[7,128,128]{2,1,0:T(8,128)(2,1)S(1)}, bf16[7,128,128]{2,1,0:T(8,128)(2,1)S(1)}, u32[]{:S(2)}, u32[]{:S(2)}) %collective-permute-start.35) | collective-permute-done | bytes 229408 | tf_op jit(solution)/shard_map/ppermute | solution.py:233
  271.5 2.9 %collective-permute-start.18 = (bf16[128,256]{1,0:T(8,128)(2,1)S(1)}, bf16[128,256]{1,0:T(8,128)(2,1)S(1)}, u32[]{:S(2)}, u32[]{:S(2)}) collective-permute-start(bf16[128,256]{1,0:T(8,128)(2,1)S(1)} %shard_map.127), channel_id=1, source_target_pairs={{0,0},{4,64},{8,128},{12,192},{64,4},{68,68},{72,132},{76,196},{12... | collective-permute-start | bytes 196616 | tf_op jit(solution)/shard_map/ppermute | solution.py:246
  275.0 3.6 %collective-permute-start.30 = (bf16[128,256]{1,0:T(8,128)(2,1)S(1)}, bf16[128,256]{1,0:T(8,128)(2,1)S(1)}, u32[]{:S(2)}, u32[]{:S(2)}) collective-permute-start(bf16[128,256]{1,0:T(8,128)(2,1)S(1)} %shard_map.133), channel_id=1, source_target_pairs={{0,0},{4,64},{8,128},{12,192},{64,4},{68,68},{72,132},{76,196},{12... | collective-permute-start | bytes 196616 | tf_op jit(solution)/shard_map/ppermute | solution.py:246
  278.6 1.6 shard_map.136
  280.3 1.8 shard_map.135
  282.1 1.8 shard_map.134
  (73 shorter events, 16.0 us)
Async XLA Ops:
  7.2 52.1 %copy-start.6 = (s32[32,7]{0,1:T(8,128)S(1)}, s32[32,7]{0,1:T(8,128)}, u32[]{:S(2)}) copy-start(s32[32,7]{0,1:T(8,128)} %param.13) | copy-start | bytes 2692
  7.2 52.2 %copy-start.7 = (s32[32,7]{0,1:T(8,128)S(1)}, s32[32,7]{0,1:T(8,128)}, u32[]{:S(2)}) copy-start(s32[32,7]{0,1:T(8,128)} %param.14) | copy-start | bytes 2692
  7.2 52.3 %copy-start.3 = (s32[7,32]{1,0:T(8,128)S(1)}, s32[7,32]{1,0:T(8,128)}, u32[]{:S(2)}) copy-start(s32[7,32]{1,0:T(8,128)} %refs_1_.3) | copy-start | bytes 2692
  7.2 52.3 %copy-start.2 = (bf16[896,256]{1,0:T(8,128)(2,1)S(1)}, bf16[896,256]{1,0:T(8,128)(2,1)}, u32[]{:S(2)}) copy-start(bf16[896,256]{1,0:T(8,128)(2,1)} %dw.1) | copy-start | bytes 1376260
  7.2 52.3 %copy-start.1 = (bf16[256,896]{1,0:T(8,128)(2,1)S(1)}, bf16[256,896]{1,0:T(8,128)(2,1)}, u32[]{:S(2)}) copy-start(bf16[256,896]{1,0:T(8,128)(2,1)} %uw.1) | copy-start | bytes 1376260
  7.2 52.3 %copy-start = (bf16[256,896]{1,0:T(8,128)(2,1)S(1)}, bf16[256,896]{1,0:T(8,128)(2,1)}, u32[]{:S(2)}) copy-start(bf16[256,896]{1,0:T(8,128)(2,1)} %gw.1) | copy-start | bytes 1376260
  7.2 52.0 %all-gather.6.cloned.1.call-start = ((), (), s32[]{:S(2)}) async-start(), calls=%async_computation | async-start | bytes 1310720 | tf_op jit(solution)/shard_map/all_gather | solution.py:277
  8.3 8.0 %collective-permute-start.3 = (bf16[2,128,256]{2,1,0:T(8,128)(2,1)S(1)}, bf16[2,128,256]{2,1,0:T(8,128)(2,1)S(1)}, u32[]{:S(2)}, u32[]{:S(2)}) collective-permute-start(bf16[2,128,256]{2,1,0:T(8,128)(2,1)S(1)} %pad_maximum_fusion), channel_id=1, source_target_pairs={{0,0},{4,64},{8,128},{12,192},{64,4},{68,68},{72,132},{76,196},{12... | collective-permute-start | bytes 393224 | tf_op jit(solution)/shard_map/ppermute | solution.py:246
  28.8 79.0 %all-gather.8.cloned.1.call-start = ((), (), s32[]{:S(2)}) async-start(), calls=%async_computation.1 | async-start | bytes 3145728 | tf_op jit(solution)/shard_map/all_gather | solution.py:277
  61.1 34.1 %collective-permute-start.2 = (bf16[14,128,128]{2,1,0:T(8,128)(2,1)S(1)}, bf16[14,128,128]{2,1,0:T(8,128)(2,1)S(1)}, u32[]{:S(2)}, u32[]{:S(2)}) collective-permute-start(bf16[14,128,128]{2,1,0:T(8,128)(2,1)S(1)} %get-tuple-element.46.p0), channel_id=1, source_target_pairs={{0,48},{16,32},{32,16},{48,0},{1,49},{17,33},{33,17},{49,1},{2,50}... | collective-permute-start | bytes 1376264 | tf_op jit(solution)/shard_map/ppermute | solution.py:233
  62.8 45.1 %collective-permute-start.1 = (bf16[14,128,128]{2,1,0:T(8,128)(2,1)S(1)}, bf16[14,128,128]{2,1,0:T(8,128)(2,1)S(1)}, u32[]{:S(2)}, u32[]{:S(2)}) collective-permute-start(bf16[14,128,128]{2,1,0:T(8,128)(2,1)S(1)} %get-tuple-element.46.p0), channel_id=1, source_target_pairs={{0,32},{16,48},{32,0},{48,16},{1,33},{17,49},{33,1},{49,17},{2,34}... | collective-permute-start | bytes 1376264 | tf_op jit(solution)/shard_map/ppermute | solution.py:233
  64.1 43.8 %collective-permute-start = (bf16[14,128,128]{2,1,0:T(8,128)(2,1)S(1)}, bf16[14,128,128]{2,1,0:T(8,128)(2,1)S(1)}, u32[]{:S(2)}, u32[]{:S(2)}) collective-permute-start(bf16[14,128,128]{2,1,0:T(8,128)(2,1)S(1)} %get-tuple-element.46.p0), channel_id=1, source_target_pairs={{0,16},{16,0},{32,48},{48,32},{1,17},{17,1},{33,49},{49,33},{2,18}... | collective-permute-start | bytes 1376264 | tf_op jit(solution)/shard_map/ppermute | solution.py:233
  65.2 56.8 %collective-permute-start.12 = (bf16[7,128,128]{2,1,0:T(8,128)(2,1)S(1)}, bf16[7,128,128]{2,1,0:T(8,128)(2,1)S(1)}, u32[]{:S(2)}, u32[]{:S(2)}) collective-permute-start(bf16[7,128,128]{2,1,0:T(8,128)(2,1)S(1)} %get-tuple-element.51.p0), channel_id=1, source_target_pairs={{0,48},{16,32},{32,16},{48,0},{1,49},{17,33},{33,17},{49,1},{2,50}... | collective-permute-start | bytes 688136 | tf_op jit(solution)/shard_map/ppermute | solution.py:233
  107.8 1.6 copy-start.4
  109.4 18.6 %copy-start.5 = (bf16[8,2,2,128,256]{4,3,2,1,0:T(8,128)(2,1)S(1)}, bf16[8,2,2,128,256]{4,3,2,1,0:T(8,128)(2,1)}, u32[]{:S(2)}) copy-start(bf16[8,2,2,128,256]{4,3,2,1,0:T(8,128)(2,1)} %all-gather.8.cloned.1.call-done) | copy-start | bytes 6291460
  113.9 20.9 %collective-permute-start.4 = (bf16[128,1792]{1,0:T(8,128)(2,1)S(1)}, bf16[128,1792]{1,0:T(8,128)(2,1)S(1)}, u32[]{:S(2)}, u32[]{:S(2)}) collective-permute-start(bf16[128,1792]{1,0:T(8,128)(2,1)S(1)} %get-tuple-element.48), channel_id=1, source_target_pairs={{0,64},{64,0},{128,192},{192,128},{1,65},{65,1},{129,193},{193,129... | collective-permute-start | bytes 1376264 | tf_op jit(solution)/shard_map/ppermute | solution.py:233
  115.4 21.2 %collective-permute-start.5 = (bf16[128,1792]{1,0:T(8,128)(2,1)S(1)}, bf16[128,1792]{1,0:T(8,128)(2,1)S(1)}, u32[]{:S(2)}, u32[]{:S(2)}) collective-permute-start(bf16[128,1792]{1,0:T(8,128)(2,1)S(1)} %get-tuple-element.49), channel_id=1, source_target_pairs={{0,128},{64,192},{128,0},{192,64},{1,129},{65,193},{129,1},{193,65... | collective-permute-start | bytes 1376264 | tf_op jit(solution)/shard_map/ppermute | solution.py:233
  118.2 21.5 %collective-permute-start.6 = (bf16[128,1792]{1,0:T(8,128)(2,1)S(1)}, bf16[128,1792]{1,0:T(8,128)(2,1)S(1)}, u32[]{:S(2)}, u32[]{:S(2)}) collective-permute-start(bf16[128,1792]{1,0:T(8,128)(2,1)S(1)} %get-tuple-element.50), channel_id=1, source_target_pairs={{0,192},{64,128},{128,64},{192,0},{1,193},{65,129},{129,65},{193,1... | collective-permute-start | bytes 1376264 | tf_op jit(solution)/shard_map/ppermute | solution.py:233
  118.6 8.4 %collective-permute-start.11 = (bf16[7,128,128]{2,1,0:T(8,128)(2,1)S(1)}, bf16[7,128,128]{2,1,0:T(8,128)(2,1)S(1)}, u32[]{:S(2)}, u32[]{:S(2)}) collective-permute-start(bf16[7,128,128]{2,1,0:T(8,128)(2,1)S(1)} %get-tuple-element.51.p0), channel_id=1, source_target_pairs={{0,32},{16,48},{32,0},{48,16},{1,33},{17,49},{33,1},{49,17},{2,34}... | collective-permute-start | bytes 688136 | tf_op jit(solution)/shard_map/ppermute | solution.py:233
  122.0 6.0 %collective-permute-start.10 = (bf16[7,128,128]{2,1,0:T(8,128)(2,1)S(1)}, bf16[7,128,128]{2,1,0:T(8,128)(2,1)S(1)}, u32[]{:S(2)}, u32[]{:S(2)}) collective-permute-start(bf16[7,128,128]{2,1,0:T(8,128)(2,1)S(1)} %get-tuple-element.51.p0), channel_id=1, source_target_pairs={{0,16},{16,0},{32,48},{48,32},{1,17},{17,1},{33,49},{49,33},{2,18}... | collective-permute-start | bytes 688136 | tf_op jit(solution)/shard_map/ppermute | solution.py:233
  130.5 10.1 %collective-permute-start.19 = (bf16[128,896]{1,0:T(8,128)(2,1)S(1)}, bf16[128,896]{1,0:T(8,128)(2,1)S(1)}, u32[]{:S(2)}, u32[]{:S(2)}) collective-permute-start(bf16[128,896]{1,0:T(8,128)(2,1)S(1)} %get-tuple-element.64), channel_id=1, source_target_pairs={{0,64},{64,0},{128,192},{192,128},{1,65},{65,1},{129,193},{193,129... | collective-permute-start | bytes 688136 | tf_op jit(solution)/shard_map/ppermute | solution.py:233
  130.9 13.4 %collective-permute-start.20 = (bf16[128,896]{1,0:T(8,128)(2,1)S(1)}, bf16[128,896]{1,0:T(8,128)(2,1)S(1)}, u32[]{:S(2)}, u32[]{:S(2)}) collective-permute-start(bf16[128,896]{1,0:T(8,128)(2,1)S(1)} %get-tuple-element.65), channel_id=1, source_target_pairs={{0,128},{64,192},{128,0},{192,64},{1,129},{65,193},{129,1},{193,65... | collective-permute-start | bytes 688136 | tf_op jit(solution)/shard_map/ppermute | solution.py:233
  134.8 13.4 %collective-permute-start.21 = (bf16[128,896]{1,0:T(8,128)(2,1)S(1)}, bf16[128,896]{1,0:T(8,128)(2,1)S(1)}, u32[]{:S(2)}, u32[]{:S(2)}) collective-permute-start(bf16[128,896]{1,0:T(8,128)(2,1)S(1)} %get-tuple-element.66), channel_id=1, source_target_pairs={{0,192},{64,128},{128,64},{192,0},{1,193},{65,129},{129,65},{193,1... | collective-permute-start | bytes 688136 | tf_op jit(solution)/shard_map/ppermute | solution.py:233
  140.0 21.7 %collective-permute-start.9 = (bf16[128,896]{1,0:T(8,128)(2,1)S(1)}, bf16[128,896]{1,0:T(8,128)(2,1)S(1)}, u32[]{:S(2)}, u32[]{:S(2)}) collective-permute-start(bf16[128,896]{1,0:T(8,128)(2,1)S(1)} %shard_map.121.h0), channel_id=1, source_target_pairs={{0,192},{64,128},{128,64},{192,0},{1,193},{65,129},{129,65},{193,1... | collective-permute-start | bytes 688136 | tf_op jit(solution)/shard_map/ppermute | solution.py:233
  148.7 37.2 %collective-permute-start.24 = (bf16[128,1792]{1,0:T(8,128)(2,1)S(1)}, bf16[128,1792]{1,0:T(8,128)(2,1)S(1)}, u32[]{:S(2)}, u32[]{:S(2)}) collective-permute-start(bf16[128,1792]{1,0:T(8,128)(2,1)S(1)} %shard_map.128.a0), channel_id=1, source_target_pairs={{0,192},{64,128},{128,64},{192,0},{1,193},{65,129},{129,65},{193,1... | collective-permute-start | bytes 1376264 | tf_op jit(solution)/shard_map/ppermute | solution.py:233
  149.3 36.6 %collective-permute-start.23 = (bf16[128,1792]{1,0:T(8,128)(2,1)S(1)}, bf16[128,1792]{1,0:T(8,128)(2,1)S(1)}, u32[]{:S(2)}, u32[]{:S(2)}) collective-permute-start(bf16[128,1792]{1,0:T(8,128)(2,1)S(1)} %shard_map.128.a0), channel_id=1, source_target_pairs={{0,128},{64,192},{128,0},{192,64},{1,129},{65,193},{129,1},{193,65... | collective-permute-start | bytes 1376264 | tf_op jit(solution)/shard_map/ppermute | solution.py:233
  149.8 36.1 %collective-permute-start.22 = (bf16[128,1792]{1,0:T(8,128)(2,1)S(1)}, bf16[128,1792]{1,0:T(8,128)(2,1)S(1)}, u32[]{:S(2)}, u32[]{:S(2)}) collective-permute-start(bf16[128,1792]{1,0:T(8,128)(2,1)S(1)} %shard_map.128.a0), channel_id=1, source_target_pairs={{0,64},{64,0},{128,192},{192,128},{1,65},{65,1},{129,193},{193,129... | collective-permute-start | bytes 1376264 | tf_op jit(solution)/shard_map/ppermute | solution.py:233
  152.9 24.8 %collective-permute-start.8 = (bf16[128,896]{1,0:T(8,128)(2,1)S(1)}, bf16[128,896]{1,0:T(8,128)(2,1)S(1)}, u32[]{:S(2)}, u32[]{:S(2)}) collective-permute-start(bf16[128,896]{1,0:T(8,128)(2,1)S(1)} %shard_map.121.h0), channel_id=1, source_target_pairs={{0,128},{64,192},{128,0},{192,64},{1,129},{65,193},{129,1},{193,65... | collective-permute-start | bytes 688136 | tf_op jit(solution)/shard_map/ppermute | solution.py:233
  161.7 18.5 %collective-permute-start.7 = (bf16[128,896]{1,0:T(8,128)(2,1)S(1)}, bf16[128,896]{1,0:T(8,128)(2,1)S(1)}, u32[]{:S(2)}, u32[]{:S(2)}) collective-permute-start(bf16[128,896]{1,0:T(8,128)(2,1)S(1)} %shard_map.121.h0), channel_id=1, source_target_pairs={{0,64},{64,0},{128,192},{192,128},{1,65},{65,1},{129,193},{193,129... | collective-permute-start | bytes 688136 | tf_op jit(solution)/shard_map/ppermute | solution.py:233
  185.8 9.0 %collective-permute-start.13 = (bf16[4,2,128,256]{3,2,1,0:T(8,128)(2,1)S(1)}, bf16[4,2,128,256]{3,2,1,0:T(8,128)(2,1)S(1)}, u32[]{:S(2)}, u32[]{:S(2)}) collective-permute-start(bf16[4,2,128,256]{3,2,1,0:T(8,128)(2,1)S(1)} %get-tuple-element.56), channel_id=1, source_target_pairs={{0,1},{1,0},{2,3},{3,2},{4,5},{5,4},{6,7},{7,6},{8,9},{9,8},{10,11... | collective-permute-start | bytes 1572872 | tf_op jit(solution)/shard_map/ppermute | solution.py:233
  194.0 5.0 %collective-permute-start.25 = (bf16[4,2,128,256]{3,2,1,0:T(8,128)(2,1)S(1)}, bf16[4,2,128,256]{3,2,1,0:T(8,128)(2,1)S(1)}, u32[]{:S(2)}, u32[]{:S(2)}) collective-permute-start(bf16[4,2,128,256]{3,2,1,0:T(8,128)(2,1)S(1)} %get-tuple-element.72), channel_id=1, source_target_pairs={{0,1},{1,0},{2,3},{3,2},{4,5},{5,4},{6,7},{7,6},{8,9},{9,8},{10,11... | collective-permute-start | bytes 1572872 | tf_op jit(solution)/shard_map/ppermute | solution.py:233
  195.4 7.7 %collective-permute-start.14 = (bf16[2,128,256]{2,1,0:T(8,128)(2,1)S(1)}, bf16[2,128,256]{2,1,0:T(8,128)(2,1)S(1)}, u32[]{:S(2)}, u32[]{:S(2)}) collective-permute-start(bf16[2,128,256]{2,1,0:T(8,128)(2,1)S(1)} %get-tuple-element.58), channel_id=1, source_target_pairs={{0,4},{4,0},{8,12},{12,8},{1,5},{5,1},{9,13},{13,9},{2,6},{6,2},{1... | collective-permute-start | bytes 393224 | tf_op jit(solution)/shard_map/ppermute | solution.py:233
  197.2 8.7 %collective-permute-start.15 = (bf16[2,128,256]{2,1,0:T(8,128)(2,1)S(1)}, bf16[2,128,256]{2,1,0:T(8,128)(2,1)S(1)}, u32[]{:S(2)}, u32[]{:S(2)}) collective-permute-start(bf16[2,128,256]{2,1,0:T(8,128)(2,1)S(1)} %get-tuple-element.59), channel_id=1, source_target_pairs={{0,8},{4,12},{8,0},{12,4},{1,9},{5,13},{9,1},{13,5},{2,10},{6,14},... | collective-permute-start | bytes 393224 | tf_op jit(solution)/shard_map/ppermute | solution.py:233
  198.8 7.9 %collective-permute-start.16 = (bf16[2,128,256]{2,1,0:T(8,128)(2,1)S(1)}, bf16[2,128,256]{2,1,0:T(8,128)(2,1)S(1)}, u32[]{:S(2)}, u32[]{:S(2)}) collective-permute-start(bf16[2,128,256]{2,1,0:T(8,128)(2,1)S(1)} %get-tuple-element.60), channel_id=1, source_target_pairs={{0,12},{4,8},{8,4},{12,0},{1,13},{5,9},{9,5},{13,1},{2,14},{6,10},... | collective-permute-start | bytes 393224 | tf_op jit(solution)/shard_map/ppermute | solution.py:233
  199.6 9.2 %collective-permute-start.26 = (bf16[2,128,256]{2,1,0:T(8,128)(2,1)S(1)}, bf16[2,128,256]{2,1,0:T(8,128)(2,1)S(1)}, u32[]{:S(2)}, u32[]{:S(2)}) collective-permute-start(bf16[2,128,256]{2,1,0:T(8,128)(2,1)S(1)} %get-tuple-element.74), channel_id=1, source_target_pairs={{0,4},{4,0},{8,12},{12,8},{1,5},{5,1},{9,13},{13,9},{2,6},{6,2},{1... | collective-permute-start | bytes 393224 | tf_op jit(solution)/shard_map/ppermute | solution.py:233
  202.7 8.2 %collective-permute-start.27 = (bf16[2,128,256]{2,1,0:T(8,128)(2,1)S(1)}, bf16[2,128,256]{2,1,0:T(8,128)(2,1)S(1)}, u32[]{:S(2)}, u32[]{:S(2)}) collective-permute-start(bf16[2,128,256]{2,1,0:T(8,128)(2,1)S(1)} %get-tuple-element.75), channel_id=1, source_target_pairs={{0,8},{4,12},{8,0},{12,4},{1,9},{5,13},{9,1},{13,5},{2,10},{6,14},... | collective-permute-start | bytes 393224 | tf_op jit(solution)/shard_map/ppermute | solution.py:233
  203.1 16.6 %collective-permute-start.34 = (bf16[7,128,128]{2,1,0:T(8,128)(2,1)S(1)}, bf16[7,128,128]{2,1,0:T(8,128)(2,1)S(1)}, u32[]{:S(2)}, u32[]{:S(2)}) collective-permute-start(bf16[7,128,128]{2,1,0:T(8,128)(2,1)S(1)} %get-tuple-element.84), channel_id=1, source_target_pairs={{0,16},{16,0},{32,48},{48,32},{1,17},{17,1},{33,49},{49,33},{2,18}... | collective-permute-start | bytes 688136 | tf_op jit(solution)/shard_map/ppermute | solution.py:233
  206.0 6.4 %collective-permute-start.28 = (bf16[2,128,256]{2,1,0:T(8,128)(2,1)S(1)}, bf16[2,128,256]{2,1,0:T(8,128)(2,1)S(1)}, u32[]{:S(2)}, u32[]{:S(2)}) collective-permute-start(bf16[2,128,256]{2,1,0:T(8,128)(2,1)S(1)} %get-tuple-element.76), channel_id=1, source_target_pairs={{0,12},{4,8},{8,4},{12,0},{1,13},{5,9},{9,5},{13,1},{2,14},{6,10},... | collective-permute-start | bytes 393224 | tf_op jit(solution)/shard_map/ppermute | solution.py:233
  206.7 73.6 %collective-permute-start.31 = (bf16[14,128,128]{2,1,0:T(8,128)(2,1)S(1)}, bf16[14,128,128]{2,1,0:T(8,128)(2,1)S(1)}, u32[]{:S(2)}, u32[]{:S(2)}) collective-permute-start(bf16[14,128,128]{2,1,0:T(8,128)(2,1)S(1)} %get-tuple-element.80), channel_id=1, source_target_pairs={{0,16},{16,0},{32,48},{48,32},{1,17},{17,1},{33,49},{49,33},{2,18}... | collective-permute-start | bytes 1376264 | tf_op jit(solution)/shard_map/ppermute | solution.py:233
  208.9 71.4 %collective-permute-start.32 = (bf16[14,128,128]{2,1,0:T(8,128)(2,1)S(1)}, bf16[14,128,128]{2,1,0:T(8,128)(2,1)S(1)}, u32[]{:S(2)}, u32[]{:S(2)}) collective-permute-start(bf16[14,128,128]{2,1,0:T(8,128)(2,1)S(1)} %get-tuple-element.81), channel_id=1, source_target_pairs={{0,32},{16,48},{32,0},{48,16},{1,33},{17,49},{33,1},{49,17},{2,34}... | collective-permute-start | bytes 1376264 | tf_op jit(solution)/shard_map/ppermute | solution.py:233
  210.8 69.5 %collective-permute-start.33 = (bf16[14,128,128]{2,1,0:T(8,128)(2,1)S(1)}, bf16[14,128,128]{2,1,0:T(8,128)(2,1)S(1)}, u32[]{:S(2)}, u32[]{:S(2)}) collective-permute-start(bf16[14,128,128]{2,1,0:T(8,128)(2,1)S(1)} %get-tuple-element.82), channel_id=1, source_target_pairs={{0,48},{16,32},{32,16},{48,0},{1,49},{17,33},{33,17},{49,1},{2,50}... | collective-permute-start | bytes 1376264 | tf_op jit(solution)/shard_map/ppermute | solution.py:233
  212.4 24.5 %collective-permute-start.17 = (bf16[128,256]{1,0:T(8,128)(2,1)S(1)}, bf16[128,256]{1,0:T(8,128)(2,1)S(1)}, u32[]{:S(2)}, u32[]{:S(2)}) collective-permute-start(bf16[128,256]{1,0:T(8,128)(2,1)S(1)} %get-tuple-element.62), channel_id=1, source_target_pairs={{0,2},{2,0},{1,3},{3,1},{4,6},{6,4},{5,7},{7,5},{8,10},{10,8},{9,1... | collective-permute-start | bytes 196616 | tf_op jit(solution)/shard_map/ppermute | solution.py:233
  219.7 29.8 %collective-permute-start.29 = (bf16[128,256]{1,0:T(8,128)(2,1)S(1)}, bf16[128,256]{1,0:T(8,128)(2,1)S(1)}, u32[]{:S(2)}, u32[]{:S(2)}) collective-permute-start(bf16[128,256]{1,0:T(8,128)(2,1)S(1)} %get-tuple-element.78), channel_id=1, source_target_pairs={{0,2},{2,0},{1,3},{3,1},{4,6},{6,4},{5,7},{7,5},{8,10},{10,8},{9,1... | collective-permute-start | bytes 196616 | tf_op jit(solution)/shard_map/ppermute | solution.py:233
  236.9 34.6 %collective-permute-start.35 = (bf16[7,128,128]{2,1,0:T(8,128)(2,1)S(1)}, bf16[7,128,128]{2,1,0:T(8,128)(2,1)S(1)}, u32[]{:S(2)}, u32[]{:S(2)}) collective-permute-start(bf16[7,128,128]{2,1,0:T(8,128)(2,1)S(1)} %get-tuple-element.85), channel_id=1, source_target_pairs={{0,32},{16,48},{32,0},{48,16},{1,33},{17,49},{33,1},{49,17},{2,34}... | collective-permute-start | bytes 688136 | tf_op jit(solution)/shard_map/ppermute | solution.py:233
  249.5 25.5 %collective-permute-start.36 = (bf16[7,128,128]{2,1,0:T(8,128)(2,1)S(1)}, bf16[7,128,128]{2,1,0:T(8,128)(2,1)S(1)}, u32[]{:S(2)}, u32[]{:S(2)}) collective-permute-start(bf16[7,128,128]{2,1,0:T(8,128)(2,1)S(1)} %get-tuple-element.86), channel_id=1, source_target_pairs={{0,48},{16,32},{32,16},{48,0},{1,49},{17,33},{33,17},{49,1},{2,50}... | collective-permute-start | bytes 688136 | tf_op jit(solution)/shard_map/ppermute | solution.py:233
  271.5 12.4 %collective-permute-start.18 = (bf16[128,256]{1,0:T(8,128)(2,1)S(1)}, bf16[128,256]{1,0:T(8,128)(2,1)S(1)}, u32[]{:S(2)}, u32[]{:S(2)}) collective-permute-start(bf16[128,256]{1,0:T(8,128)(2,1)S(1)} %shard_map.127), channel_id=1, source_target_pairs={{0,0},{4,64},{8,128},{12,192},{64,4},{68,68},{72,132},{76,196},{12... | collective-permute-start | bytes 196616 | tf_op jit(solution)/shard_map/ppermute | solution.py:246
  275.0 9.0 %collective-permute-start.30 = (bf16[128,256]{1,0:T(8,128)(2,1)S(1)}, bf16[128,256]{1,0:T(8,128)(2,1)S(1)}, u32[]{:S(2)}, u32[]{:S(2)}) collective-permute-start(bf16[128,256]{1,0:T(8,128)(2,1)S(1)} %shard_map.133), channel_id=1, source_target_pairs={{0,0},{4,64},{8,128},{12,192},{64,4},{68,68},{72,132},{76,196},{12... | collective-permute-start | bytes 196616 | tf_op jit(solution)/shard_map/ppermute | solution.py:246
Sparse Core Ops, SparseCore 0:
  28.9 30.2 all-gather.5
  61.0 17.1 all-gather.7

commit v2 on v1

v2 whole, which is shorter than its diff:
```python
import jax
import jax.numpy as jnp
from jax import lax
from jax.experimental import pallas as pl
from jax.experimental.pallas import tpu as pltpu
from jax.sharding import Mesh, PartitionSpec as P

B = 128
VM = pl.BlockSpec(memory_space=pltpu.VMEM)
SM = pl.BlockSpec(memory_space=pltpu.SMEM)
BF = jnp.bfloat16
F32 = jnp.float32


def sds(shape, dtype=BF):
    return jax.ShapeDtypeStruct(shape, dtype)


def call(kernel, specs, args, outs, scratch=(), flops=0, mib=24):
    nbytes = sum(a.size * a.dtype.itemsize for a in list(args) + list(outs))
    return pl.pallas_call(
        kernel,
        out_shape=tuple(outs),
        in_specs=[(VM, SM, pl.BlockSpec(memory_space=pltpu.HBM))[s] for s in specs],
        out_specs=tuple(VM for _ in outs),
        scratch_shapes=list(scratch),
        compiler_params=pltpu.CompilerParams(vmem_limit_bytes=mib * 1024 * 1024),
        cost_estimate=pl.CostEstimate(flops=flops, bytes_accessed=nbytes, transcendentals=0),
    )(*args)


def cells(mask, tile, down):
    slot = jnp.int32(0)
    for cc in range(7):
        for rr in range(2):
            on = mask[cc, 2 * tile + rr] if down else mask[2 * tile + rr, cc]
            yield rr, cc, on == 1, jnp.minimum(slot, 6)
            slot = slot + on
    yield None, None, slot, None


def sub(rr, cc, down):
    a, b = (cc, rr) if down else (rr, cc)
    return pl.ds(a * B, B), pl.ds(b * B, B)


def pack(mask, tile, down, source, out):
    for rr, cc, on, slot in cells(mask, tile, down):
        if rr is None:
            for p in range(5, 7):

                @pl.when(on <= p)
                def _(p=p):
                    out[p] = jnp.zeros((B, B), out.dtype)

        else:

            @pl.when(on)
            def _(rr=rr, cc=cc, slot=slot):
                out[slot] = source[sub(rr, cc, down)].astype(out.dtype)


def unpack(mask, tile, down, block, store):
    for rr, cc, on, slot in cells(mask, tile, down):
        if rr is not None:
            found = block(slot)
            store(rr, cc, jnp.where(on, found, jnp.zeros_like(found)))


def k_pack(pos, gm, um, dm, gw, uw, dw, gp, up, dp, gv, uv, dv, sems):
    tile = pos[0] * 4 + pos[1]
    copies = [
        pltpu.make_async_copy(src, dst, sems.at[i])
        for i, (src, dst) in enumerate(((dw, dv), (gw, gv), (uw, uv)))
    ]
    for c in copies:
        c.start()
    copies[0].wait()
    pack(dm, tile, True, dv, dp)
    copies[1].wait()
    pack(gm, tile, False, gv, gp)
    copies[2].wait()
    pack(um, tile, False, uv, up)


def assemble(pos, mine, other, which, out):
    x, h, k = pos[2], pos[3], pos[4]
    for s in range(4):
        rows = pl.ds(pl.multiple_of(jnp.bitwise_xor(x, s) * B, B), B)
        for a in range(2):
            for b, piece in enumerate((mine, other)):
                q = 2 * jnp.bitwise_xor(h, a) + jnp.bitwise_xor(k, b)
                out[rows, columns(q)] = piece[s, a, which]


def dense_tile_rows(y, mask, panel, dense):
    for z in range(4):

        def store(rr, cc, v):
            dense[z * 256 + rr * B : z * 256 + (rr + 1) * B, cc * B : (cc + 1) * B] = v

        unpack(mask, 4 * y + z, False, lambda s: panel[z, s], store)


def shares(y, acc, outs, at=()):
    outs[0][at + (Ellipsis,)] = acc[y]
    for j in (1, 2, 3):
        outs[j][at + (Ellipsis,)] = acc[jnp.bitwise_xor(y, j)].astype(BF)


def k_grad_gate(pos, dm, gm, dp, gp, mine, other, o0, o1, o2, o3, wd, wg, cot, tok, acc):
    y = pos[0]
    for z in range(4):

        def store(rr, cc, v):
            wd[z, cc * B : (cc + 1) * B, rr * B : (rr + 1) * B] = v

        unpack(dm, 4 * y + z, True, lambda s: dp[z, s], store)
    assemble(pos, mine, other, 1, cot)
    got = None
    for q in range(4):
        term = lax.dot_general(
            cot[:, q * 256 : (q + 1) * 256], wd[q], NT, preferred_element_type=F32
        )
        got = term if got is None else got + term
    acc[...] = got.reshape(4, B, 896)
    shares(y, acc, (o0, o1, o2, o3), (0,))
    dense_tile_rows(y, gm, gp, wg)
    assemble(pos, mine, other, 0, tok)
    got = jnp.dot(tok[...], wg[...], preferred_element_type=F32)
    acc[...] = got.reshape(4, B, 896)
    shares(y, acc, (o0, o1, o2, o3), (1,))


def k_up(pos, mask, panel, tok, o0, o1, o2, o3, dense, acc):
    dense_tile_rows(pos[0], mask, panel, dense)
    got = jnp.dot(tok[...], dense[...], preferred_element_type=F32)
    acc[...] = got.reshape(4, B, 896)
    shares(pos[0], acc, (o0, o1, o2, o3))


def total(own, *others):
    out = own[...]
    for o in others:
        out = out + o[...].astype(F32)
    return out


def k_act(a0, a1, a2, a3, b0, b1, b2, b3, hid, act):
    both = total(a0, a1, a2, a3)
    grad, gate = both[0], both[1]
    up = total(b0, b1, b2, b3)
    sig = jax.nn.sigmoid(gate)
    hid[...] = (gate * sig * up).astype(BF)
    act[0] = (grad * up * sig * (1.0 + gate * (1.0 - sig))).astype(BF)
    act[1] = (grad * (gate * sig)).astype(BF)


def columns(q):
    return pl.ds(pl.multiple_of(q * 256, 256), 256)


TN = (((0,), (0,)), ((), ()))
NT = (((1,), (1,)), ((), ()))


def k_down_grad(pos, dm, hid, cot, d0, d1, d2, d3, acc):
    y, z = pos[0], pos[1]
    left = hid[...].reshape(512, 896)
    for j, out in ((1, d1), (2, d2), (3, d3), (0, d0)):
        zz = jnp.bitwise_xor(z, j)
        acc[...] = lax.dot_general(left, cot[:, columns(zz)], TN, preferred_element_type=F32)
        pack(dm, 4 * y + zz, True, acc, out)


def k_weight_grad(pos, gm, um, act, tok, d0, d1, d2, d3, acc):
    y, z = pos[0], pos[1]
    for half, mask in enumerate((gm, um)):
        right = act[:, half].reshape(512, 896)
        for j, out in ((1, d1), (2, d2), (3, d3), (0, d0)):
            zz = jnp.bitwise_xor(z, j)
            acc[...] = lax.dot_general(tok[:, columns(zz)], right, TN, preferred_element_type=F32)
            pack(mask, 4 * y + zz, False, acc, out.at[half])


def k_out(pos, hid, wd, keep, send):
    k = pos[4]
    left = hid[...].reshape(512, 896)
    for out, kk in ((send, 1 - k), (keep, k)):
        for h in range(2):
            got = jnp.dot(left, wd[2 * h + kk], preferred_element_type=F32)
            out[:, h] = got.reshape(4, B, 256).astype(out.dtype)


def k_in(pos, act, wg, wu, keep, send):
    k = pos[4]
    gact, uact = act[:, 0].reshape(512, 896), act[:, 1].reshape(512, 896)
    for out, kk in ((send, 1 - k), (keep, k)):
        for h in range(2):
            rows = columns(2 * h + kk)
            got = lax.dot_general(gact, wg[rows, :], NT, preferred_element_type=F32)
            got = got + lax.dot_general(uact, wu[rows, :], NT, preferred_element_type=F32)
            out[:, h] = got.reshape(4, B, 256).astype(out.dtype)


def k_sum_core(pos, keep, got, o0, o1, o2, o3):
    x = pos[2]
    for j, out in enumerate((o0, o1, o2, o3)):
        at = jnp.bitwise_xor(x, j)
        out[...] = (keep[at] + got[at].astype(F32)).astype(out.dtype)


def k_sum_x(pos, a0, a1, a2, a3, keep, send, acc):
    h = pos[3]
    acc[...] = total(a0, a1, a2, a3)
    keep[...] = acc[h].astype(BF)
    send[...] = acc[1 - h].astype(BF)


def k_sum_x_join(pos, a0, a1, a2, a3, first, second, keep, send, acc):
    h = pos[3]
    acc[...] = total(a0, a1, a2, a3)
    keep[0] = first[...]
    keep[1] = acc[h].astype(BF)
    send[0] = second[...]
    send[1] = acc[1 - h].astype(BF)


def k_sum_pair(a, b, out, grad):
    both = a[...].astype(F32) + b[...].astype(F32)
    out[...] = both[0].astype(BF)
    grad[...] = both[1].astype(BF)


def k_place(pos, mask, a0, a1, a2, a3, out, *, down, at):
    tile = pos[0] * 4 + pos[1]

    def block(s):
        return total(a0.at[at + (s,)], a1.at[at + (s,)], a2.at[at + (s,)], a3.at[at + (s,)])

    def store(rr, cc, v):
        out[sub(rr, cc, down)] = v.astype(BF)

    unpack(mask, tile, down, block, store)


def exchange(value, axis, by, size=4):
    return lax.ppermute(value, axis, [(i, i ^ by) for i in range(size)])


def spread(value, axis):
    return [value] + [exchange(value, axis, j) for j in (1, 2, 3)]


def collect(own, others, axis):
    return [own] + [exchange(v, axis, j) for j, v in zip((1, 2, 3), others)]


def swap(value, flip):
    pairs = [
        ((y * 4 + x) * 2 + h, (x * 4 + y) * 2 + (h ^ flip))
        for y in range(4)
        for x in range(4)
        for h in range(2)
    ]
    return lax.ppermute(value, ("y", "x", "h"), pairs)


def body(tokens, cotangent, gate_weight, up_weight, down_weight, gate_mask, up_mask, down_mask):
    pos = jnp.stack([lax.axis_index(a) for a in ("y", "z", "x", "h", "k")]).astype(jnp.int32)
    masks = (gate_mask, up_mask, down_mask)
    both = jnp.stack([tokens, cotangent])
    pair = jnp.stack([swap(both, 0), swap(both, 1)])
    packed = sds((7, B, B))
    gp, up, dp = call(
        k_pack, (1, 1, 1, 1, 2, 2, 2),
        (pos, *masks, gate_weight, up_weight, down_weight), (packed,) * 3,
        (pltpu.VMEM((256, 896), BF), pltpu.VMEM((256, 896), BF), pltpu.VMEM((896, 256), BF),
         pltpu.SemaphoreType.DMA((3,))),
    )
    dp, pair = lax.optimization_barrier((dp, pair))
    mine = spread(pair, "x")
    dp = lax.all_gather(dp, "z", axis=0)
    gp, dp, mine = lax.optimization_barrier((gp, dp, mine))
    mine = jnp.stack(mine)
    other = exchange(mine, "k", 1, 2)
    gp = lax.all_gather(gp, "z", axis=0)
    acc = pltpu.VMEM((4, B, 896), F32)
    flops = 2 * 512 * 1024 * 896
    blk = (2, B, 896)
    g = call(
        k_grad_gate, (1, 1, 1, 0, 0, 0, 0), (pos, down_mask, gate_mask, dp, gp, mine, other),
        (sds(blk, F32), sds(blk), sds(blk), sds(blk),
         sds((4, 896, 256)), sds((1024, 896)), sds((512, 1024)), sds((512, 1024))),
        (acc,), flops=2 * flops,
    )
    wd, wg, cot, tok = g[4:]
    g_all = collect(g[0], g[1:4], "y")
    up, _ = lax.optimization_barrier((up, g[1]))
    up = lax.all_gather(up, "z", axis=0)
    up, g_all = lax.optimization_barrier((up, g_all))
    blk = (B, 896)
    u = call(
        k_up, (1, 1, 0, 0), (pos, up_mask, up, tok),
        (sds(blk, F32), sds(blk), sds(blk), sds(blk), sds((1024, 896))), (acc,), flops=flops,
    )
    wu = u[4]
    u_all = collect(u[0], u[1:4], "y")
    hidden, act = call(k_act, (0,) * 8, (*g_all, *u_all), (sds(blk), sds((2, B, 896))))
    act = lax.all_gather(act, "y", axis=0)
    hidden = lax.all_gather(hidden, "y", axis=0)
    blk = (7, B, B)
    e = call(
        k_down_grad, (1, 1, 0, 0), (pos, down_mask, hidden, cot),
        (sds(blk, F32), sds(blk), sds(blk), sds(blk)),
        (pltpu.VMEM((896, 256), F32),), flops=flops,
    )
    e_all = collect(e[0], e[1:4], "z")
    half, part, one = (4, 2, B, 256), (2, B, 256), (B, 256)

    def sum_core(keep, got):
        return call(
            k_sum_core, (1, 0, 0), (pos, keep, got),
            (sds(part, F32), sds(part), sds(part), sds(part)),
        )

    hidden, _ = lax.optimization_barrier((hidden, e[1]))
    keep, send = call(
        k_out, (1, 0, 0), (pos, hidden, wd), (sds(half, F32), sds(half)), flops=flops
    )
    got = exchange(send, "k", 1, 2)
    s = sum_core(keep, got)
    s_all = collect(s[0], s[1:], "x")
    own, other = call(
        k_sum_x, (1, 0, 0, 0, 0), (pos, *s_all), (sds(one), sds(one)), (pltpu.VMEM(part, F32),)
    )
    act, e_all, own = lax.optimization_barrier((act, e_all, own))
    keep, send = call(
        k_in, (1, 0, 0, 0), (pos, act, wg, wu), (sds(half, F32), sds(half)), flops=2 * flops
    )
    got = exchange(send, "k", 1, 2)
    act, keep = lax.optimization_barrier((act, keep))
    blk = (2, 7, B, B)
    f = call(
        k_weight_grad, (1, 1, 1, 0, 0), (pos, gate_mask, up_mask, act, tok),
        (sds(blk, F32), sds(blk), sds(blk), sds(blk)),
        (pltpu.VMEM((256, 896), F32),), flops=2 * flops,
    )
    f_all = collect(f[0], f[1:4], "z")
    keep, _ = lax.optimization_barrier((keep, f[1]))
    s = sum_core(keep, got)
    own, other = call(
        k_sum_x_join, (1,) + (0,) * 6, (pos, *collect(s[0], s[1:], "x"), own, other),
        (sds((2, B, 256)), sds((2, B, 256))), (pltpu.VMEM(part, F32),),
    )
    output, input_grad = call(
        k_sum_pair, (0, 0), (swap(own, 0), swap(other, 1)), (sds((B, 256)),) * 2
    )

    def place(mask, parts, down, at, shape):
        def kernel(*refs):
            k_place(*refs, down=down, at=at)

        return call(kernel, (1, 1, 0, 0, 0, 0), (pos, mask, *parts), (sds(shape),))[0]

    down_grad = place(down_mask, e_all, True, (), (896, 256))
    gate_grad = place(gate_mask, f_all, False, (0,), (256, 896))
    up_grad = place(up_mask, f_all, False, (1,), (256, 896))
    return (output, input_grad, gate_grad, up_grad, down_grad)


def solution(mesh):
    mesh = Mesh(mesh.devices.reshape(4, 4, 4, 2, 2), ("y", "z", "x", "h", "k"))
    row, col = ("y", "z"), ("x", "h", "k")
    return jax.shard_map(
        body,
        mesh=mesh,
        in_specs=(
            P(row, col),
            P(row, col),
            P(row, col),
            P(row, col),
            P(col, row),
            P(None, col),
            P(None, col),
            P(col, None),
        ),
        out_specs=(P(row, col), P(row, col), P(row, col), P(row, col), P(col, row)),
        check_vma=False,
    )
```

time: 297 us -> 245 us (0.82); the launches traced: 292 us -> 245 us
  waiting for transfers between devices: 156 us -> 58 us
  blocking collectives: 12.5 us -> 74.7 us
  starting transfers between devices: 74.1 us -> 50.5 us
  local copies, waits for them, and re-layouts: 3.14 us -> 13.1 us
    ppermute x34 -> x24, waiting for transfers between devices: 121 us -> 57.9 us  [exchange(): return lax.ppermute(value, axis, [(i, i ^ by) for i in range(size)])]
    all_gather x1 -> x4, blocking collectives: 12.5 us -> 74.7 us  [the longest x1 20.7 us: body(): dp = lax.all_gather(dp, 'z', axis=0)]
    ppermute x34 -> x24, starting transfers between devices: 64 us -> 30 us  [exchange(): return lax.ppermute(value, axis, [(i, i ^ by) for i in range(size)])]
    all_gather x2 -> x1, waiting for transfers between devices: 30.3 us -> 0.01 us  [body(): act = lax.all_gather(act, 'y', axis=0)]
    ppermute x3 -> x4, starting transfers between devices: 10 us -> 20.5 us  [swap(): return lax.ppermute(value, ('y', 'x', 'h'), pairs)]
    unnamed x20 -> x32, local copies, waits for them, and re-layouts: 3.06 us -> 13.1 us
    ppermute x3 -> x4, waiting for transfers between devices: 4.57 us -> 0.01 us  [swap(): return lax.ppermute(value, ('y', 'x', 'h'), pairs)]
    pallas_call x18 -> x16, Pallas kernels: 30.7 us -> 32.9 us  [call(): pl.pallas_call(kernel, out_shape=tuple(outs), in_specs=[(VM, SM, pl.Block...]
  transfers between devices with their start and end apart: 39 -> 29, of which waited for: 19 -> 14; matrix products, arithmetic and copies ran while one was open for 0% -> 1% of each run, Pallas kernels for 11% -> 9%
where the time goes in v2:
time: 245 us
  blocking collectives  74.7 us (30%)
  waiting for transfers between devices  58 us (24%)
  starting transfers between devices  50.5 us (21%)
  Pallas kernels  32.9 us (13%)
  between operations  14.3 us (6%)
  local copies, waits for them, and re-layouts  13.1 us (5%)
    ppermute x24, waiting for transfers between devices, exchange(): return lax.ppermute(value, axis, [(i, i ^ by) for i in range(size)])  57.9 us
    pallas_call x16, Pallas kernels, call(): pl.pallas_call(kernel, out_shape=tuple(outs), in_specs=[(VM, SM, pl.Block...  32.9 us
    ppermute x24, starting transfers between devices, exchange(): return lax.ppermute(value, axis, [(i, i ^ by) for i in range(size)])  30 us
    all_gather x1, blocking collectives, body(): dp = lax.all_gather(dp, 'z', axis=0)  20.7 us
    ppermute x4, starting transfers between devices, swap(): return lax.ppermute(value, ('y', 'x', 'h'), pairs)  20.5 us
    all_gather x1, blocking collectives, body(): gp = lax.all_gather(gp, 'z', axis=0)  20.3 us
    all_gather x1, blocking collectives, body(): up = lax.all_gather(up, 'z', axis=0)  19 us
    all_gather x1, blocking collectives, body(): hidden = lax.all_gather(hidden, 'y', axis=0)  14.8 us
  transfers between devices with their start and end apart: 29, of which 14 were waited for; matrix products, arithmetic and copies ran while one was open for 1% of the time, Pallas kernels for 9%

profile of v2, /device:TPU:34, one launch (start us, length us, event | category | flops | bytes accessed | tf_op | source)
XLA Modules:
  0.0 244.5 jit_solution(11855827074830384386)
XLA Ops:
  8.1 7.4 %collective-permute-start.1 = (bf16[2,128,256]{2,1,0:T(8,128)(2,1)S(1)}, bf16[2,128,256]{2,1,0:T(8,128)(2,1)S(1)}, u32[]{:S(2)}, u32[]{:S(2)}) collective-permute-start(bf16[2,128,256]{2,1,0:T(8,128)(2,1)S(1)} %pad_maximum_fusion.2), channel_id=1, source_target_pairs={{0,2},{2,0},{4,66},{6,64},{8,130},{10,128},{12,194},{14,192},{64,6... | collective-permute-start | bytes 393224 | tf_op jit(solution)/shard_map/ppermute | solution.py:266
  15.5 3.3 %collective-permute-start = (bf16[2,128,256]{2,1,0:T(8,128)(2,1)S(1)}, bf16[2,128,256]{2,1,0:T(8,128)(2,1)S(1)}, u32[]{:S(2)}, u32[]{:S(2)}) collective-permute-start(bf16[2,128,256]{2,1,0:T(8,128)(2,1)S(1)} %pad_maximum_fusion.2), channel_id=1, source_target_pairs={{0,0},{2,2},{4,64},{6,66},{8,128},{10,130},{12,192},{14,194},{64,4... | collective-permute-start | bytes 393224 | tf_op jit(solution)/shard_map/ppermute | solution.py:266
  24.1 2.4 shard_map.119
  26.6 5.0 %collective-permute-start.4 = (bf16[2,2,128,256]{3,2,1,0:T(8,128)(2,1)S(1)}, bf16[2,2,128,256]{3,2,1,0:T(8,128)(2,1)S(1)}, u32[]{:S(2)}, u32[]{:S(2)}) collective-permute-start(bf16[2,2,128,256]{3,2,1,0:T(8,128)(2,1)S(1)} %pad_maximum_fusion.1), channel_id=1, source_target_pairs={{0,12},{4,8},{8,4},{12,0},{1,13},{5,9},{9,5},{13,1},{2,14},{6,10},... | collective-permute-start | bytes 786440 | tf_op jit(solution)/shard_map/ppermute | solution.py:248
  32.3 1.5 collective-permute-start.2
  33.8 20.7 %all-gather = bf16[28,128,128]{2,1,0:T(8,128)(2,1)S(1)} all-gather(bf16[7,128,128]{2,1,0:T(8,128)(2,1)S(1)} %get-tuple-element.76), channel_id=2, replica_groups=mesh['y'=4,'z'=4,'x'=4,'h'=2,'k'=2] {'z'}, dimensions={0}, use_global_device_ids=true | all-gather | bytes 1146880 | tf_op jit(solution)/shard_map/all_gather | solution.py:283
  54.8 20.3 %all-gather.1 = bf16[28,128,128]{2,1,0:T(8,128)(2,1)S(1)} all-gather(bf16[7,128,128]{2,1,0:T(8,128)(2,1)S(1)} %get-tuple-element.79), channel_id=3, replica_groups=mesh['y'=4,'z'=4,'x'=4,'h'=2,'k'=2] {'z'}, dimensions={0}, use_global_device_ids=true | all-gather | bytes 1146880 | tf_op jit(solution)/shard_map/all_gather | solution.py:287
  75.0 3.9 %shard_map.120 = (f32[2,128,896]{2,1,0:T(8,128)S(1)}, bf16[2,128,896]{2,1,0:T(8,128)(2,1)S(1)}, bf16[2,128,896]{2,1,0:T(8,128)(2,1)S(1)}, bf16[2,128,896]{2,1,0:...) custom-call(s32[5]{0:T(128)S(1)} %stack.56.pos.refs_0_, ...), custom_call_target="tpu_custom_call" | custom-call | flops 1879048192 | bytes 11994900 | tf_op jit(solution)/shard_map/pallas_call | solution.py:21
  79.0 1.3 copy-done.7
  81.3 1.3 collective-permute-start.7
  82.5 1.4 collective-permute-start.8
  84.8 19.0 %all-gather.2 = bf16[28,128,128]{2,1,0:T(8,128)(2,1)S(1)} all-gather(bf16[7,128,128]{2,1,0:T(8,128)(2,1)S(1)} %get-tuple-element.85), channel_id=4, replica_groups=mesh['y'=4,'z'=4,'x'=4,'h'=2,'k'=2] {'z'}, dimensions={0}, use_global_device_ids=true | all-gather | bytes 1146880 | tf_op jit(solution)/shard_map/all_gather | solution.py:300
  104.1 2.3 shard_map.121
  106.5 1.2 copy-done.9
  108.6 2.0 collective-permute-start.10
  110.5 1.9 collective-permute-start.11
  112.4 3.8 %collective-permute-done.9.b1 = bf16[128,896]{1,0:T(8,128)(2,1)S(1)} collective-permute-done((bf16[128,896]{1,0:T(8,128)(2,1)S(1)}, bf16[128,896]{1,0:T(8,128)(2,1)S(1)}, u32[]{:S(2)}, u32[]{:S(2)}) %collective-permute-start.9) | collective-permute-done | bytes 229408 | tf_op jit(solution)/shard_map/ppermute | solution.py:248
  116.2 4.9 %collective-permute-done.10.b2 = bf16[128,896]{1,0:T(8,128)(2,1)S(1)} collective-permute-done((bf16[128,896]{1,0:T(8,128)(2,1)S(1)}, bf16[128,896]{1,0:T(8,128)(2,1)S(1)}, u32[]{:S(2)}, u32[]{:S(2)}) %collective-permute-start.10) | collective-permute-done | bytes 229408 | tf_op jit(solution)/shard_map/ppermute | solution.py:248
  121.1 2.6 %collective-permute-done.11.b3 = bf16[128,896]{1,0:T(8,128)(2,1)S(1)} collective-permute-done((bf16[128,896]{1,0:T(8,128)(2,1)S(1)}, bf16[128,896]{1,0:T(8,128)(2,1)S(1)}, u32[]{:S(2)}, u32[]{:S(2)}) %collective-permute-start.11) | collective-permute-done | bytes 229408 | tf_op jit(solution)/shard_map/ppermute | solution.py:248
  123.6 1.2 shard_map.122
  124.9 14.8 %all-gather.4 = bf16[512,896]{1,0:T(8,128)(2,1)S(1)} all-gather(bf16[128,896]{1,0:T(8,128)(2,1)S(1)} %get-tuple-element.100), channel_id=6, replica_groups=mesh['y'=4,'z'=4,'x'=4,'h'=2,'k'=2] {'y'}, dimensions={0}, use_global_device_ids=true | all-gather | bytes 1146880 | tf_op jit(solution)/shard_map/all_gather | solution.py:311
  140.9 3.7 %shard_map.123 = (f32[7,128,128]{2,1,0:T(8,128)S(1)}, bf16[7,128,128]{2,1,0:T(8,128)(2,1)S(1)}, bf16[7,128,128]{2,1,0:T(8,128)(2,1)S(1)}, bf16[7,128,128]{2,1,0:T(8,128)(2,1)S(1)}) custom-call(s32[5]{0:T(128)S(1)} %stack.56.pos.refs_0_, s32[7,32]{1,0:T(8,128)S(1)} %copy-done.4, bf16[4,128,896]{2,1,0:T(8,128)(2,1)S(1)} %bitcast.21, ...), custom_call_target="tpu_custom_call" | custom-call | flops 939524096 | bytes 3113876 | tf_op jit(solution)/shard_map/pallas_call | solution.py:21
  144.6 1.8 shard_map.124
  146.5 1.9 collective-permute-done.15.got
  150.0 2.7 %collective-permute-start.13 = (bf16[7,128,128]{2,1,0:T(8,128)(2,1)S(1)}, bf16[7,128,128]{2,1,0:T(8,128)(2,1)S(1)}, u32[]{:S(2)}, u32[]{:S(2)}) collective-permute-start(bf16[7,128,128]{2,1,0:T(8,128)(2,1)S(1)} %get-tuple-element.104), channel_id=1, source_target_pairs={{0,32},{16,48},{32,0},{48,16},{1,33},{17,49},{33,1},{49,17},{2,34}... | collective-permute-start | bytes 688136 | tf_op jit(solution)/shard_map/ppermute | solution.py:248
  152.7 1.7 collective-permute-start.14
  155.4 1.6 collective-permute-start.18
  157.0 3.9 %collective-permute-done.17.a2 = bf16[2,128,256]{2,1,0:T(8,128)(2,1)S(1)} collective-permute-done((bf16[2,128,256]{2,1,0:T(8,128)(2,1)S(1)}, bf16[2,128,256]{2,1,0:T(8,128)(2,1)S(1)}, u32[]{:S(2)}, u32[]{:S(2)}) %collective-permute-start.17) | collective-permute-done | bytes 131104 | tf_op jit(solution)/shard_map/ppermute | solution.py:248
  160.9 1.7 collective-permute-done.18.a3
  163.3 4.2 %collective-permute-done.13.refs_4_ = bf16[7,128,128]{2,1,0:T(8,128)(2,1)S(1)} collective-permute-done((bf16[7,128,128]{2,1,0:T(8,128)(2,1)S(1)}, bf16[7,128,128]{2,1,0:T(8,128)(2,1)S(1)}, u32[]{:S(2)}, u32[]{:S(2)}) %collective-permute-start.13) | collective-permute-done | bytes 229408 | tf_op jit(solution)/shard_map/ppermute | solution.py:248
  167.5 5.6 %collective-permute-done.14.refs_5_ = bf16[7,128,128]{2,1,0:T(8,128)(2,1)S(1)} collective-permute-done((bf16[7,128,128]{2,1,0:T(8,128)(2,1)S(1)}, bf16[7,128,128]{2,1,0:T(8,128)(2,1)S(1)}, u32[]{:S(2)}, u32[]{:S(2)}) %collective-permute-start.14) | collective-permute-done | bytes 229408 | tf_op jit(solution)/shard_map/ppermute | solution.py:248
  173.2 1.5 copy-done.5
  174.7 1.5 copy-done.10
  176.2 2.9 %shard_map.127 = (f32[4,2,128,256]{3,2,1,0:T(8,128)S(1)}, bf16[4,2,128,256]{3,2,1,0:T(8,128)(2,1)S(1)}) custom-call(s32[5]{0:T(128)S(1)} %stack.56.pos.refs_0_, bf16[4,2,128,896]{3,2,1,0:T(8,128)(2,1)S(1)} %bitcast.23, bf16[1024,896]{1,0:T(8,128)(2,1)S(1)} %copy-done.8, bf16[1024,896]{1,0:T(8,128)(2,1)S(1)} %copy-done.10), custom_call_target="tpu_custom_call" | custom-call | flops 1879048192 | bytes 7077908 | tf_op jit(solution)/shard_map/pallas_call | solution.py:21
  179.2 6.1 %shard_map.128 = (f32[2,7,128,128]{3,2,1,0:T(8,128)S(1)}, bf16[2,7,128,128]{3,2,1,0:T(8,128)(2,1)S(1)}, bf16[2,7,128,128]{3,2,1,0:T(8,128)(2,1)S(1)}, bf16[2,7,128,128]{3,2,1,0:T(8,128)(2,1)S(1)}) custom-call(s32[5]{0:T(128)S(1)} %stack.56.pos.refs_0_, s32[32,7]{1,0:T(8,128)S(1)} %copy.21.gm.refs_1_, s32[32,7]{1,0:T(8,128)S(1)} %copy.22.um.mask.refs_1_, ...), custom_call_target="tpu_custom_call" | custom-call | flops 1879048192 | bytes 5179156 | tf_op jit(solution)/shard_map/pallas_call | solution.py:21
  185.4 1.7 collective-permute-start.27
  187.2 2.6 %collective-permute-start.25 = (bf16[2,7,128,128]{3,2,1,0:T(8,128)(2,1)S(1)}, bf16[2,7,128,128]{3,2,1,0:T(8,128)(2,1)S(1)}, u32[]{:S(2)}, u32[]{:S(2)}) collective-permute-start(bf16[2,7,128,128]{3,2,1,0:T(8,128)(2,1)S(1)} %get-tuple-element.121), channel_id=1, source_target_pairs={{0,16},{16,0},{32,48},{48,32},{1,17},{17,1},{33,49},{49,33},{2,18}... | collective-permute-start | bytes 1376264 | tf_op jit(solution)/shard_map/ppermute | solution.py:248
  190.4 1.4 collective-permute-start.20
  192.3 4.5 %collective-permute-done.20.a1 = bf16[2,128,256]{2,1,0:T(8,128)(2,1)S(1)} collective-permute-done((bf16[2,128,256]{2,1,0:T(8,128)(2,1)S(1)}, bf16[2,128,256]{2,1,0:T(8,128)(2,1)S(1)}, u32[]{:S(2)}, u32[]{:S(2)}) %collective-permute-start.20) | collective-permute-done | bytes 131104 | tf_op jit(solution)/shard_map/ppermute | solution.py:248
  196.8 1.6 collective-permute-done.21.a2
  198.4 3.4 %collective-permute-done.22.a3 = bf16[2,128,256]{2,1,0:T(8,128)(2,1)S(1)} collective-permute-done((bf16[2,128,256]{2,1,0:T(8,128)(2,1)S(1)}, bf16[2,128,256]{2,1,0:T(8,128)(2,1)S(1)}, u32[]{:S(2)}, u32[]{:S(2)}) %collective-permute-start.22) | collective-permute-done | bytes 131104 | tf_op jit(solution)/shard_map/ppermute | solution.py:248
  202.4 6.0 %collective-permute-start.23 = (bf16[2,128,256]{2,1,0:T(8,128)(2,1)S(1)}, bf16[2,128,256]{2,1,0:T(8,128)(2,1)S(1)}, u32[]{:S(2)}, u32[]{:S(2)}) collective-permute-start(bf16[2,128,256]{2,1,0:T(8,128)(2,1)S(1)} %get-tuple-element.130), channel_id=1, source_target_pairs={{0,0},{2,2},{4,64},{6,66},{8,128},{10,130},{12,192},{14,194},{64,4... | collective-permute-start | bytes 393224 | tf_op jit(solution)/shard_map/ppermute | solution.py:266
  208.4 3.9 %collective-permute-start.24 = (bf16[2,128,256]{2,1,0:T(8,128)(2,1)S(1)}, bf16[2,128,256]{2,1,0:T(8,128)(2,1)S(1)}, u32[]{:S(2)}, u32[]{:S(2)}) collective-permute-start(bf16[2,128,256]{2,1,0:T(8,128)(2,1)S(1)} %get-tuple-element.131), channel_id=1, source_target_pairs={{0,2},{2,0},{4,66},{6,64},{8,130},{10,128},{12,194},{14,192},{64,6... | collective-permute-start | bytes 393224 | tf_op jit(solution)/shard_map/ppermute | solution.py:266
  212.3 1.6 shard_map.134
  213.9 2.1 collective-permute-done.26.refs_4_
  216.0 17.4 %collective-permute-done.27.refs_5_ = bf16[2,7,128,128]{3,2,1,0:T(8,128)(2,1)S(1)} collective-permute-done((bf16[2,7,128,128]{3,2,1,0:T(8,128)(2,1)S(1)}, bf16[2,7,128,128]{3,2,1,0:T(8,128)(2,1)S(1)}, u32[]{:S(2)}, u32[]{:S(2)}) %collective-permute-start.27) | collective-permute-done | bytes 458784 | tf_op jit(solution)/shard_map/ppermute | solution.py:248
  233.4 1.8 shard_map.133
  235.2 1.8 shard_map.132
  (67 shorter events, 17.5 us)
Async XLA Ops:
  7.2 166.0 %all-gather.7.cloned.1.call-start = ((), (), s32[]{:S(2)}) async-start(), calls=%async_computation | async-start | bytes 2293760 | tf_op jit(solution)/shard_map/all_gather | solution.py:310
  8.1 18.5 %collective-permute-start.1 = (bf16[2,128,256]{2,1,0:T(8,128)(2,1)S(1)}, bf16[2,128,256]{2,1,0:T(8,128)(2,1)S(1)}, u32[]{:S(2)}, u32[]{:S(2)}) collective-permute-start(bf16[2,128,256]{2,1,0:T(8,128)(2,1)S(1)} %pad_maximum_fusion.2), channel_id=1, source_target_pairs={{0,2},{2,0},{4,66},{6,64},{8,130},{10,128},{12,194},{14,192},{64,6... | collective-permute-start | bytes 393224 | tf_op jit(solution)/shard_map/ppermute | solution.py:266
  15.5 11.1 %collective-permute-start = (bf16[2,128,256]{2,1,0:T(8,128)(2,1)S(1)}, bf16[2,128,256]{2,1,0:T(8,128)(2,1)S(1)}, u32[]{:S(2)}, u32[]{:S(2)}) collective-permute-start(bf16[2,128,256]{2,1,0:T(8,128)(2,1)S(1)} %pad_maximum_fusion.2), channel_id=1, source_target_pairs={{0,0},{2,2},{4,64},{6,66},{8,128},{10,130},{12,192},{14,194},{64,4... | collective-permute-start | bytes 393224 | tf_op jit(solution)/shard_map/ppermute | solution.py:266
  20.4 1.0 copy-start
  21.4 1.0 copy-start.1
  22.4 1.0 copy-start.2
  23.4 0.7 copy-start.3
  26.6 27.9 %collective-permute-start.4 = (bf16[2,2,128,256]{3,2,1,0:T(8,128)(2,1)S(1)}, bf16[2,2,128,256]{3,2,1,0:T(8,128)(2,1)S(1)}, u32[]{:S(2)}, u32[]{:S(2)}) collective-permute-start(bf16[2,2,128,256]{3,2,1,0:T(8,128)(2,1)S(1)} %pad_maximum_fusion.1), channel_id=1, source_target_pairs={{0,12},{4,8},{8,4},{12,0},{1,13},{5,9},{9,5},{13,1},{2,14},{6,10},... | collective-permute-start | bytes 786440 | tf_op jit(solution)/shard_map/ppermute | solution.py:248
  31.6 22.9 %collective-permute-start.3 = (bf16[2,2,128,256]{3,2,1,0:T(8,128)(2,1)S(1)}, bf16[2,2,128,256]{3,2,1,0:T(8,128)(2,1)S(1)}, u32[]{:S(2)}, u32[]{:S(2)}) collective-permute-start(bf16[2,2,128,256]{3,2,1,0:T(8,128)(2,1)S(1)} %pad_maximum_fusion.1), channel_id=1, source_target_pairs={{0,8},{4,12},{8,0},{12,4},{1,9},{5,13},{9,1},{13,5},{2,10},{6,14},... | collective-permute-start | bytes 786440 | tf_op jit(solution)/shard_map/ppermute | solution.py:248
  32.3 22.2 %collective-permute-start.2 = (bf16[2,2,128,256]{3,2,1,0:T(8,128)(2,1)S(1)}, bf16[2,2,128,256]{3,2,1,0:T(8,128)(2,1)S(1)}, u32[]{:S(2)}, u32[]{:S(2)}) collective-permute-start(bf16[2,2,128,256]{3,2,1,0:T(8,128)(2,1)S(1)} %pad_maximum_fusion.1), channel_id=1, source_target_pairs={{0,4},{4,0},{8,12},{12,8},{1,5},{5,1},{9,13},{13,9},{2,6},{6,2},{1... | collective-permute-start | bytes 786440 | tf_op jit(solution)/shard_map/ppermute | solution.py:248
  54.7 20.4 %collective-permute-start.5 = (bf16[4,2,2,128,256]{4,3,2,1,0:T(8,128)(2,1)S(1)}, bf16[4,2,2,128,256]{4,3,2,1,0:T(8,128)(2,1)S(1)}, u32[]{:S(2)}, u32[]{:S(2)}) collective-permute-start(bf16[4,2,2,128,256]{4,3,2,1,0:T(8,128)(2,1)S(1)} %pad_maximum_fusion.mine), channel_id=1, source_target_pairs={{0,1},{1,0},{2,3},{3,2},{4,5},{5,4},{6,7},{7,6},{8,9},{9,8},{10,11... | collective-permute-start | bytes 3145736 | tf_op jit(solution)/shard_map/ppermute | solution.py:248
  79.0 1.3 copy-start.7
  80.3 1.0 copy-start.13
  81.3 25.2 %copy-start.11 = (bf16[512,1024]{1,0:T(8,128)(2,1)}, bf16[512,1024]{1,0:T(8,128)(2,1)S(1)}, u32[]{:S(2)}) copy-start(bf16[512,1024]{1,0:T(8,128)(2,1)S(1)} %get-tuple-element.94.tok) | copy-start | bytes 3145732
  81.3 22.5 %collective-permute-start.7 = (bf16[2,128,896]{2,1,0:T(8,128)(2,1)S(1)}, bf16[2,128,896]{2,1,0:T(8,128)(2,1)S(1)}, u32[]{:S(2)}, u32[]{:S(2)}) collective-permute-start(bf16[2,128,896]{2,1,0:T(8,128)(2,1)S(1)} %get-tuple-element.87), channel_id=1, source_target_pairs={{0,128},{64,192},{128,0},{192,64},{1,129},{65,193},{129,1},{193,65... | collective-permute-start | bytes 1376264 | tf_op jit(solution)/shard_map/ppermute | solution.py:248
  82.5 21.6 %collective-permute-start.8 = (bf16[2,128,896]{2,1,0:T(8,128)(2,1)S(1)}, bf16[2,128,896]{2,1,0:T(8,128)(2,1)S(1)}, u32[]{:S(2)}, u32[]{:S(2)}) collective-permute-start(bf16[2,128,896]{2,1,0:T(8,128)(2,1)S(1)} %get-tuple-element.88), channel_id=1, source_target_pairs={{0,192},{64,128},{128,64},{192,0},{1,193},{65,129},{129,65},{193,1... | collective-permute-start | bytes 1376264 | tf_op jit(solution)/shard_map/ppermute | solution.py:248
  84.0 20.2 %collective-permute-start.6 = (bf16[2,128,896]{2,1,0:T(8,128)(2,1)S(1)}, bf16[2,128,896]{2,1,0:T(8,128)(2,1)S(1)}, u32[]{:S(2)}, u32[]{:S(2)}) collective-permute-start(bf16[2,128,896]{2,1,0:T(8,128)(2,1)S(1)} %get-tuple-element.84), channel_id=1, source_target_pairs={{0,64},{64,0},{128,192},{192,128},{1,65},{65,1},{129,193},{193,129... | collective-permute-start | bytes 1376264 | tf_op jit(solution)/shard_map/ppermute | solution.py:248
  106.5 1.3 copy-start.9
  107.7 8.5 %collective-permute-start.9 = (bf16[128,896]{1,0:T(8,128)(2,1)S(1)}, bf16[128,896]{1,0:T(8,128)(2,1)S(1)}, u32[]{:S(2)}, u32[]{:S(2)}) collective-permute-start(bf16[128,896]{1,0:T(8,128)(2,1)S(1)} %get-tuple-element.96), channel_id=1, source_target_pairs={{0,64},{64,0},{128,192},{192,128},{1,65},{65,1},{129,193},{193,129... | collective-permute-start | bytes 688136 | tf_op jit(solution)/shard_map/ppermute | solution.py:248
  108.6 12.5 %collective-permute-start.10 = (bf16[128,896]{1,0:T(8,128)(2,1)S(1)}, bf16[128,896]{1,0:T(8,128)(2,1)S(1)}, u32[]{:S(2)}, u32[]{:S(2)}) collective-permute-start(bf16[128,896]{1,0:T(8,128)(2,1)S(1)} %get-tuple-element.97), channel_id=1, source_target_pairs={{0,128},{64,192},{128,0},{192,64},{1,129},{65,193},{129,1},{193,65... | collective-permute-start | bytes 688136 | tf_op jit(solution)/shard_map/ppermute | solution.py:248
  110.5 13.1 %collective-permute-start.11 = (bf16[128,896]{1,0:T(8,128)(2,1)S(1)}, bf16[128,896]{1,0:T(8,128)(2,1)S(1)}, u32[]{:S(2)}, u32[]{:S(2)}) collective-permute-start(bf16[128,896]{1,0:T(8,128)(2,1)S(1)} %get-tuple-element.98), channel_id=1, source_target_pairs={{0,192},{64,128},{128,64},{192,0},{1,193},{65,129},{129,65},{193,1... | collective-permute-start | bytes 688136 | tf_op jit(solution)/shard_map/ppermute | solution.py:248
  123.6 16.1 %copy-start.4 = (s32[7,32]{1,0:T(8,128)S(1)}, s32[7,32]{1,0:T(8,128)}, u32[]{:S(2)}) copy-start(s32[7,32]{1,0:T(8,128)} %refs_1_.3) | copy-start | bytes 2692
  139.7 1.2 copy-start.14
  146.4 26.8 %copy-start.8 = (bf16[1024,896]{1,0:T(8,128)(2,1)S(1)}, bf16[1024,896]{1,0:T(8,128)(2,1)}, u32[]{:S(2)}) copy-start(bf16[1024,896]{1,0:T(8,128)(2,1)} %copy-done.7) | copy-start | bytes 5505028
  146.4 2.0 collective-permute-start.15
  149.1 6.4 %collective-permute-start.16 = (bf16[2,128,256]{2,1,0:T(8,128)(2,1)S(1)}, bf16[2,128,256]{2,1,0:T(8,128)(2,1)S(1)}, u32[]{:S(2)}, u32[]{:S(2)}) collective-permute-start(bf16[2,128,256]{2,1,0:T(8,128)(2,1)S(1)} %get-tuple-element.111), channel_id=1, source_target_pairs={{0,4},{4,0},{8,12},{12,8},{1,5},{5,1},{9,13},{13,9},{2,6},{6,2},{1... | collective-permute-start | bytes 393224 | tf_op jit(solution)/shard_map/ppermute | solution.py:248
  150.0 17.5 %collective-permute-start.13 = (bf16[7,128,128]{2,1,0:T(8,128)(2,1)S(1)}, bf16[7,128,128]{2,1,0:T(8,128)(2,1)S(1)}, u32[]{:S(2)}, u32[]{:S(2)}) collective-permute-start(bf16[7,128,128]{2,1,0:T(8,128)(2,1)S(1)} %get-tuple-element.104), channel_id=1, source_target_pairs={{0,32},{16,48},{32,0},{48,16},{1,33},{17,49},{33,1},{49,17},{2,34}... | collective-permute-start | bytes 688136 | tf_op jit(solution)/shard_map/ppermute | solution.py:248
  152.7 20.4 %collective-permute-start.14 = (bf16[7,128,128]{2,1,0:T(8,128)(2,1)S(1)}, bf16[7,128,128]{2,1,0:T(8,128)(2,1)S(1)}, u32[]{:S(2)}, u32[]{:S(2)}) collective-permute-start(bf16[7,128,128]{2,1,0:T(8,128)(2,1)S(1)} %get-tuple-element.105), channel_id=1, source_target_pairs={{0,48},{16,32},{32,16},{48,0},{1,49},{17,33},{33,17},{49,1},{2,50}... | collective-permute-start | bytes 688136 | tf_op jit(solution)/shard_map/ppermute | solution.py:248
  154.4 18.8 %collective-permute-start.12 = (bf16[7,128,128]{2,1,0:T(8,128)(2,1)S(1)}, bf16[7,128,128]{2,1,0:T(8,128)(2,1)S(1)}, u32[]{:S(2)}, u32[]{:S(2)}) collective-permute-start(bf16[7,128,128]{2,1,0:T(8,128)(2,1)S(1)} %get-tuple-element.103), channel_id=1, source_target_pairs={{0,16},{16,0},{32,48},{48,32},{1,17},{17,1},{33,49},{49,33},{2,18}... | collective-permute-start | bytes 688136 | tf_op jit(solution)/shard_map/ppermute | solution.py:248
  154.4 6.5 %collective-permute-start.17 = (bf16[2,128,256]{2,1,0:T(8,128)(2,1)S(1)}, bf16[2,128,256]{2,1,0:T(8,128)(2,1)S(1)}, u32[]{:S(2)}, u32[]{:S(2)}) collective-permute-start(bf16[2,128,256]{2,1,0:T(8,128)(2,1)S(1)} %get-tuple-element.112), channel_id=1, source_target_pairs={{0,8},{4,12},{8,0},{12,4},{1,9},{5,13},{9,1},{13,5},{2,10},{6,14},... | collective-permute-start | bytes 393224 | tf_op jit(solution)/shard_map/ppermute | solution.py:248
  155.4 7.2 %collective-permute-start.18 = (bf16[2,128,256]{2,1,0:T(8,128)(2,1)S(1)}, bf16[2,128,256]{2,1,0:T(8,128)(2,1)S(1)}, u32[]{:S(2)}, u32[]{:S(2)}) collective-permute-start(bf16[2,128,256]{2,1,0:T(8,128)(2,1)S(1)} %get-tuple-element.113), channel_id=1, source_target_pairs={{0,12},{4,8},{8,4},{12,0},{1,13},{5,9},{9,5},{13,1},{2,14},{6,10},... | collective-permute-start | bytes 393224 | tf_op jit(solution)/shard_map/ppermute | solution.py:248
  173.2 1.5 copy-start.5
  174.7 1.5 copy-start.10
  176.2 3.0 %copy-start.6 = (bf16[8,128,896]{2,1,0:T(8,128)(2,1)S(1)}, bf16[8,128,896]{2,1,0:T(8,128)(2,1)}, u32[]{:S(2)}) copy-start(bf16[8,128,896]{2,1,0:T(8,128)(2,1)} %all-gather.7.cloned.1.call-done) | copy-start | bytes 5505028
  176.2 3.0 %copy-start.12 = (bf16[512,1024]{1,0:T(8,128)(2,1)S(1)}, bf16[512,1024]{1,0:T(8,128)(2,1)}, u32[]{:S(2)}) copy-start(bf16[512,1024]{1,0:T(8,128)(2,1)} %copy-done.11) | copy-start | bytes 3145732
  179.1 10.7 %collective-permute-start.19 = (bf16[4,2,128,256]{3,2,1,0:T(8,128)(2,1)S(1)}, bf16[4,2,128,256]{3,2,1,0:T(8,128)(2,1)S(1)}, u32[]{:S(2)}, u32[]{:S(2)}) collective-permute-start(bf16[4,2,128,256]{3,2,1,0:T(8,128)(2,1)S(1)} %get-tuple-element.123), channel_id=1, source_target_pairs={{0,1},{1,0},{2,3},{3,2},{4,5},{5,4},{6,7},{7,6},{8,9},{9,8},{10,11... | collective-permute-start | bytes 1572872 | tf_op jit(solution)/shard_map/ppermute | solution.py:248
  185.3 30.7 %collective-permute-start.26 = (bf16[2,7,128,128]{3,2,1,0:T(8,128)(2,1)S(1)}, bf16[2,7,128,128]{3,2,1,0:T(8,128)(2,1)S(1)}, u32[]{:S(2)}, u32[]{:S(2)}) collective-permute-start(bf16[2,7,128,128]{3,2,1,0:T(8,128)(2,1)S(1)} %get-tuple-element.135), channel_id=1, source_target_pairs={{0,32},{16,48},{32,0},{48,16},{1,33},{17,49},{33,1},{49,17},{2,34}... | collective-permute-start | bytes 1376264 | tf_op jit(solution)/shard_map/ppermute | solution.py:248
  185.4 48.0 %collective-permute-start.27 = (bf16[2,7,128,128]{3,2,1,0:T(8,128)(2,1)S(1)}, bf16[2,7,128,128]{3,2,1,0:T(8,128)(2,1)S(1)}, u32[]{:S(2)}, u32[]{:S(2)}) collective-permute-start(bf16[2,7,128,128]{3,2,1,0:T(8,128)(2,1)S(1)} %get-tuple-element.136), channel_id=1, source_target_pairs={{0,48},{16,32},{32,16},{48,0},{1,49},{17,33},{33,17},{49,1},{2,50}... | collective-permute-start | bytes 1376264 | tf_op jit(solution)/shard_map/ppermute | solution.py:248
  187.2 46.2 %collective-permute-start.25 = (bf16[2,7,128,128]{3,2,1,0:T(8,128)(2,1)S(1)}, bf16[2,7,128,128]{3,2,1,0:T(8,128)(2,1)S(1)}, u32[]{:S(2)}, u32[]{:S(2)}) collective-permute-start(bf16[2,7,128,128]{3,2,1,0:T(8,128)(2,1)S(1)} %get-tuple-element.121), channel_id=1, source_target_pairs={{0,16},{16,0},{32,48},{48,32},{1,17},{17,1},{33,49},{49,33},{2,18}... | collective-permute-start | bytes 1376264 | tf_op jit(solution)/shard_map/ppermute | solution.py:248
  190.4 6.4 %collective-permute-start.20 = (bf16[2,128,256]{2,1,0:T(8,128)(2,1)S(1)}, bf16[2,128,256]{2,1,0:T(8,128)(2,1)S(1)}, u32[]{:S(2)}, u32[]{:S(2)}) collective-permute-start(bf16[2,128,256]{2,1,0:T(8,128)(2,1)S(1)} %get-tuple-element.125), channel_id=1, source_target_pairs={{0,4},{4,0},{8,12},{12,8},{1,5},{5,1},{9,13},{13,9},{2,6},{6,2},{1... | collective-permute-start | bytes 393224 | tf_op jit(solution)/shard_map/ppermute | solution.py:248
  191.8 6.6 %collective-permute-start.21 = (bf16[2,128,256]{2,1,0:T(8,128)(2,1)S(1)}, bf16[2,128,256]{2,1,0:T(8,128)(2,1)S(1)}, u32[]{:S(2)}, u32[]{:S(2)}) collective-permute-start(bf16[2,128,256]{2,1,0:T(8,128)(2,1)S(1)} %get-tuple-element.126), channel_id=1, source_target_pairs={{0,8},{4,12},{8,0},{12,4},{1,9},{5,13},{9,1},{13,5},{2,10},{6,14},... | collective-permute-start | bytes 393224 | tf_op jit(solution)/shard_map/ppermute | solution.py:248
  196.8 5.0 %collective-permute-start.22 = (bf16[2,128,256]{2,1,0:T(8,128)(2,1)S(1)}, bf16[2,128,256]{2,1,0:T(8,128)(2,1)S(1)}, u32[]{:S(2)}, u32[]{:S(2)}) collective-permute-start(bf16[2,128,256]{2,1,0:T(8,128)(2,1)S(1)} %get-tuple-element.127), channel_id=1, source_target_pairs={{0,12},{4,8},{8,4},{12,0},{1,13},{5,9},{9,5},{13,1},{2,14},{6,10},... | collective-permute-start | bytes 393224 | tf_op jit(solution)/shard_map/ppermute | solution.py:248
  202.4 34.6 %collective-permute-start.23 = (bf16[2,128,256]{2,1,0:T(8,128)(2,1)S(1)}, bf16[2,128,256]{2,1,0:T(8,128)(2,1)S(1)}, u32[]{:S(2)}, u32[]{:S(2)}) collective-permute-start(bf16[2,128,256]{2,1,0:T(8,128)(2,1)S(1)} %get-tuple-element.130), channel_id=1, source_target_pairs={{0,0},{2,2},{4,64},{6,66},{8,128},{10,130},{12,192},{14,194},{64,4... | collective-permute-start | bytes 393224 | tf_op jit(solution)/shard_map/ppermute | solution.py:266
  208.4 28.6 %collective-permute-start.24 = (bf16[2,128,256]{2,1,0:T(8,128)(2,1)S(1)}, bf16[2,128,256]{2,1,0:T(8,128)(2,1)S(1)}, u32[]{:S(2)}, u32[]{:S(2)}) collective-permute-start(bf16[2,128,256]{2,1,0:T(8,128)(2,1)S(1)} %get-tuple-element.131), channel_id=1, source_target_pairs={{0,2},{2,0},{4,66},{6,64},{8,130},{10,128},{12,194},{14,192},{64,6... | collective-permute-start | bytes 393224 | tf_op jit(solution)/shard_map/ppermute | solution.py:266
Sparse Core Ops, SparseCore 0:
  125.0 31.1 all-gather.6

commit v3 on v2

v3 whole, which is shorter than its diff:
```python
import jax
import jax.numpy as jnp
from jax import lax
from jax.experimental import pallas as pl
from jax.experimental.pallas import tpu as pltpu
from jax.sharding import Mesh, PartitionSpec as P

B = 128
VM = pl.BlockSpec(memory_space=pltpu.VMEM)
SM = pl.BlockSpec(memory_space=pltpu.SMEM)
BF = jnp.bfloat16
F32 = jnp.float32


def sds(shape, dtype=BF):
    return jax.ShapeDtypeStruct(shape, dtype)


def call(kernel, specs, args, outs, scratch=(), flops=0, mib=24, small=False):
    nbytes = 0 if small else sum(a.size * a.dtype.itemsize for a in list(args) + list(outs))
    return pl.pallas_call(
        kernel,
        out_shape=tuple(outs),
        in_specs=[(VM, SM, pl.BlockSpec(memory_space=pltpu.HBM))[s] for s in specs],
        out_specs=tuple(VM for _ in outs),
        scratch_shapes=list(scratch),
        compiler_params=pltpu.CompilerParams(vmem_limit_bytes=mib and mib * 1024 * 1024),
        cost_estimate=pl.CostEstimate(flops=flops, bytes_accessed=nbytes, transcendentals=0),
    )(*args)


GATE, UP, DOWN = 0, 7, 14


def cells(mask, tile, which):
    slot = jnp.int32(0)
    for cc in range(7):
        for rr in range(2):
            on = mask[which + cc, 2 * tile + rr]
            yield rr, cc, on == 1, jnp.minimum(slot, 6)
            slot = slot + on
    yield None, None, slot, None


def sub(rr, cc, which):
    a, b = (cc, rr) if which == DOWN else (rr, cc)
    return pl.ds(a * B, B), pl.ds(b * B, B)


def pack(mask, tile, which, source, out):
    for rr, cc, on, slot in cells(mask, tile, which):
        if rr is None:
            for p in range(5, 7):

                @pl.when(on <= p)
                def _(p=p):
                    out[p] = jnp.zeros((B, B), out.dtype)

        else:

            @pl.when(on)
            def _(rr=rr, cc=cc, slot=slot):
                out[slot] = source[sub(rr, cc, which)].astype(out.dtype)


def unpack(mask, tile, which, block, store):
    for rr, cc, on, slot in cells(mask, tile, which):
        if rr is not None:
            found = block(slot)
            store(rr, cc, jnp.where(on, found, jnp.zeros_like(found)))


def k_pack(pos, mask, gw, uw, dw, gp, up, dp, gv, uv, dv, sems):
    tile = pos[0] * 4 + pos[1]
    copies = [
        pltpu.make_async_copy(src, dst, sems.at[i])
        for i, (src, dst) in enumerate(((dw, dv), (gw, gv), (uw, uv)))
    ]
    for c in copies:
        c.start()
    copies[0].wait()
    pack(mask, tile, DOWN, dv, dp)
    copies[1].wait()
    pack(mask, tile, GATE, gv, gp)
    copies[2].wait()
    pack(mask, tile, UP, uv, up)


def assemble(pos, mine, other, which, out):
    x, h, k = pos[2], pos[3], pos[4]
    for s in range(4):
        rows = pl.ds(pl.multiple_of(jnp.bitwise_xor(x, s) * B, B), B)
        for a in range(2):
            for b, piece in enumerate((mine, other)):
                q = 2 * jnp.bitwise_xor(h, a) + jnp.bitwise_xor(k, b)
                out[rows, columns(q)] = piece[s, a, which]


def dense_tile_rows(y, mask, which, panel, dense):
    for z in range(4):

        def store(rr, cc, v):
            dense[z * 256 + rr * B : z * 256 + (rr + 1) * B, cc * B : (cc + 1) * B] = v

        unpack(mask, 4 * y + z, which, lambda s: panel[z, s], store)


def shares(y, acc, outs, at=()):
    outs[0][at + (Ellipsis,)] = acc[y]
    for j in (1, 2, 3):
        outs[j][at + (Ellipsis,)] = acc[jnp.bitwise_xor(y, j)].astype(BF)


def k_grad_gate(pos, mask, dp, gp, mine, other, o0, o1, o2, o3, wd, wg, cot, tok, acc):
    y = pos[0]
    for z in range(4):

        def store(rr, cc, v):
            wd[z, cc * B : (cc + 1) * B, rr * B : (rr + 1) * B] = v

        unpack(mask, 4 * y + z, DOWN, lambda s: dp[z, s], store)
    assemble(pos, mine, other, 1, cot)
    got = None
    for q in range(4):
        term = lax.dot_general(
            cot[:, q * 256 : (q + 1) * 256], wd[q], NT, preferred_element_type=F32
        )
        got = term if got is None else got + term
    acc[...] = got.reshape(4, B, 896)
    shares(y, acc, (o0, o1, o2, o3), (0,))
    dense_tile_rows(y, mask, GATE, gp, wg)
    assemble(pos, mine, other, 0, tok)
    got = jnp.dot(tok[...], wg[...], preferred_element_type=F32)
    acc[...] = got.reshape(4, B, 896)
    shares(y, acc, (o0, o1, o2, o3), (1,))


def k_up(pos, mask, panel, tok, o0, o1, o2, o3, dense, acc):
    dense_tile_rows(pos[0], mask, UP, panel, dense)
    got = jnp.dot(tok[...], dense[...], preferred_element_type=F32)
    acc[...] = got.reshape(4, B, 896)
    shares(pos[0], acc, (o0, o1, o2, o3))


def total(own, *others):
    out = own[...]
    for o in others:
        out = out + o[...].astype(F32)
    return out


def k_act(a0, a1, a2, a3, b0, b1, b2, b3, hid, act):
    both = total(a0, a1, a2, a3)
    grad, gate = both[0], both[1]
    up = total(b0, b1, b2, b3)
    sig = jax.nn.sigmoid(gate)
    hid[...] = (gate * sig * up).astype(BF)
    act[0] = (grad * up * sig * (1.0 + gate * (1.0 - sig))).astype(BF)
    act[1] = (grad * (gate * sig)).astype(BF)


def columns(q):
    return pl.ds(pl.multiple_of(q * 256, 256), 256)


TN = (((0,), (0,)), ((), ()))
NT = (((1,), (1,)), ((), ()))


def k_down_grad(pos, mask, hid, cot, d0, d1, d2, d3, acc):
    y, z = pos[0], pos[1]
    left = hid[...].reshape(512, 896)
    for j, out in ((1, d1), (2, d2), (3, d3), (0, d0)):
        zz = jnp.bitwise_xor(z, j)
        acc[...] = lax.dot_general(left, cot[:, columns(zz)], TN, preferred_element_type=F32)
        pack(mask, 4 * y + zz, DOWN, acc, out)


def k_weight_grad(pos, mask, act, tok, d0, d1, d2, d3, acc):
    y, z = pos[0], pos[1]
    for half, which in enumerate((GATE, UP)):
        right = act[half].reshape(512, 896)
        for j, out in ((1, d1), (2, d2), (3, d3), (0, d0)):
            zz = jnp.bitwise_xor(z, j)
            acc[...] = lax.dot_general(tok[:, columns(zz)], right, TN, preferred_element_type=F32)
            pack(mask, 4 * y + zz, which, acc, out.at[half])


def k_out_in(pos, hid, a0, a1, a2, a3, wd, wg, wu, act, keep, send):
    y, k = pos[0], pos[4]
    for j, a in enumerate((a0, a1, a2, a3)):
        for half in range(2):
            act[half, jnp.bitwise_xor(y, j)] = a[half]
    left = hid[...].reshape(512, 896)
    gact, uact = act[0].reshape(512, 896), act[1].reshape(512, 896)
    for out, kk in ((send, 1 - k), (keep, k)):
        for h in range(2):
            q = 2 * h + kk
            got = jnp.dot(left, wd[q], preferred_element_type=F32)
            out[:, 0, h] = got.reshape(4, B, 256).astype(out.dtype)
            rows = columns(q)
            got = lax.dot_general(gact, wg[rows, :], NT, preferred_element_type=F32)
            got = got + lax.dot_general(uact, wu[rows, :], NT, preferred_element_type=F32)
            out[:, 1, h] = got.reshape(4, B, 256).astype(out.dtype)


def k_sum_core(pos, keep, got, o0, o1, o2, o3):
    x = pos[2]
    for j, out in enumerate((o0, o1, o2, o3)):
        at = jnp.bitwise_xor(x, j)
        out[...] = (keep[at] + got[at].astype(F32)).astype(out.dtype)


def k_sum_x(pos, a0, a1, a2, a3, keep, send, acc):
    h = pos[3]
    acc[...] = total(a0, a1, a2, a3)
    for i in range(2):
        keep[i] = acc[i, h].astype(BF)
        send[i] = acc[i, 1 - h].astype(BF)


def k_sum_pair(a, b, out, grad):
    both = a[...].astype(F32) + b[...].astype(F32)
    out[...] = both[0].astype(BF)
    grad[...] = both[1].astype(BF)


def place(pos, mask, parts, which, at, out):
    a0, a1, a2, a3 = parts

    def block(s):
        i = at + (s,)
        return total(a0.at[i], a1.at[i], a2.at[i], a3.at[i])

    def store(rr, cc, v):
        out[sub(rr, cc, which)] = v.astype(BF)

    unpack(mask, pos[0] * 4 + pos[1], which, block, store)


def k_place_down(pos, mask, a0, a1, a2, a3, out):
    place(pos, mask, (a0, a1, a2, a3), DOWN, (), out)


def k_place_both(pos, mask, a0, a1, a2, a3, gate, up):
    place(pos, mask, (a0, a1, a2, a3), GATE, (0,), gate)
    place(pos, mask, (a0, a1, a2, a3), UP, (1,), up)


def exchange(value, axis, by, size=4):
    return lax.ppermute(value, axis, [(i, i ^ by) for i in range(size)])


def spread(value, axis):
    return [value] + [exchange(value, axis, j) for j in (1, 2, 3)]


def collect(own, others, axis):
    return [own] + [exchange(v, axis, j) for j, v in zip((1, 2, 3), others)]


def swap(value, flip):
    pairs = [
        ((y * 4 + x) * 2 + h, (x * 4 + y) * 2 + (h ^ flip))
        for y in range(4)
        for x in range(4)
        for h in range(2)
    ]
    return lax.ppermute(value, ("y", "x", "h"), pairs)


def body(tokens, cotangent, gate_weight, up_weight, down_weight, gate_mask, up_mask, down_mask):
    pos = jnp.stack([lax.axis_index(a) for a in ("y", "z", "x", "h", "k")]).astype(jnp.int32)
    mask = jnp.concatenate([gate_mask.T, up_mask.T, down_mask])
    both = jnp.stack([tokens, cotangent])
    pair = jnp.stack([swap(both, 0), swap(both, 1)])
    packed = sds((7, B, B))
    gp, up, dp = call(
        k_pack, (1, 1, 2, 2, 2),
        (pos, mask, gate_weight, up_weight, down_weight), (packed,) * 3,
        (pltpu.VMEM((256, 896), BF), pltpu.VMEM((256, 896), BF), pltpu.VMEM((896, 256), BF),
         pltpu.SemaphoreType.DMA((3,))),
        mib=None,
    )
    dp, pair = lax.optimization_barrier((dp, pair))
    mine = spread(pair, "x")
    dp = lax.all_gather(dp, "z", axis=0)
    gp, dp, mine = lax.optimization_barrier((gp, dp, mine))
    mine = jnp.stack(mine)
    other = exchange(mine, "k", 1, 2)
    gp = lax.all_gather(gp, "z", axis=0)
    acc = pltpu.VMEM((4, B, 896), F32)
    flops = 2 * 512 * 1024 * 896
    blk = (2, B, 896)
    g = call(
        k_grad_gate, (1, 1, 0, 0, 0, 0), (pos, mask, dp, gp, mine, other),
        (sds(blk, F32), sds(blk), sds(blk), sds(blk),
         sds((4, 896, 256)), sds((1024, 896)), sds((512, 1024)), sds((512, 1024))),
        (acc,), flops=2 * flops,
    )
    wd, wg, cot, tok = g[4:]
    g_all = collect(g[0], g[1:4], "y")
    up, _ = lax.optimization_barrier((up, g[1]))
    up = lax.all_gather(up, "z", axis=0)
    up, g_all = lax.optimization_barrier((up, g_all))
    blk = (B, 896)
    u = call(
        k_up, (1, 1, 0, 0), (pos, mask, up, tok),
        (sds(blk, F32), sds(blk), sds(blk), sds(blk), sds((1024, 896))), (acc,), flops=flops,
    )
    wu = u[4]
    u_all = collect(u[0], u[1:4], "y")
    hidden, act = call(k_act, (0,) * 8, (*g_all, *u_all), (sds(blk), sds((2, B, 896))))
    hidden = lax.all_gather(hidden, "y", axis=0)
    hidden, act = lax.optimization_barrier((hidden, act))
    act_all = spread(act, "y")
    blk = (7, B, B)
    e = call(
        k_down_grad, (1, 1, 0, 0), (pos, mask, hidden, cot),
        (sds(blk, F32), sds(blk), sds(blk), sds(blk)),
        (pltpu.VMEM((896, 256), F32),), small=True,
    )
    e_all = collect(e[0], e[1:4], "z")
    act_all, e_all = lax.optimization_barrier((act_all, e_all))
    half, part = (4, 2, 2, B, 256), (2, 2, B, 256)
    act, keep, send = call(
        k_out_in, (1,) + (0,) * 8, (pos, hidden, *act_all, wd, wg, wu),
        (sds((2, 4, B, 896)), sds(half, F32), sds(half)), flops=3 * flops,
    )
    got = exchange(send, "k", 1, 2)
    act, keep = lax.optimization_barrier((act, keep))
    blk = (2, 7, B, B)
    f = call(
        k_weight_grad, (1, 1, 0, 0), (pos, mask, act, tok),
        (sds(blk, F32), sds(blk), sds(blk), sds(blk)),
        (pltpu.VMEM((256, 896), F32),), flops=2 * flops,
    )
    f_all = collect(f[0], f[1:4], "z")
    keep, _ = lax.optimization_barrier((keep, f[1]))
    s = call(
        k_sum_core, (1, 0, 0), (pos, keep, got),
        (sds(part, F32), sds(part), sds(part), sds(part)),
    )
    own, other = call(
        k_sum_x, (1, 0, 0, 0, 0), (pos, *collect(s[0], s[1:], "x")),
        (sds((2, B, 256)), sds((2, B, 256))), (pltpu.VMEM(part, F32),),
    )
    output, input_grad = call(
        k_sum_pair, (0, 0), (swap(own, 0), swap(other, 1)), (sds((B, 256)),) * 2
    )

    spec = (1, 1, 0, 0, 0, 0)
    (down_grad,) = call(k_place_down, spec, (pos, mask, *e_all), (sds((896, 256)),))
    gate_grad, up_grad = call(
        k_place_both, spec, (pos, mask, *f_all), (sds((256, 896)), sds((256, 896)))
    )
    return (output, input_grad, gate_grad, up_grad, down_grad)


def solution(mesh):
    mesh = Mesh(mesh.devices.reshape(4, 4, 4, 2, 2), ("y", "z", "x", "h", "k"))
    row, col = ("y", "z"), ("x", "h", "k")
    return jax.shard_map(
        body,
        mesh=mesh,
        in_specs=(
            P(row, col),
            P(row, col),
            P(row, col),
            P(row, col),
            P(col, row),
            P(None, col),
            P(None, col),
            P(col, None),
        ),
        out_specs=(P(row, col), P(row, col), P(row, col), P(row, col), P(col, row)),
        check_vma=False,
    )
```

time: 245 us -> 220 us (0.90)
  between operations: 14.3 us -> 0.85 us
  local copies, waits for them, and re-layouts: 13.1 us -> 0.65 us
  Pallas kernels: 32.9 us -> 29.5 us
    unnamed x32 -> x8, local copies, waits for them, and re-layouts: 13.1 us -> 0.02 us
    pallas_call x16 -> x12, Pallas kernels: 32.9 us -> 29.5 us  [call(): pl.pallas_call(kernel, out_shape=tuple(outs), in_specs=[(VM, SM, pl.Block...]
    ppermute x24 -> x23, starting transfers between devices: 30 us -> 32.4 us  [exchange(): return lax.ppermute(value, axis, [(i, i ^ by) for i in range(size)])]
    ppermute x24 -> x23, waiting for transfers between devices: 57.9 us -> 57 us  [exchange(): return lax.ppermute(value, axis, [(i, i ^ by) for i in range(size)])]
  transfers between devices with their start and end apart: 29 -> 27, of which waited for: 14 -> 11; matrix products, arithmetic and copies ran while one was open for 1% -> 1% of each run, Pallas kernels for 9% -> 6%
where the time goes in v3:
time: 220 us; the launch traced here: 219 us
  blocking collectives  74.7 us (34%)
  waiting for transfers between devices  59.2 us (27%)
  starting transfers between devices  52.1 us (24%)
  Pallas kernels  29.5 us (13%)
  other arithmetic  2.37 us (1%)
    ppermute x23, waiting for transfers between devices, exchange(): return lax.ppermute(value, axis, [(i, i ^ by) for i in range(size)])  57 us
    ppermute x23, starting transfers between devices, exchange(): return lax.ppermute(value, axis, [(i, i ^ by) for i in range(size)])  32.4 us
    pallas_call x12, Pallas kernels, call(): pl.pallas_call(kernel, out_shape=tuple(outs), in_specs=[(VM, SM, pl.Block...  29.5 us
    all_gather x1, blocking collectives, body(): dp = lax.all_gather(dp, 'z', axis=0)  21 us
    all_gather x1, blocking collectives, body(): gp = lax.all_gather(gp, 'z', axis=0)  20.3 us
    ppermute x4, starting transfers between devices, swap(): return lax.ppermute(value, ('y', 'x', 'h'), pairs)  19.7 us
    all_gather x1, blocking collectives, body(): up = lax.all_gather(up, 'z', axis=0)  19 us
    all_gather x1, blocking collectives, body(): hidden = lax.all_gather(hidden, 'y', axis=0)  14.5 us
  transfers between devices with their start and end apart: 27, of which 11 were waited for; matrix products, arithmetic and copies ran while one was open for 1% of the time, Pallas kernels for 6%

profile of v3, /device:TPU:34, one launch (start us, length us, event | category | flops | bytes accessed | tf_op | source)
XLA Modules:
  0.0 219.3 jit_solution(16497978877719804177)
XLA Ops:
  0.6 0.9 pad_maximum_fusion.2
  1.5 7.4 %collective-permute-start.1 = (bf16[2,128,256]{2,1,0:T(8,128)(2,1)S(1)}, bf16[2,128,256]{2,1,0:T(8,128)(2,1)S(1)}, u32[]{:S(2)}, u32[]{:S(2)}) collective-permute-start(bf16[2,128,256]{2,1,0:T(8,128)(2,1)S(1)} %pad_maximum_fusion.2), channel_id=1, source_target_pairs={{0,2},{2,0},{4,66},{6,64},{8,130},{10,128},{12,194},{14,192},{64,6... | collective-permute-start | bytes 393224 | tf_op jit(solution)/shard_map/ppermute | solution.py:269
  8.9 3.3 %collective-permute-start = (bf16[2,128,256]{2,1,0:T(8,128)(2,1)S(1)}, bf16[2,128,256]{2,1,0:T(8,128)(2,1)S(1)}, u32[]{:S(2)}, u32[]{:S(2)}) collective-permute-start(bf16[2,128,256]{2,1,0:T(8,128)(2,1)S(1)} %pad_maximum_fusion.2), channel_id=1, source_target_pairs={{0,0},{2,2},{4,64},{6,66},{8,128},{10,130},{12,192},{14,194},{64,4... | collective-permute-start | bytes 393224 | tf_op jit(solution)/shard_map/ppermute | solution.py:269
  12.2 0.6 stack.56.pos
  12.8 1.3 pad_add_fusion.mask
  14.1 3.2 %shard_map.119 = (bf16[7,128,128]{2,1,0:T(8,128)(2,1)}, bf16[7,128,128]{2,1,0:T(8,128)(2,1)}, bf16[7,128,128]{2,1,0:T(8,128)(2,1)}) custom-call(s32[5]{0:T(128)} %stack.56.pos, s32[21,32]{1,0:T(8,128)} %pad_add_fusion.mask, bf16[256,896]{1,0:T(8,128)(2,1)} %gw.1, bf16[256,896]{1,0:T(8,128)(2,1)} %uw.1, bf16[896,256]{1,0:T(8,128)(2,1)} %dw.1), custom_call_target="tpu_custom_call" | custom-call | bytes 2067092 | tf_op jit(solution)/shard_map/pallas_call | solution.py:21
  17.3 2.2 collective-permute-done
  19.6 6.9 %collective-permute-start.3 = (bf16[2,2,128,256]{3,2,1,0:T(8,128)(2,1)S(1)}, bf16[2,2,128,256]{3,2,1,0:T(8,128)(2,1)S(1)}, u32[]{:S(2)}, u32[]{:S(2)}) collective-permute-start(bf16[2,2,128,256]{3,2,1,0:T(8,128)(2,1)S(1)} %pad_maximum_fusion.1), channel_id=1, source_target_pairs={{0,8},{4,12},{8,0},{12,4},{1,9},{5,13},{9,1},{13,5},{2,10},{6,14},... | collective-permute-start | bytes 786440 | tf_op jit(solution)/shard_map/ppermute | solution.py:251
  26.5 21.0 %all-gather = bf16[28,128,128]{2,1,0:T(8,128)(2,1)S(1)} all-gather(bf16[7,128,128]{2,1,0:T(8,128)(2,1)} %get-tuple-element.74), channel_id=2, replica_groups=mesh['y'=4,'z'=4,'x'=4,'h'=2,'k'=2] {'z'}, dimensions={0}, use_global_device_ids=true | all-gather | bytes 1146880 | tf_op jit(solution)/shard_map/all_gather | solution.py:287
  47.7 20.3 %all-gather.1 = bf16[28,128,128]{2,1,0:T(8,128)(2,1)S(1)} all-gather(bf16[7,128,128]{2,1,0:T(8,128)(2,1)S(1)} %copy-done.3), channel_id=3, replica_groups=mesh['y'=4,'z'=4,'x'=4,'h'=2,'k'=2] {'z'}, dimensions={0}, use_global_device_ids=true | all-gather | bytes 1146880 | tf_op jit(solution)/shard_map/all_gather | solution.py:291
  68.0 3.8 %shard_map.120 = (f32[2,128,896]{2,1,0:T(8,128)S(1)}, bf16[2,128,896]{2,1,0:T(8,128)(2,1)S(1)}, bf16[2,128,896]{2,1,0:T(8,128)(2,1)S(1)}, bf16[2,128,896]{2,1,0:...) custom-call(s32[5]{0:T(128)S(1)} %copy-done.1, ...), custom_call_target="tpu_custom_call" | custom-call | flops 1879048192 | bytes 11995796 | tf_op jit(solution)/shard_map/pallas_call | solution.py:21
  72.0 2.8 %collective-permute-start.7 = (bf16[2,128,896]{2,1,0:T(8,128)(2,1)S(1)}, bf16[2,128,896]{2,1,0:T(8,128)(2,1)S(1)}, u32[]{:S(2)}, u32[]{:S(2)}) collective-permute-start(bf16[2,128,896]{2,1,0:T(8,128)(2,1)S(1)} %get-tuple-element.85), channel_id=1, source_target_pairs={{0,128},{64,192},{128,0},{192,64},{1,129},{65,193},{129,1},{193,65... | collective-permute-start | bytes 1376264 | tf_op jit(solution)/shard_map/ppermute | solution.py:251
  74.9 1.8 collective-permute-start.8
  76.6 19.0 %all-gather.2 = bf16[28,128,128]{2,1,0:T(8,128)(2,1)S(1)} all-gather(bf16[7,128,128]{2,1,0:T(8,128)(2,1)S(1)} %copy-done.2), channel_id=4, replica_groups=mesh['y'=4,'z'=4,'x'=4,'h'=2,'k'=2] {'z'}, dimensions={0}, use_global_device_ids=true | all-gather | bytes 1146880 | tf_op jit(solution)/shard_map/all_gather | solution.py:304
  95.6 1.3 collective-permute-done.8.a3
  96.9 2.3 %shard_map.121 = (f32[128,896]{1,0:T(8,128)S(1)}, bf16[128,896]{1,0:T(8,128)(2,1)S(1)}, bf16[128,896]{1,0:T(8,128)(2,1)S(1)}, bf16[128,896]{1,0:T(8,128)(2,1)S(1)}, bf16[1024,896]{1,0:T(8,128)(2,1)S(1)}) custom-call(s32[5]{0:T(128)S(1)} %copy-done.1, s32[21,32]{1,0:T(8,128)S(1)} %copy-done, bf16[4,7,128,128]{3,2,1,0:T(8,128)(2,1)S(1)} %bitcast.22, ...), custom_call_target="tpu_custom_call" | custom-call | flops 939524096 | bytes 4950676 | tf_op jit(solution)/shard_map/pallas_call | solution.py:21
  99.3 1.8 collective-permute-start.11
  101.1 1.7 collective-permute-start.9
  102.8 5.7 %collective-permute-done.10.b2 = bf16[128,896]{1,0:T(8,128)(2,1)S(1)} collective-permute-done((bf16[128,896]{1,0:T(8,128)(2,1)S(1)}, bf16[128,896]{1,0:T(8,128)(2,1)S(1)}, u32[]{:S(2)}, u32[]{:S(2)}) %collective-permute-start.10) | collective-permute-done | bytes 229408 | tf_op jit(solution)/shard_map/ppermute | solution.py:251
  108.5 2.2 collective-permute-done.11.b3
  110.7 0.5 shard_map.122
  111.2 14.5 %all-gather.3 = bf16[512,896]{1,0:T(8,128)(2,1)S(1)} all-gather(bf16[128,896]{1,0:T(8,128)(2,1)S(1)} %get-tuple-element.97), channel_id=5, replica_groups=mesh['y'=4,'z'=4,'x'=4,'h'=2,'k'=2] {'y'}, dimensions={0}, use_global_device_ids=true | all-gather | bytes 1146880 | tf_op jit(solution)/shard_map/all_gather | solution.py:314
  125.7 3.8 %shard_map.123 = (f32[7,128,128]{2,1,0:T(8,128)S(1)}, bf16[7,128,128]{2,1,0:T(8,128)(2,1)S(1)}, bf16[7,128,128]{2,1,0:T(8,128)(2,1)S(1)}, bf16[7,128,128]{2,1,0:T(8,128)(2,1)S(1)}) custom-call(s32[5]{0:T(128)S(1)} %copy-done.1, s32[21,32]{1,0:T(8,128)S(1)} %copy-done, bf16[4,128,896]{2,1,0:T(8,128)(2,1)S(1)} %bitcast.19, ...), custom_call_target="tpu_custom_call" | custom-call | tf_op jit(solution)/shard_map/pallas_call | solution.py:21
  129.5 2.5 %collective-permute-start.15 = (bf16[7,128,128]{2,1,0:T(8,128)(2,1)S(1)}, bf16[7,128,128]{2,1,0:T(8,128)(2,1)S(1)}, u32[]{:S(2)}, u32[]{:S(2)}) collective-permute-start(bf16[7,128,128]{2,1,0:T(8,128)(2,1)S(1)} %get-tuple-element.103), channel_id=1, source_target_pairs={{0,16},{16,0},{32,48},{48,32},{1,17},{17,1},{33,49},{49,33},{2,18}... | collective-permute-start | bytes 688136 | tf_op jit(solution)/shard_map/ppermute | solution.py:251
  132.0 2.5 %collective-permute-start.13 = (bf16[2,128,896]{2,1,0:T(8,128)(2,1)S(1)}, bf16[2,128,896]{2,1,0:T(8,128)(2,1)S(1)}, u32[]{:S(2)}, u32[]{:S(2)}) collective-permute-start(bf16[2,128,896]{2,1,0:T(8,128)(2,1)S(1)} %get-tuple-element.106.a0), channel_id=1, source_target_pairs={{0,128},{64,192},{128,0},{192,64},{1,129},{65,193},{129,1},{193,65... | collective-permute-start | bytes 1376264 | tf_op jit(solution)/shard_map/ppermute | solution.py:251
  134.5 2.2 %collective-permute-start.14 = (bf16[2,128,896]{2,1,0:T(8,128)(2,1)S(1)}, bf16[2,128,896]{2,1,0:T(8,128)(2,1)S(1)}, u32[]{:S(2)}, u32[]{:S(2)}) collective-permute-start(bf16[2,128,896]{2,1,0:T(8,128)(2,1)S(1)} %get-tuple-element.106.a0), channel_id=1, source_target_pairs={{0,192},{64,128},{128,64},{192,0},{1,193},{65,129},{129,65},{193,1... | collective-permute-start | bytes 1376264 | tf_op jit(solution)/shard_map/ppermute | solution.py:251
  136.7 1.2 collective-permute-start.16
  137.8 1.7 collective-permute-start.17
  139.5 10.3 %collective-permute-done.16.a2 = bf16[7,128,128]{2,1,0:T(8,128)(2,1)S(1)} collective-permute-done((bf16[7,128,128]{2,1,0:T(8,128)(2,1)S(1)}, bf16[7,128,128]{2,1,0:T(8,128)(2,1)S(1)}, u32[]{:S(2)}, u32[]{:S(2)}) %collective-permute-start.16) | collective-permute-done | bytes 229408 | tf_op jit(solution)/shard_map/ppermute | solution.py:251
  149.8 4.6 %collective-permute-done.17.a3 = bf16[7,128,128]{2,1,0:T(8,128)(2,1)S(1)} collective-permute-done((bf16[7,128,128]{2,1,0:T(8,128)(2,1)S(1)}, bf16[7,128,128]{2,1,0:T(8,128)(2,1)S(1)}, u32[]{:S(2)}, u32[]{:S(2)}) %collective-permute-start.17) | collective-permute-done | bytes 229408 | tf_op jit(solution)/shard_map/ppermute | solution.py:251
  154.4 4.0 %shard_map.124 = (bf16[2,4,128,896]{3,2,1,0:T(8,128)(2,1)S(1)}, f32[4,2,2,128,256]{4,3,2,1,0:T(8,128)S(1)}, bf16[4,2,2,128,256]{4,3,2,1,0:T(8,128)(2,1)S(1)}) custom-call(s32[5]{0:T(128)S(1)} %copy-done.1, bf16[4,128,896]{2,1,0:T(8,128)(2,1)S(1)} %bitcast.20, bf16[2,128,896]{2,1,0:T(8,128)(2,1)S(1)} %get-tuple-element.106.a0, ...), custom_call_target="tpu_custom_call" | custom-call | flops 2818572288 | bytes 13238292 | tf_op jit(solution)/shard_map/pallas_call | solution.py:21
  158.6 5.9 %shard_map.125 = (f32[2,7,128,128]{3,2,1,0:T(8,128)S(1)}, bf16[2,7,128,128]{3,2,1,0:T(8,128)(2,1)S(1)}, bf16[2,7,128,128]{3,2,1,0:T(8,128)(2,1)S(1)}, bf16[2,7,128,128]{3,2,1,0:T(8,128)(2,1)S(1)}) custom-call(s32[5]{0:T(128)S(1)} %copy-done.1, s32[21,32]{1,0:T(8,128)S(1)} %copy-done, bf16[2,4,128,896]{3,2,1,0:T(8,128)(2,1)S(1)} %get-tuple-element.116.act, ...), custom_call_target="tpu_custom_call" | custom-call | flops 1879048192 | bytes 5180052 | tf_op jit(solution)/shard_map/pallas_call | solution.py:21
  164.5 0.8 shard_map.126
  165.2 2.3 %collective-permute-start.19 = (bf16[2,2,128,256]{3,2,1,0:T(8,128)(2,1)S(1)}, bf16[2,2,128,256]{3,2,1,0:T(8,128)(2,1)S(1)}, u32[]{:S(2)}, u32[]{:S(2)}) collective-permute-start(bf16[2,2,128,256]{3,2,1,0:T(8,128)(2,1)S(1)} %get-tuple-element.121), channel_id=1, source_target_pairs={{0,4},{4,0},{8,12},{12,8},{1,5},{5,1},{9,13},{13,9},{2,6},{6,2},{1... | collective-permute-start | bytes 786440 | tf_op jit(solution)/shard_map/ppermute | solution.py:251
  167.6 3.1 %collective-permute-start.25 = (bf16[2,7,128,128]{3,2,1,0:T(8,128)(2,1)S(1)}, bf16[2,7,128,128]{3,2,1,0:T(8,128)(2,1)S(1)}, u32[]{:S(2)}, u32[]{:S(2)}) collective-permute-start(bf16[2,7,128,128]{3,2,1,0:T(8,128)(2,1)S(1)} %get-tuple-element.129), channel_id=1, source_target_pairs={{0,32},{16,48},{32,0},{48,16},{1,33},{17,49},{33,1},{49,17},{2,34}... | collective-permute-start | bytes 1376264 | tf_op jit(solution)/shard_map/ppermute | solution.py:251
  170.7 0.4 collective-permute-start.26
  171.4 3.4 %collective-permute-done.19.a1 = bf16[2,2,128,256]{3,2,1,0:T(8,128)(2,1)S(1)} collective-permute-done((bf16[2,2,128,256]{3,2,1,0:T(8,128)(2,1)S(1)}, bf16[2,2,128,256]{3,2,1,0:T(8,128)(2,1)S(1)}, u32[]{:S(2)}, u32[]{:S(2)}) %collective-permute-start.19) | collective-permute-done | bytes 262176 | tf_op jit(solution)/shard_map/ppermute | solution.py:251
  174.7 0.7 collective-permute-start.21
  175.4 5.0 %collective-permute-done.20.a2 = bf16[2,2,128,256]{3,2,1,0:T(8,128)(2,1)S(1)} collective-permute-done((bf16[2,2,128,256]{3,2,1,0:T(8,128)(2,1)S(1)}, bf16[2,2,128,256]{3,2,1,0:T(8,128)(2,1)S(1)}, u32[]{:S(2)}, u32[]{:S(2)}) %collective-permute-start.20) | collective-permute-done | bytes 262176 | tf_op jit(solution)/shard_map/ppermute | solution.py:251
  180.5 5.5 %collective-permute-done.21.a3 = bf16[2,2,128,256]{3,2,1,0:T(8,128)(2,1)S(1)} collective-permute-done((bf16[2,2,128,256]{3,2,1,0:T(8,128)(2,1)S(1)}, bf16[2,2,128,256]{3,2,1,0:T(8,128)(2,1)S(1)}, u32[]{:S(2)}, u32[]{:S(2)}) %collective-permute-start.21) | collective-permute-done | bytes 262176 | tf_op jit(solution)/shard_map/ppermute | solution.py:251
  186.0 0.7 shard_map.127
  186.7 2.9 %collective-permute-start.22 = (bf16[2,128,256]{2,1,0:T(8,128)(2,1)S(1)}, bf16[2,128,256]{2,1,0:T(8,128)(2,1)S(1)}, u32[]{:S(2)}, u32[]{:S(2)}) collective-permute-start(bf16[2,128,256]{2,1,0:T(8,128)(2,1)S(1)} %get-tuple-element.124), channel_id=1, source_target_pairs={{0,0},{2,2},{4,64},{6,66},{8,128},{10,130},{12,192},{14,194},{64,4... | collective-permute-start | bytes 393224 | tf_op jit(solution)/shard_map/ppermute | solution.py:269
  189.6 6.2 %collective-permute-start.23 = (bf16[2,128,256]{2,1,0:T(8,128)(2,1)S(1)}, bf16[2,128,256]{2,1,0:T(8,128)(2,1)S(1)}, u32[]{:S(2)}, u32[]{:S(2)}) collective-permute-start(bf16[2,128,256]{2,1,0:T(8,128)(2,1)S(1)} %get-tuple-element.125), channel_id=1, source_target_pairs={{0,2},{2,0},{4,66},{6,64},{8,130},{10,128},{12,194},{14,192},{64,6... | collective-permute-start | bytes 393224 | tf_op jit(solution)/shard_map/ppermute | solution.py:269
  195.8 1.8 shard_map.130
  197.6 6.6 %collective-permute-done.25.a2 = bf16[2,7,128,128]{3,2,1,0:T(8,128)(2,1)S(1)} collective-permute-done((bf16[2,7,128,128]{3,2,1,0:T(8,128)(2,1)S(1)}, bf16[2,7,128,128]{3,2,1,0:T(8,128)(2,1)S(1)}, u32[]{:S(2)}, u32[]{:S(2)}) %collective-permute-start.25) | collective-permute-done | bytes 458784 | tf_op jit(solution)/shard_map/ppermute | solution.py:251
  204.2 12.4 %collective-permute-done.26.a3 = bf16[2,7,128,128]{3,2,1,0:T(8,128)(2,1)S(1)} collective-permute-done((bf16[2,7,128,128]{3,2,1,0:T(8,128)(2,1)S(1)}, bf16[2,7,128,128]{3,2,1,0:T(8,128)(2,1)S(1)}, u32[]{:S(2)}, u32[]{:S(2)}) %collective-permute-start.26) | collective-permute-done | bytes 458784 | tf_op jit(solution)/shard_map/ppermute | solution.py:251
  216.6 2.1 shard_map.129
  218.6 0.7 shard_map.128
  (35 shorter events, 1.1 us)
Async XLA Ops:
  1.5 15.8 %collective-permute-start.1 = (bf16[2,128,256]{2,1,0:T(8,128)(2,1)S(1)}, bf16[2,128,256]{2,1,0:T(8,128)(2,1)S(1)}, u32[]{:S(2)}, u32[]{:S(2)}) collective-permute-start(bf16[2,128,256]{2,1,0:T(8,128)(2,1)S(1)} %pad_maximum_fusion.2), channel_id=1, source_target_pairs={{0,2},{2,0},{4,66},{6,64},{8,130},{10,128},{12,194},{14,192},{64,6... | collective-permute-start | bytes 393224 | tf_op jit(solution)/shard_map/ppermute | solution.py:269
  8.9 10.6 %collective-permute-start = (bf16[2,128,256]{2,1,0:T(8,128)(2,1)S(1)}, bf16[2,128,256]{2,1,0:T(8,128)(2,1)S(1)}, u32[]{:S(2)}, u32[]{:S(2)}) collective-permute-start(bf16[2,128,256]{2,1,0:T(8,128)(2,1)S(1)} %pad_maximum_fusion.2), channel_id=1, source_target_pairs={{0,0},{2,2},{4,64},{6,66},{8,128},{10,130},{12,192},{14,194},{64,4... | collective-permute-start | bytes 393224 | tf_op jit(solution)/shard_map/ppermute | solution.py:269
  19.5 28.2 %copy-start.3 = (bf16[7,128,128]{2,1,0:T(8,128)(2,1)S(1)}, bf16[7,128,128]{2,1,0:T(8,128)(2,1)}, u32[]{:S(2)}) copy-start(bf16[7,128,128]{2,1,0:T(8,128)(2,1)} %get-tuple-element.77) | copy-start | bytes 688132
  19.5 27.9 %collective-permute-start.2 = (bf16[2,2,128,256]{3,2,1,0:T(8,128)(2,1)S(1)}, bf16[2,2,128,256]{3,2,1,0:T(8,128)(2,1)S(1)}, u32[]{:S(2)}, u32[]{:S(2)}) collective-permute-start(bf16[2,2,128,256]{3,2,1,0:T(8,128)(2,1)S(1)} %pad_maximum_fusion.1), channel_id=1, source_target_pairs={{0,4},{4,0},{8,12},{12,8},{1,5},{5,1},{9,13},{13,9},{2,6},{6,2},{1... | collective-permute-start | bytes 786440 | tf_op jit(solution)/shard_map/ppermute | solution.py:251
  19.6 27.8 %collective-permute-start.3 = (bf16[2,2,128,256]{3,2,1,0:T(8,128)(2,1)S(1)}, bf16[2,2,128,256]{3,2,1,0:T(8,128)(2,1)S(1)}, u32[]{:S(2)}, u32[]{:S(2)}) collective-permute-start(bf16[2,2,128,256]{3,2,1,0:T(8,128)(2,1)S(1)} %pad_maximum_fusion.1), channel_id=1, source_target_pairs={{0,8},{4,12},{8,0},{12,4},{1,9},{5,13},{9,1},{13,5},{2,10},{6,14},... | collective-permute-start | bytes 786440 | tf_op jit(solution)/shard_map/ppermute | solution.py:251
  26.5 21.0 %collective-permute-start.4 = (bf16[2,2,128,256]{3,2,1,0:T(8,128)(2,1)S(1)}, bf16[2,2,128,256]{3,2,1,0:T(8,128)(2,1)S(1)}, u32[]{:S(2)}, u32[]{:S(2)}) collective-permute-start(bf16[2,2,128,256]{3,2,1,0:T(8,128)(2,1)S(1)} %pad_maximum_fusion.1), channel_id=1, source_target_pairs={{0,12},{4,8},{8,4},{12,0},{1,13},{5,9},{9,5},{13,1},{2,14},{6,10},... | collective-permute-start | bytes 786440 | tf_op jit(solution)/shard_map/ppermute | solution.py:251
  47.5 20.5 %copy-start = (s32[21,32]{1,0:T(8,128)S(1)}, s32[21,32]{1,0:T(8,128)}, u32[]{:S(2)}) copy-start(s32[21,32]{1,0:T(8,128)} %pad_add_fusion.mask) | copy-start | bytes 8068
  47.5 20.5 %copy-start.1 = (s32[5]{0:T(128)S(1)}, s32[5]{0:T(128)}, u32[]{:S(2)}) copy-start(s32[5]{0:T(128)} %stack.56.pos) | copy-start | bytes 64
  47.6 20.4 %collective-permute-start.5 = (bf16[4,2,2,128,256]{4,3,2,1,0:T(8,128)(2,1)S(1)}, bf16[4,2,2,128,256]{4,3,2,1,0:T(8,128)(2,1)S(1)}, u32[]{:S(2)}, u32[]{:S(2)}) collective-permute-start(bf16[4,2,2,128,256]{4,3,2,1,0:T(8,128)(2,1)S(1)} %pad_maximum_fusion.mine), channel_id=1, source_target_pairs={{0,1},{1,0},{2,3},{3,2},{4,5},{5,4},{6,7},{7,6},{8,9},{9,8},{10,11... | collective-permute-start | bytes 3145736 | tf_op jit(solution)/shard_map/ppermute | solution.py:251
  68.0 8.6 %copy-start.2 = (bf16[7,128,128]{2,1,0:T(8,128)(2,1)S(1)}, bf16[7,128,128]{2,1,0:T(8,128)(2,1)}, u32[]{:S(2)}) copy-start(bf16[7,128,128]{2,1,0:T(8,128)(2,1)} %get-tuple-element.83) | copy-start | bytes 688132
  71.9 23.8 %collective-permute-start.6 = (bf16[2,128,896]{2,1,0:T(8,128)(2,1)S(1)}, bf16[2,128,896]{2,1,0:T(8,128)(2,1)S(1)}, u32[]{:S(2)}, u32[]{:S(2)}) collective-permute-start(bf16[2,128,896]{2,1,0:T(8,128)(2,1)S(1)} %get-tuple-element.82), channel_id=1, source_target_pairs={{0,64},{64,0},{128,192},{192,128},{1,65},{65,1},{129,193},{193,129... | collective-permute-start | bytes 1376264 | tf_op jit(solution)/shard_map/ppermute | solution.py:251
  72.0 23.6 %collective-permute-start.7 = (bf16[2,128,896]{2,1,0:T(8,128)(2,1)S(1)}, bf16[2,128,896]{2,1,0:T(8,128)(2,1)S(1)}, u32[]{:S(2)}, u32[]{:S(2)}) collective-permute-start(bf16[2,128,896]{2,1,0:T(8,128)(2,1)S(1)} %get-tuple-element.85), channel_id=1, source_target_pairs={{0,128},{64,192},{128,0},{192,64},{1,129},{65,193},{129,1},{193,65... | collective-permute-start | bytes 1376264 | tf_op jit(solution)/shard_map/ppermute | solution.py:251
  74.9 22.0 %collective-permute-start.8 = (bf16[2,128,896]{2,1,0:T(8,128)(2,1)S(1)}, bf16[2,128,896]{2,1,0:T(8,128)(2,1)S(1)}, u32[]{:S(2)}, u32[]{:S(2)}) collective-permute-start(bf16[2,128,896]{2,1,0:T(8,128)(2,1)S(1)} %get-tuple-element.86), channel_id=1, source_target_pairs={{0,192},{64,128},{128,64},{192,0},{1,193},{65,129},{129,65},{193,1... | collective-permute-start | bytes 1376264 | tf_op jit(solution)/shard_map/ppermute | solution.py:251
  99.2 9.3 %collective-permute-start.10 = (bf16[128,896]{1,0:T(8,128)(2,1)S(1)}, bf16[128,896]{1,0:T(8,128)(2,1)S(1)}, u32[]{:S(2)}, u32[]{:S(2)}) collective-permute-start(bf16[128,896]{1,0:T(8,128)(2,1)S(1)} %get-tuple-element.95), channel_id=1, source_target_pairs={{0,128},{64,192},{128,0},{192,64},{1,129},{65,193},{129,1},{193,65... | collective-permute-start | bytes 688136 | tf_op jit(solution)/shard_map/ppermute | solution.py:251
  99.3 11.4 %collective-permute-start.11 = (bf16[128,896]{1,0:T(8,128)(2,1)S(1)}, bf16[128,896]{1,0:T(8,128)(2,1)S(1)}, u32[]{:S(2)}, u32[]{:S(2)}) collective-permute-start(bf16[128,896]{1,0:T(8,128)(2,1)S(1)} %get-tuple-element.96), channel_id=1, source_target_pairs={{0,192},{64,128},{128,64},{192,0},{1,193},{65,129},{129,65},{193,1... | collective-permute-start | bytes 688136 | tf_op jit(solution)/shard_map/ppermute | solution.py:251
  101.1 9.6 %collective-permute-start.9 = (bf16[128,896]{1,0:T(8,128)(2,1)S(1)}, bf16[128,896]{1,0:T(8,128)(2,1)S(1)}, u32[]{:S(2)}, u32[]{:S(2)}) collective-permute-start(bf16[128,896]{1,0:T(8,128)(2,1)S(1)} %get-tuple-element.94), channel_id=1, source_target_pairs={{0,64},{64,0},{128,192},{192,128},{1,65},{65,1},{129,193},{193,129... | collective-permute-start | bytes 688136 | tf_op jit(solution)/shard_map/ppermute | solution.py:251
  129.5 8.3 %collective-permute-start.15 = (bf16[7,128,128]{2,1,0:T(8,128)(2,1)S(1)}, bf16[7,128,128]{2,1,0:T(8,128)(2,1)S(1)}, u32[]{:S(2)}, u32[]{:S(2)}) collective-permute-start(bf16[7,128,128]{2,1,0:T(8,128)(2,1)S(1)} %get-tuple-element.103), channel_id=1, source_target_pairs={{0,16},{16,0},{32,48},{48,32},{1,17},{17,1},{33,49},{49,33},{2,18}... | collective-permute-start | bytes 688136 | tf_op jit(solution)/shard_map/ppermute | solution.py:251
  131.9 22.5 %collective-permute-start.12 = (bf16[2,128,896]{2,1,0:T(8,128)(2,1)S(1)}, bf16[2,128,896]{2,1,0:T(8,128)(2,1)S(1)}, u32[]{:S(2)}, u32[]{:S(2)}) collective-permute-start(bf16[2,128,896]{2,1,0:T(8,128)(2,1)S(1)} %get-tuple-element.106.a0), channel_id=1, source_target_pairs={{0,64},{64,0},{128,192},{192,128},{1,65},{65,1},{129,193},{193,129... | collective-permute-start | bytes 1376264 | tf_op jit(solution)/shard_map/ppermute | solution.py:251
  132.0 22.5 %collective-permute-start.13 = (bf16[2,128,896]{2,1,0:T(8,128)(2,1)S(1)}, bf16[2,128,896]{2,1,0:T(8,128)(2,1)S(1)}, u32[]{:S(2)}, u32[]{:S(2)}) collective-permute-start(bf16[2,128,896]{2,1,0:T(8,128)(2,1)S(1)} %get-tuple-element.106.a0), channel_id=1, source_target_pairs={{0,128},{64,192},{128,0},{192,64},{1,129},{65,193},{129,1},{193,65... | collective-permute-start | bytes 1376264 | tf_op jit(solution)/shard_map/ppermute | solution.py:251
  134.5 20.0 %collective-permute-start.14 = (bf16[2,128,896]{2,1,0:T(8,128)(2,1)S(1)}, bf16[2,128,896]{2,1,0:T(8,128)(2,1)S(1)}, u32[]{:S(2)}, u32[]{:S(2)}) collective-permute-start(bf16[2,128,896]{2,1,0:T(8,128)(2,1)S(1)} %get-tuple-element.106.a0), channel_id=1, source_target_pairs={{0,192},{64,128},{128,64},{192,0},{1,193},{65,129},{129,65},{193,1... | collective-permute-start | bytes 1376264 | tf_op jit(solution)/shard_map/ppermute | solution.py:251
  136.7 13.2 %collective-permute-start.16 = (bf16[7,128,128]{2,1,0:T(8,128)(2,1)S(1)}, bf16[7,128,128]{2,1,0:T(8,128)(2,1)S(1)}, u32[]{:S(2)}, u32[]{:S(2)}) collective-permute-start(bf16[7,128,128]{2,1,0:T(8,128)(2,1)S(1)} %get-tuple-element.104), channel_id=1, source_target_pairs={{0,32},{16,48},{32,0},{48,16},{1,33},{17,49},{33,1},{49,17},{2,34}... | collective-permute-start | bytes 688136 | tf_op jit(solution)/shard_map/ppermute | solution.py:251
  137.8 16.6 %collective-permute-start.17 = (bf16[7,128,128]{2,1,0:T(8,128)(2,1)S(1)}, bf16[7,128,128]{2,1,0:T(8,128)(2,1)S(1)}, u32[]{:S(2)}, u32[]{:S(2)}) collective-permute-start(bf16[7,128,128]{2,1,0:T(8,128)(2,1)S(1)} %get-tuple-element.105), channel_id=1, source_target_pairs={{0,48},{16,32},{32,16},{48,0},{1,49},{17,33},{33,17},{49,1},{2,50}... | collective-permute-start | bytes 688136 | tf_op jit(solution)/shard_map/ppermute | solution.py:251
  158.5 6.0 %collective-permute-start.18 = (bf16[4,2,2,128,256]{4,3,2,1,0:T(8,128)(2,1)S(1)}, bf16[4,2,2,128,256]{4,3,2,1,0:T(8,128)(2,1)S(1)}, u32[]{:S(2)}, u32[]{:S(2)}) collective-permute-start(bf16[4,2,2,128,256]{4,3,2,1,0:T(8,128)(2,1)S(1)} %get-tuple-element.119), channel_id=1, source_target_pairs={{0,1},{1,0},{2,3},{3,2},{4,5},{5,4},{6,7},{7,6},{8,9},{9,8},{10,11... | collective-permute-start | bytes 3145736 | tf_op jit(solution)/shard_map/ppermute | solution.py:251
  165.2 9.5 %collective-permute-start.19 = (bf16[2,2,128,256]{3,2,1,0:T(8,128)(2,1)S(1)}, bf16[2,2,128,256]{3,2,1,0:T(8,128)(2,1)S(1)}, u32[]{:S(2)}, u32[]{:S(2)}) collective-permute-start(bf16[2,2,128,256]{3,2,1,0:T(8,128)(2,1)S(1)} %get-tuple-element.121), channel_id=1, source_target_pairs={{0,4},{4,0},{8,12},{12,8},{1,5},{5,1},{9,13},{13,9},{2,6},{6,2},{1... | collective-permute-start | bytes 786440 | tf_op jit(solution)/shard_map/ppermute | solution.py:251
  167.6 30.0 %collective-permute-start.24 = (bf16[2,7,128,128]{3,2,1,0:T(8,128)(2,1)S(1)}, bf16[2,7,128,128]{3,2,1,0:T(8,128)(2,1)S(1)}, u32[]{:S(2)}, u32[]{:S(2)}) collective-permute-start(bf16[2,7,128,128]{3,2,1,0:T(8,128)(2,1)S(1)} %get-tuple-element.117), channel_id=1, source_target_pairs={{0,16},{16,0},{32,48},{48,32},{1,17},{17,1},{33,49},{49,33},{2,18}... | collective-permute-start | bytes 1376264 | tf_op jit(solution)/shard_map/ppermute | solution.py:251
  167.6 36.6 %collective-permute-start.25 = (bf16[2,7,128,128]{3,2,1,0:T(8,128)(2,1)S(1)}, bf16[2,7,128,128]{3,2,1,0:T(8,128)(2,1)S(1)}, u32[]{:S(2)}, u32[]{:S(2)}) collective-permute-start(bf16[2,7,128,128]{3,2,1,0:T(8,128)(2,1)S(1)} %get-tuple-element.129), channel_id=1, source_target_pairs={{0,32},{16,48},{32,0},{48,16},{1,33},{17,49},{33,1},{49,17},{2,34}... | collective-permute-start | bytes 1376264 | tf_op jit(solution)/shard_map/ppermute | solution.py:251
  170.7 45.9 %collective-permute-start.26 = (bf16[2,7,128,128]{3,2,1,0:T(8,128)(2,1)S(1)}, bf16[2,7,128,128]{3,2,1,0:T(8,128)(2,1)S(1)}, u32[]{:S(2)}, u32[]{:S(2)}) collective-permute-start(bf16[2,7,128,128]{3,2,1,0:T(8,128)(2,1)S(1)} %get-tuple-element.130), channel_id=1, source_target_pairs={{0,48},{16,32},{32,16},{48,0},{1,49},{17,33},{33,17},{49,1},{2,50}... | collective-permute-start | bytes 1376264 | tf_op jit(solution)/shard_map/ppermute | solution.py:251
  171.1 9.4 %collective-permute-start.20 = (bf16[2,2,128,256]{3,2,1,0:T(8,128)(2,1)S(1)}, bf16[2,2,128,256]{3,2,1,0:T(8,128)(2,1)S(1)}, u32[]{:S(2)}, u32[]{:S(2)}) collective-permute-start(bf16[2,2,128,256]{3,2,1,0:T(8,128)(2,1)S(1)} %get-tuple-element.122), channel_id=1, source_target_pairs={{0,8},{4,12},{8,0},{12,4},{1,9},{5,13},{9,1},{13,5},{2,10},{6,14},... | collective-permute-start | bytes 786440 | tf_op jit(solution)/shard_map/ppermute | solution.py:251
  174.7 11.2 %collective-permute-start.21 = (bf16[2,2,128,256]{3,2,1,0:T(8,128)(2,1)S(1)}, bf16[2,2,128,256]{3,2,1,0:T(8,128)(2,1)S(1)}, u32[]{:S(2)}, u32[]{:S(2)}) collective-permute-start(bf16[2,2,128,256]{3,2,1,0:T(8,128)(2,1)S(1)} %get-tuple-element.123), channel_id=1, source_target_pairs={{0,12},{4,8},{8,4},{12,0},{1,13},{5,9},{9,5},{13,1},{2,14},{6,10},... | collective-permute-start | bytes 786440 | tf_op jit(solution)/shard_map/ppermute | solution.py:251
  186.7 31.9 %collective-permute-start.22 = (bf16[2,128,256]{2,1,0:T(8,128)(2,1)S(1)}, bf16[2,128,256]{2,1,0:T(8,128)(2,1)S(1)}, u32[]{:S(2)}, u32[]{:S(2)}) collective-permute-start(bf16[2,128,256]{2,1,0:T(8,128)(2,1)S(1)} %get-tuple-element.124), channel_id=1, source_target_pairs={{0,0},{2,2},{4,64},{6,66},{8,128},{10,130},{12,192},{14,194},{64,4... | collective-permute-start | bytes 393224 | tf_op jit(solution)/shard_map/ppermute | solution.py:269
  189.6 29.0 %collective-permute-start.23 = (bf16[2,128,256]{2,1,0:T(8,128)(2,1)S(1)}, bf16[2,128,256]{2,1,0:T(8,128)(2,1)S(1)}, u32[]{:S(2)}, u32[]{:S(2)}) collective-permute-start(bf16[2,128,256]{2,1,0:T(8,128)(2,1)S(1)} %get-tuple-element.125), channel_id=1, source_target_pairs={{0,2},{2,0},{4,66},{6,64},{8,130},{10,128},{12,194},{14,192},{64,6... | collective-permute-start | bytes 393224 | tf_op jit(solution)/shard_map/ppermute | solution.py:269

commit v4 on v3

--- a/solution.py
+++ b/solution.py
@@ -47,8 +47,9 @@
     return pl.ds(a * B, B), pl.ds(b * B, B)
 
 
-def pack(mask, tile, which, source, out):
-    for rr, cc, on, slot in cells(mask, tile, which):
+def pack(mask, tile, which, source, out, layout=None):
+    layout = which if layout is None else layout
+    for at, (rr, cc, on, slot) in enumerate(cells(mask, tile, which)):
         if rr is None:
             for p in range(5, 7):
 
@@ -56,11 +57,13 @@
                 def _(p=p):
                     out[p] = jnp.zeros((B, B), out.dtype)
 
+        elif at < 7:
+            out[slot] = source[sub(rr, cc, layout)].astype(out.dtype)
         else:
 
             @pl.when(on)
             def _(rr=rr, cc=cc, slot=slot):
-                out[slot] = source[sub(rr, cc, which)].astype(out.dtype)
+                out[slot] = source[sub(rr, cc, layout)].astype(out.dtype)
 
 
 def unpack(mask, tile, which, block, store):
@@ -167,22 +170,31 @@
 NT = (((1,), (1,)), ((), ()))
 
 
-def k_down_grad(pos, mask, hid, cot, d0, d1, d2, d3, acc):
+def k_turn(a, b, at, bt):
+    at[...] = a[...].T
+    bt[...] = b[...].T
+
+
+def rows_of(q):
+    return pl.ds(pl.multiple_of(q * 256, 256), 256)
+
+
+def k_down_grad(pos, mask, hid, cot_t, d0, d1, d2, d3, acc):
     y, z = pos[0], pos[1]
-    left = hid[...].reshape(512, 896)
+    right = hid[...].reshape(512, 896)
     for j, out in ((1, d1), (2, d2), (3, d3), (0, d0)):
         zz = jnp.bitwise_xor(z, j)
-        acc[...] = lax.dot_general(left, cot[:, columns(zz)], TN, preferred_element_type=F32)
-        pack(mask, 4 * y + zz, DOWN, acc, out)
-
-
-def k_weight_grad(pos, mask, act, tok, d0, d1, d2, d3, acc):
+        acc[...] = jnp.dot(cot_t[rows_of(zz), :], right, preferred_element_type=F32)
+        pack(mask, 4 * y + zz, DOWN, acc, out, GATE)
+
+
+def k_weight_grad(pos, mask, act, tok_t, d0, d1, d2, d3, acc):
     y, z = pos[0], pos[1]
     for half, which in enumerate((GATE, UP)):
         right = act[half].reshape(512, 896)
         for j, out in ((1, d1), (2, d2), (3, d3), (0, d0)):
             zz = jnp.bitwise_xor(z, j)
-            acc[...] = lax.dot_general(tok[:, columns(zz)], right, TN, preferred_element_type=F32)
+            acc[...] = jnp.dot(tok_t[rows_of(zz), :], right, preferred_element_type=F32)
             pack(mask, 4 * y + zz, which, acc, out.at[half])
 
 
@@ -233,7 +245,7 @@
         return total(a0.at[i], a1.at[i], a2.at[i], a3.at[i])
 
     def store(rr, cc, v):
-        out[sub(rr, cc, which)] = v.astype(BF)
+        out[sub(rr, cc, which)] = (v.T if which == DOWN else v).astype(BF)
 
     unpack(mask, pos[0] * 4 + pos[1], which, block, store)
 
@@ -310,15 +322,19 @@
     )
     wu = u[4]
     u_all = collect(u[0], u[1:4], "y")
+    cot, tok, _ = lax.optimization_barrier((cot, tok, u[1]))
+    cot_t, tok_t = call(k_turn, (0, 0), (cot, tok), (sds((1024, 512)), sds((1024, 512))))
+    u_own, cot_t, tok_t = lax.optimization_barrier((u[0], cot_t, tok_t))
+    u_all = [u_own] + u_all[1:]
     hidden, act = call(k_act, (0,) * 8, (*g_all, *u_all), (sds(blk), sds((2, B, 896))))
     hidden = lax.all_gather(hidden, "y", axis=0)
     hidden, act = lax.optimization_barrier((hidden, act))
     act_all = spread(act, "y")
     blk = (7, B, B)
     e = call(
-        k_down_grad, (1, 1, 0, 0), (pos, mask, hidden, cot),
+        k_down_grad, (1, 1, 0, 0), (pos, mask, hidden, cot_t),
         (sds(blk, F32), sds(blk), sds(blk), sds(blk)),
-        (pltpu.VMEM((896, 256), F32),), small=True,
+        (pltpu.VMEM((256, 896), F32),), small=True,
     )
     e_all = collect(e[0], e[1:4], "z")
     act_all, e_all = lax.optimization_barrier((act_all, e_all))
@@ -331,7 +347,7 @@
     act, keep = lax.optimization_barrier((act, keep))
     blk = (2, 7, B, B)
     f = call(
-        k_weight_grad, (1, 1, 0, 0), (pos, mask, act, tok),
+        k_weight_grad, (1, 1, 0, 0), (pos, mask, act, tok_t),
         (sds(blk, F32), sds(blk), sds(blk), sds(blk)),
         (pltpu.VMEM((256, 896), F32),), flops=2 * flops,
     )

time: 220 us -> 218 us (level)
    pallas_call x12 -> x13, Pallas kernels: 29.5 us -> 28.2 us  [call(): pl.pallas_call(kernel, out_shape=tuple(outs), in_specs=[(VM, SM, pl.Block...]
where the time goes in v4:
time: 218 us; the launch traced here: 217 us
  blocking collectives  74.6 us (34%)
  waiting for transfers between devices  58.5 us (27%)
  starting transfers between devices  52.2 us (24%)
  Pallas kernels  28.2 us (13%)
  other arithmetic  2.37 us (1%)
    ppermute x23, waiting for transfers between devices, exchange(): return lax.ppermute(value, axis, [(i, i ^ by) for i in range(size)])  56.3 us
    ppermute x23, starting transfers between devices, exchange(): return lax.ppermute(value, axis, [(i, i ^ by) for i in range(size)])  32.5 us
    pallas_call x13, Pallas kernels, call(): pl.pallas_call(kernel, out_shape=tuple(outs), in_specs=[(VM, SM, pl.Block...  28.2 us
    all_gather x1, blocking collectives, body(): dp = lax.all_gather(dp, 'z', axis=0)  21 us
    all_gather x1, blocking collectives, body(): gp = lax.all_gather(gp, 'z', axis=0)  20.3 us
    ppermute x4, starting transfers between devices, swap(): return lax.ppermute(value, ('y', 'x', 'h'), pairs)  19.7 us
    all_gather x1, blocking collectives, body(): up = lax.all_gather(up, 'z', axis=0)  19 us
    all_gather x1, blocking collectives, body(): hidden = lax.all_gather(hidden, 'y', axis=0)  14.4 us
  transfers between devices with their start and end apart: 27, of which 11 were waited for; matrix products, arithmetic and copies ran while one was open for 1% of the time, Pallas kernels for 6%

profile of v4, /device:TPU:34, one launch (start us, length us, event | category | flops | bytes accessed | tf_op | source)
XLA Modules:
  0.0 217.4 jit_solution(18053671057184005910)
XLA Ops:
  0.6 0.9 pad_maximum_fusion.2
  1.5 7.4 %collective-permute-start.1 = (bf16[2,128,256]{2,1,0:T(8,128)(2,1)S(1)}, bf16[2,128,256]{2,1,0:T(8,128)(2,1)S(1)}, u32[]{:S(2)}, u32[]{:S(2)}) collective-permute-start(bf16[2,128,256]{2,1,0:T(8,128)(2,1)S(1)} %pad_maximum_fusion.2), channel_id=1, source_target_pairs={{0,2},{2,0},{4,66},{6,64},{8,130},{10,128},{12,194},{14,192},{64,6... | collective-permute-start | bytes 393224 | tf_op jit(solution)/shard_map/ppermute | solution.py:281
  8.9 3.3 %collective-permute-start = (bf16[2,128,256]{2,1,0:T(8,128)(2,1)S(1)}, bf16[2,128,256]{2,1,0:T(8,128)(2,1)S(1)}, u32[]{:S(2)}, u32[]{:S(2)}) collective-permute-start(bf16[2,128,256]{2,1,0:T(8,128)(2,1)S(1)} %pad_maximum_fusion.2), channel_id=1, source_target_pairs={{0,0},{2,2},{4,64},{6,66},{8,128},{10,130},{12,192},{14,194},{64,4... | collective-permute-start | bytes 393224 | tf_op jit(solution)/shard_map/ppermute | solution.py:281
  12.2 0.6 stack.56.pos
  12.8 1.3 pad_add_fusion.mask
  14.1 3.1 %shard_map.119 = (bf16[7,128,128]{2,1,0:T(8,128)(2,1)}, bf16[7,128,128]{2,1,0:T(8,128)(2,1)}, bf16[7,128,128]{2,1,0:T(8,128)(2,1)}) custom-call(s32[5]{0:T(128)} %stack.56.pos, s32[21,32]{1,0:T(8,128)} %pad_add_fusion.mask, bf16[256,896]{1,0:T(8,128)(2,1)} %gw.1, bf16[256,896]{1,0:T(8,128)(2,1)} %uw.1, bf16[896,256]{1,0:T(8,128)(2,1)} %dw.1), custom_call_target="tpu_custom_call" | custom-call | bytes 2067092 | tf_op jit(solution)/shard_map/pallas_call | solution.py:21
  17.3 2.2 %collective-permute-done = bf16[2,128,256]{2,1,0:T(8,128)(2,1)S(1)} collective-permute-done((bf16[2,128,256]{2,1,0:T(8,128)(2,1)S(1)}, bf16[2,128,256]{2,1,0:T(8,128)(2,1)S(1)}, u32[]{:S(2)}, u32[]{:S(2)}) %collective-permute-start) | collective-permute-done | bytes 131104 | tf_op jit(solution)/shard_map/ppermute | solution.py:281
  19.6 6.9 %collective-permute-start.3 = (bf16[2,2,128,256]{3,2,1,0:T(8,128)(2,1)S(1)}, bf16[2,2,128,256]{3,2,1,0:T(8,128)(2,1)S(1)}, u32[]{:S(2)}, u32[]{:S(2)}) collective-permute-start(bf16[2,2,128,256]{3,2,1,0:T(8,128)(2,1)S(1)} %pad_maximum_fusion.1), channel_id=1, source_target_pairs={{0,8},{4,12},{8,0},{12,4},{1,9},{5,13},{9,1},{13,5},{2,10},{6,14},... | collective-permute-start | bytes 786440 | tf_op jit(solution)/shard_map/ppermute | solution.py:263
  26.5 21.0 %all-gather = bf16[28,128,128]{2,1,0:T(8,128)(2,1)S(1)} all-gather(bf16[7,128,128]{2,1,0:T(8,128)(2,1)} %get-tuple-element.81), channel_id=2, replica_groups=mesh['y'=4,'z'=4,'x'=4,'h'=2,'k'=2] {'z'}, dimensions={0}, use_global_device_ids=true | all-gather | bytes 1146880 | tf_op jit(solution)/shard_map/all_gather | solution.py:299
  47.7 20.3 %all-gather.1 = bf16[28,128,128]{2,1,0:T(8,128)(2,1)S(1)} all-gather(bf16[7,128,128]{2,1,0:T(8,128)(2,1)S(1)} %copy-done.3), channel_id=3, replica_groups=mesh['y'=4,'z'=4,'x'=4,'h'=2,'k'=2] {'z'}, dimensions={0}, use_global_device_ids=true | all-gather | bytes 1146880 | tf_op jit(solution)/shard_map/all_gather | solution.py:303
  68.0 3.8 %shard_map.120 = (f32[2,128,896]{2,1,0:T(8,128)S(1)}, bf16[2,128,896]{2,1,0:T(8,128)(2,1)S(1)}, bf16[2,128,896]{2,1,0:T(8,128)(2,1)S(1)}, bf16[2,128,896]{2,1,0:...) custom-call(s32[5]{0:T(128)S(1)} %copy-done.1, ...), custom_call_target="tpu_custom_call" | custom-call | flops 1879048192 | bytes 11995796 | tf_op jit(solution)/shard_map/pallas_call | solution.py:21
  72.0 2.8 %collective-permute-start.7 = (bf16[2,128,896]{2,1,0:T(8,128)(2,1)S(1)}, bf16[2,128,896]{2,1,0:T(8,128)(2,1)S(1)}, u32[]{:S(2)}, u32[]{:S(2)}) collective-permute-start(bf16[2,128,896]{2,1,0:T(8,128)(2,1)S(1)} %get-tuple-element.92), channel_id=1, source_target_pairs={{0,128},{64,192},{128,0},{192,64},{1,129},{65,193},{129,1},{193,65... | collective-permute-start | bytes 1376264 | tf_op jit(solution)/shard_map/ppermute | solution.py:263
  74.9 1.8 collective-permute-start.8
  76.6 19.0 %all-gather.2 = bf16[28,128,128]{2,1,0:T(8,128)(2,1)S(1)} all-gather(bf16[7,128,128]{2,1,0:T(8,128)(2,1)S(1)} %copy-done.2), channel_id=4, replica_groups=mesh['y'=4,'z'=4,'x'=4,'h'=2,'k'=2] {'z'}, dimensions={0}, use_global_device_ids=true | all-gather | bytes 1146880 | tf_op jit(solution)/shard_map/all_gather | solution.py:316
  95.6 1.3 collective-permute-done.8.a3
  96.9 2.3 %shard_map.121 = (f32[128,896]{1,0:T(8,128)S(1)}, bf16[128,896]{1,0:T(8,128)(2,1)S(1)}, bf16[128,896]{1,0:T(8,128)(2,1)S(1)}, bf16[128,896]{1,0:T(8,128)(2,1)S(1)}, bf16[1024,896]{1,0:T(8,128)(2,1)S(1)}) custom-call(s32[5]{0:T(128)S(1)} %copy-done.1, s32[21,32]{1,0:T(8,128)S(1)} %copy-done, bf16[4,7,128,128]{3,2,1,0:T(8,128)(2,1)S(1)} %bitcast.22, ...), custom_call_target="tpu_custom_call" | custom-call | flops 939524096 | bytes 4950676 | tf_op jit(solution)/shard_map/pallas_call | solution.py:21
  99.3 1.8 collective-permute-start.11
  101.1 1.7 collective-permute-start.9
  102.8 0.6 shard_map.122
  103.4 5.1 %collective-permute-done.10.b2 = bf16[128,896]{1,0:T(8,128)(2,1)S(1)} collective-permute-done((bf16[128,896]{1,0:T(8,128)(2,1)S(1)}, bf16[128,896]{1,0:T(8,128)(2,1)S(1)}, u32[]{:S(2)}, u32[]{:S(2)}) %collective-permute-start.10) | collective-permute-done | bytes 229408 | tf_op jit(solution)/shard_map/ppermute | solution.py:263
  108.5 2.2 collective-permute-done.11.b3
  111.2 14.4 %all-gather.3 = bf16[512,896]{1,0:T(8,128)(2,1)S(1)} all-gather(bf16[128,896]{1,0:T(8,128)(2,1)S(1)} %get-tuple-element.110), channel_id=5, replica_groups=mesh['y'=4,'z'=4,'x'=4,'h'=2,'k'=2] {'y'}, dimensions={0}, use_global_device_ids=true | all-gather | bytes 1146880 | tf_op jit(solution)/shard_map/all_gather | solution.py:330
  125.6 2.8 %shard_map.124 = (f32[7,128,128]{2,1,0:T(8,128)S(1)}, bf16[7,128,128]{2,1,0:T(8,128)(2,1)S(1)}, bf16[7,128,128]{2,1,0:T(8,128)(2,1)S(1)}, bf16[7,128,128]{2,1,0:T(8,128)(2,1)S(1)}) custom-call(s32[5]{0:T(128)S(1)} %copy-done.1, s32[21,32]{1,0:T(8,128)S(1)} %copy-done, bf16[4,128,896]{2,1,0:T(8,128)(2,1)S(1)} %bitcast.19, ...), custom_call_target="tpu_custom_call" | custom-call | tf_op jit(solution)/shard_map/pallas_call | solution.py:21
  128.4 2.5 %collective-permute-start.15 = (bf16[7,128,128]{2,1,0:T(8,128)(2,1)S(1)}, bf16[7,128,128]{2,1,0:T(8,128)(2,1)S(1)}, u32[]{:S(2)}, u32[]{:S(2)}) collective-permute-start(bf16[7,128,128]{2,1,0:T(8,128)(2,1)S(1)} %get-tuple-element.116), channel_id=1, source_target_pairs={{0,16},{16,0},{32,48},{48,32},{1,17},{17,1},{33,49},{49,33},{2,18}... | collective-permute-start | bytes 688136 | tf_op jit(solution)/shard_map/ppermute | solution.py:263
  130.9 2.5 %collective-permute-start.13 = (bf16[2,128,896]{2,1,0:T(8,128)(2,1)S(1)}, bf16[2,128,896]{2,1,0:T(8,128)(2,1)S(1)}, u32[]{:S(2)}, u32[]{:S(2)}) collective-permute-start(bf16[2,128,896]{2,1,0:T(8,128)(2,1)S(1)} %get-tuple-element.119.a0), channel_id=1, source_target_pairs={{0,128},{64,192},{128,0},{192,64},{1,129},{65,193},{129,1},{193,65... | collective-permute-start | bytes 1376264 | tf_op jit(solution)/shard_map/ppermute | solution.py:263
  133.4 2.2 %collective-permute-start.14 = (bf16[2,128,896]{2,1,0:T(8,128)(2,1)S(1)}, bf16[2,128,896]{2,1,0:T(8,128)(2,1)S(1)}, u32[]{:S(2)}, u32[]{:S(2)}) collective-permute-start(bf16[2,128,896]{2,1,0:T(8,128)(2,1)S(1)} %get-tuple-element.119.a0), channel_id=1, source_target_pairs={{0,192},{64,128},{128,64},{192,0},{1,193},{65,129},{129,65},{193,1... | collective-permute-start | bytes 1376264 | tf_op jit(solution)/shard_map/ppermute | solution.py:263
  135.6 1.0 collective-permute-start.16
  136.7 1.6 collective-permute-start.17
  138.3 10.5 %collective-permute-done.16.a2 = bf16[7,128,128]{2,1,0:T(8,128)(2,1)S(1)} collective-permute-done((bf16[7,128,128]{2,1,0:T(8,128)(2,1)S(1)}, bf16[7,128,128]{2,1,0:T(8,128)(2,1)S(1)}, u32[]{:S(2)}, u32[]{:S(2)}) %collective-permute-start.16) | collective-permute-done | bytes 229408 | tf_op jit(solution)/shard_map/ppermute | solution.py:263
  148.8 4.6 %collective-permute-done.17.a3 = bf16[7,128,128]{2,1,0:T(8,128)(2,1)S(1)} collective-permute-done((bf16[7,128,128]{2,1,0:T(8,128)(2,1)S(1)}, bf16[7,128,128]{2,1,0:T(8,128)(2,1)S(1)}, u32[]{:S(2)}, u32[]{:S(2)}) %collective-permute-start.17) | collective-permute-done | bytes 229408 | tf_op jit(solution)/shard_map/ppermute | solution.py:263
  153.4 4.1 %shard_map.125 = (bf16[2,4,128,896]{3,2,1,0:T(8,128)(2,1)S(1)}, f32[4,2,2,128,256]{4,3,2,1,0:T(8,128)S(1)}, bf16[4,2,2,128,256]{4,3,2,1,0:T(8,128)(2,1)S(1)}) custom-call(s32[5]{0:T(128)S(1)} %copy-done.1, bf16[4,128,896]{2,1,0:T(8,128)(2,1)S(1)} %bitcast.20, bf16[2,128,896]{2,1,0:T(8,128)(2,1)S(1)} %get-tuple-element.119.a0, ...), custom_call_target="tpu_custom_call" | custom-call | flops 2818572288 | bytes 13238292 | tf_op jit(solution)/shard_map/pallas_call | solution.py:21
  157.6 5.0 %shard_map.126 = (f32[2,7,128,128]{3,2,1,0:T(8,128)S(1)}, bf16[2,7,128,128]{3,2,1,0:T(8,128)(2,1)S(1)}, bf16[2,7,128,128]{3,2,1,0:T(8,128)(2,1)S(1)}, bf16[2,7,128,128]{3,2,1,0:T(8,128)(2,1)S(1)}) custom-call(s32[5]{0:T(128)S(1)} %copy-done.1, s32[21,32]{1,0:T(8,128)S(1)} %copy-done, bf16[2,4,128,896]{3,2,1,0:T(8,128)(2,1)S(1)} %get-tuple-element.129.act, ...), custom_call_target="tpu_custom_call" | custom-call | flops 1879048192 | bytes 5180052 | tf_op jit(solution)/shard_map/pallas_call | solution.py:21
  162.5 0.8 shard_map.127
  163.3 2.3 %collective-permute-start.19 = (bf16[2,2,128,256]{3,2,1,0:T(8,128)(2,1)S(1)}, bf16[2,2,128,256]{3,2,1,0:T(8,128)(2,1)S(1)}, u32[]{:S(2)}, u32[]{:S(2)}) collective-permute-start(bf16[2,2,128,256]{3,2,1,0:T(8,128)(2,1)S(1)} %get-tuple-element.135), channel_id=1, source_target_pairs={{0,4},{4,0},{8,12},{12,8},{1,5},{5,1},{9,13},{13,9},{2,6},{6,2},{1... | collective-permute-start | bytes 786440 | tf_op jit(solution)/shard_map/ppermute | solution.py:263
  165.7 3.0 %collective-permute-start.25 = (bf16[2,7,128,128]{3,2,1,0:T(8,128)(2,1)S(1)}, bf16[2,7,128,128]{3,2,1,0:T(8,128)(2,1)S(1)}, u32[]{:S(2)}, u32[]{:S(2)}) collective-permute-start(bf16[2,7,128,128]{3,2,1,0:T(8,128)(2,1)S(1)} %get-tuple-element.143), channel_id=1, source_target_pairs={{0,32},{16,48},{32,0},{48,16},{1,33},{17,49},{33,1},{49,17},{2,34}... | collective-permute-start | bytes 1376264 | tf_op jit(solution)/shard_map/ppermute | solution.py:263
  169.1 0.5 collective-permute-start.20
  169.7 3.1 %collective-permute-done.19.a1 = bf16[2,2,128,256]{3,2,1,0:T(8,128)(2,1)S(1)} collective-permute-done((bf16[2,2,128,256]{3,2,1,0:T(8,128)(2,1)S(1)}, bf16[2,2,128,256]{3,2,1,0:T(8,128)(2,1)S(1)}, u32[]{:S(2)}, u32[]{:S(2)}) %collective-permute-start.19) | collective-permute-done | bytes 262176 | tf_op jit(solution)/shard_map/ppermute | solution.py:263
  172.8 0.8 collective-permute-start.21
  173.6 5.0 %collective-permute-done.20.a2 = bf16[2,2,128,256]{3,2,1,0:T(8,128)(2,1)S(1)} collective-permute-done((bf16[2,2,128,256]{3,2,1,0:T(8,128)(2,1)S(1)}, bf16[2,2,128,256]{3,2,1,0:T(8,128)(2,1)S(1)}, u32[]{:S(2)}, u32[]{:S(2)}) %collective-permute-start.20) | collective-permute-done | bytes 262176 | tf_op jit(solution)/shard_map/ppermute | solution.py:263
  178.6 5.5 %collective-permute-done.21.a3 = bf16[2,2,128,256]{3,2,1,0:T(8,128)(2,1)S(1)} collective-permute-done((bf16[2,2,128,256]{3,2,1,0:T(8,128)(2,1)S(1)}, bf16[2,2,128,256]{3,2,1,0:T(8,128)(2,1)S(1)}, u32[]{:S(2)}, u32[]{:S(2)}) %collective-permute-start.21) | collective-permute-done | bytes 262176 | tf_op jit(solution)/shard_map/ppermute | solution.py:263
  184.1 0.7 shard_map.128
  184.8 2.8 %collective-permute-start.22 = (bf16[2,128,256]{2,1,0:T(8,128)(2,1)S(1)}, bf16[2,128,256]{2,1,0:T(8,128)(2,1)S(1)}, u32[]{:S(2)}, u32[]{:S(2)}) collective-permute-start(bf16[2,128,256]{2,1,0:T(8,128)(2,1)S(1)} %get-tuple-element.138), channel_id=1, source_target_pairs={{0,0},{2,2},{4,64},{6,66},{8,128},{10,130},{12,192},{14,194},{64,4... | collective-permute-start | bytes 393224 | tf_op jit(solution)/shard_map/ppermute | solution.py:281
  187.7 6.2 %collective-permute-start.23 = (bf16[2,128,256]{2,1,0:T(8,128)(2,1)S(1)}, bf16[2,128,256]{2,1,0:T(8,128)(2,1)S(1)}, u32[]{:S(2)}, u32[]{:S(2)}) collective-permute-start(bf16[2,128,256]{2,1,0:T(8,128)(2,1)S(1)} %get-tuple-element.139), channel_id=1, source_target_pairs={{0,2},{2,0},{4,66},{6,64},{8,130},{10,128},{12,194},{14,192},{64,6... | collective-permute-start | bytes 393224 | tf_op jit(solution)/shard_map/ppermute | solution.py:281
  193.9 1.9 shard_map.131
  195.7 6.5 %collective-permute-done.25.a2 = bf16[2,7,128,128]{3,2,1,0:T(8,128)(2,1)S(1)} collective-permute-done((bf16[2,7,128,128]{3,2,1,0:T(8,128)(2,1)S(1)}, bf16[2,7,128,128]{3,2,1,0:T(8,128)(2,1)S(1)}, u32[]{:S(2)}, u32[]{:S(2)}) %collective-permute-start.25) | collective-permute-done | bytes 458784 | tf_op jit(solution)/shard_map/ppermute | solution.py:263
  202.2 12.4 %collective-permute-done.26.a3 = bf16[2,7,128,128]{3,2,1,0:T(8,128)(2,1)S(1)} collective-permute-done((bf16[2,7,128,128]{3,2,1,0:T(8,128)(2,1)S(1)}, bf16[2,7,128,128]{3,2,1,0:T(8,128)(2,1)S(1)}, u32[]{:S(2)}, u32[]{:S(2)}) %collective-permute-start.26) | collective-permute-done | bytes 458784 | tf_op jit(solution)/shard_map/ppermute | solution.py:263
  214.6 2.1 shard_map.130
  216.7 0.7 shard_map.129
  (36 shorter events, 1.7 us)
Async XLA Ops:
  1.5 15.7 %collective-permute-start.1 = (bf16[2,128,256]{2,1,0:T(8,128)(2,1)S(1)}, bf16[2,128,256]{2,1,0:T(8,128)(2,1)S(1)}, u32[]{:S(2)}, u32[]{:S(2)}) collective-permute-start(bf16[2,128,256]{2,1,0:T(8,128)(2,1)S(1)} %pad_maximum_fusion.2), channel_id=1, source_target_pairs={{0,2},{2,0},{4,66},{6,64},{8,130},{10,128},{12,194},{14,192},{64,6... | collective-permute-start | bytes 393224 | tf_op jit(solution)/shard_map/ppermute | solution.py:281
  8.9 10.6 %collective-permute-start = (bf16[2,128,256]{2,1,0:T(8,128)(2,1)S(1)}, bf16[2,128,256]{2,1,0:T(8,128)(2,1)S(1)}, u32[]{:S(2)}, u32[]{:S(2)}) collective-permute-start(bf16[2,128,256]{2,1,0:T(8,128)(2,1)S(1)} %pad_maximum_fusion.2), channel_id=1, source_target_pairs={{0,0},{2,2},{4,64},{6,66},{8,128},{10,130},{12,192},{14,194},{64,4... | collective-permute-start | bytes 393224 | tf_op jit(solution)/shard_map/ppermute | solution.py:281
  19.5 28.2 %copy-start.3 = (bf16[7,128,128]{2,1,0:T(8,128)(2,1)S(1)}, bf16[7,128,128]{2,1,0:T(8,128)(2,1)}, u32[]{:S(2)}) copy-start(bf16[7,128,128]{2,1,0:T(8,128)(2,1)} %get-tuple-element.84) | copy-start | bytes 688132
  19.5 27.9 %collective-permute-start.2 = (bf16[2,2,128,256]{3,2,1,0:T(8,128)(2,1)S(1)}, bf16[2,2,128,256]{3,2,1,0:T(8,128)(2,1)S(1)}, u32[]{:S(2)}, u32[]{:S(2)}) collective-permute-start(bf16[2,2,128,256]{3,2,1,0:T(8,128)(2,1)S(1)} %pad_maximum_fusion.1), channel_id=1, source_target_pairs={{0,4},{4,0},{8,12},{12,8},{1,5},{5,1},{9,13},{13,9},{2,6},{6,2},{1... | collective-permute-start | bytes 786440 | tf_op jit(solution)/shard_map/ppermute | solution.py:263
  19.6 27.8 %collective-permute-start.3 = (bf16[2,2,128,256]{3,2,1,0:T(8,128)(2,1)S(1)}, bf16[2,2,128,256]{3,2,1,0:T(8,128)(2,1)S(1)}, u32[]{:S(2)}, u32[]{:S(2)}) collective-permute-start(bf16[2,2,128,256]{3,2,1,0:T(8,128)(2,1)S(1)} %pad_maximum_fusion.1), channel_id=1, source_target_pairs={{0,8},{4,12},{8,0},{12,4},{1,9},{5,13},{9,1},{13,5},{2,10},{6,14},... | collective-permute-start | bytes 786440 | tf_op jit(solution)/shard_map/ppermute | solution.py:263
  26.5 21.0 %collective-permute-start.4 = (bf16[2,2,128,256]{3,2,1,0:T(8,128)(2,1)S(1)}, bf16[2,2,128,256]{3,2,1,0:T(8,128)(2,1)S(1)}, u32[]{:S(2)}, u32[]{:S(2)}) collective-permute-start(bf16[2,2,128,256]{3,2,1,0:T(8,128)(2,1)S(1)} %pad_maximum_fusion.1), channel_id=1, source_target_pairs={{0,12},{4,8},{8,4},{12,0},{1,13},{5,9},{9,5},{13,1},{2,14},{6,10},... | collective-permute-start | bytes 786440 | tf_op jit(solution)/shard_map/ppermute | solution.py:263
  47.5 20.5 %copy-start = (s32[21,32]{1,0:T(8,128)S(1)}, s32[21,32]{1,0:T(8,128)}, u32[]{:S(2)}) copy-start(s32[21,32]{1,0:T(8,128)} %pad_add_fusion.mask) | copy-start | bytes 8068
  47.5 20.5 %copy-start.1 = (s32[5]{0:T(128)S(1)}, s32[5]{0:T(128)}, u32[]{:S(2)}) copy-start(s32[5]{0:T(128)} %stack.56.pos) | copy-start | bytes 64
  47.6 20.4 %collective-permute-start.5 = (bf16[4,2,2,128,256]{4,3,2,1,0:T(8,128)(2,1)S(1)}, bf16[4,2,2,128,256]{4,3,2,1,0:T(8,128)(2,1)S(1)}, u32[]{:S(2)}, u32[]{:S(2)}) collective-permute-start(bf16[4,2,2,128,256]{4,3,2,1,0:T(8,128)(2,1)S(1)} %pad_maximum_fusion.mine), channel_id=1, source_target_pairs={{0,1},{1,0},{2,3},{3,2},{4,5},{5,4},{6,7},{7,6},{8,9},{9,8},{10,11... | collective-permute-start | bytes 3145736 | tf_op jit(solution)/shard_map/ppermute | solution.py:263
  68.0 8.6 %copy-start.2 = (bf16[7,128,128]{2,1,0:T(8,128)(2,1)S(1)}, bf16[7,128,128]{2,1,0:T(8,128)(2,1)}, u32[]{:S(2)}) copy-start(bf16[7,128,128]{2,1,0:T(8,128)(2,1)} %get-tuple-element.90) | copy-start | bytes 688132
  71.8 23.8 %collective-permute-start.6 = (bf16[2,128,896]{2,1,0:T(8,128)(2,1)S(1)}, bf16[2,128,896]{2,1,0:T(8,128)(2,1)S(1)}, u32[]{:S(2)}, u32[]{:S(2)}) collective-permute-start(bf16[2,128,896]{2,1,0:T(8,128)(2,1)S(1)} %get-tuple-element.89), channel_id=1, source_target_pairs={{0,64},{64,0},{128,192},{192,128},{1,65},{65,1},{129,193},{193,129... | collective-permute-start | bytes 1376264 | tf_op jit(solution)/shard_map/ppermute | solution.py:263
  72.0 23.6 %collective-permute-start.7 = (bf16[2,128,896]{2,1,0:T(8,128)(2,1)S(1)}, bf16[2,128,896]{2,1,0:T(8,128)(2,1)S(1)}, u32[]{:S(2)}, u32[]{:S(2)}) collective-permute-start(bf16[2,128,896]{2,1,0:T(8,128)(2,1)S(1)} %get-tuple-element.92), channel_id=1, source_target_pairs={{0,128},{64,192},{128,0},{192,64},{1,129},{65,193},{129,1},{193,65... | collective-permute-start | bytes 1376264 | tf_op jit(solution)/shard_map/ppermute | solution.py:263
  74.9 22.0 %collective-permute-start.8 = (bf16[2,128,896]{2,1,0:T(8,128)(2,1)S(1)}, bf16[2,128,896]{2,1,0:T(8,128)(2,1)S(1)}, u32[]{:S(2)}, u32[]{:S(2)}) collective-permute-start(bf16[2,128,896]{2,1,0:T(8,128)(2,1)S(1)} %get-tuple-element.93), channel_id=1, source_target_pairs={{0,192},{64,128},{128,64},{192,0},{1,193},{65,129},{129,65},{193,1... | collective-permute-start | bytes 1376264 | tf_op jit(solution)/shard_map/ppermute | solution.py:263
  99.2 9.3 %collective-permute-start.10 = (bf16[128,896]{1,0:T(8,128)(2,1)S(1)}, bf16[128,896]{1,0:T(8,128)(2,1)S(1)}, u32[]{:S(2)}, u32[]{:S(2)}) collective-permute-start(bf16[128,896]{1,0:T(8,128)(2,1)S(1)} %get-tuple-element.108), channel_id=1, source_target_pairs={{0,128},{64,192},{128,0},{192,64},{1,129},{65,193},{129,1},{193,65... | collective-permute-start | bytes 688136 | tf_op jit(solution)/shard_map/ppermute | solution.py:263
  99.3 11.4 %collective-permute-start.11 = (bf16[128,896]{1,0:T(8,128)(2,1)S(1)}, bf16[128,896]{1,0:T(8,128)(2,1)S(1)}, u32[]{:S(2)}, u32[]{:S(2)}) collective-permute-start(bf16[128,896]{1,0:T(8,128)(2,1)S(1)} %get-tuple-element.109), channel_id=1, source_target_pairs={{0,192},{64,128},{128,64},{192,0},{1,193},{65,129},{129,65},{193,1... | collective-permute-start | bytes 688136 | tf_op jit(solution)/shard_map/ppermute | solution.py:263
  101.1 9.6 %collective-permute-start.9 = (bf16[128,896]{1,0:T(8,128)(2,1)S(1)}, bf16[128,896]{1,0:T(8,128)(2,1)S(1)}, u32[]{:S(2)}, u32[]{:S(2)}) collective-permute-start(bf16[128,896]{1,0:T(8,128)(2,1)S(1)} %get-tuple-element.102), channel_id=1, source_target_pairs={{0,64},{64,0},{128,192},{192,128},{1,65},{65,1},{129,193},{193,129... | collective-permute-start | bytes 688136 | tf_op jit(solution)/shard_map/ppermute | solution.py:263
  128.4 8.3 %collective-permute-start.15 = (bf16[7,128,128]{2,1,0:T(8,128)(2,1)S(1)}, bf16[7,128,128]{2,1,0:T(8,128)(2,1)S(1)}, u32[]{:S(2)}, u32[]{:S(2)}) collective-permute-start(bf16[7,128,128]{2,1,0:T(8,128)(2,1)S(1)} %get-tuple-element.116), channel_id=1, source_target_pairs={{0,16},{16,0},{32,48},{48,32},{1,17},{17,1},{33,49},{49,33},{2,18}... | collective-permute-start | bytes 688136 | tf_op jit(solution)/shard_map/ppermute | solution.py:263
  130.9 22.5 %collective-permute-start.12 = (bf16[2,128,896]{2,1,0:T(8,128)(2,1)S(1)}, bf16[2,128,896]{2,1,0:T(8,128)(2,1)S(1)}, u32[]{:S(2)}, u32[]{:S(2)}) collective-permute-start(bf16[2,128,896]{2,1,0:T(8,128)(2,1)S(1)} %get-tuple-element.119.a0), channel_id=1, source_target_pairs={{0,64},{64,0},{128,192},{192,128},{1,65},{65,1},{129,193},{193,129... | collective-permute-start | bytes 1376264 | tf_op jit(solution)/shard_map/ppermute | solution.py:263
  130.9 22.5 %collective-permute-start.13 = (bf16[2,128,896]{2,1,0:T(8,128)(2,1)S(1)}, bf16[2,128,896]{2,1,0:T(8,128)(2,1)S(1)}, u32[]{:S(2)}, u32[]{:S(2)}) collective-permute-start(bf16[2,128,896]{2,1,0:T(8,128)(2,1)S(1)} %get-tuple-element.119.a0), channel_id=1, source_target_pairs={{0,128},{64,192},{128,0},{192,64},{1,129},{65,193},{129,1},{193,65... | collective-permute-start | bytes 1376264 | tf_op jit(solution)/shard_map/ppermute | solution.py:263
  133.4 20.0 %collective-permute-start.14 = (bf16[2,128,896]{2,1,0:T(8,128)(2,1)S(1)}, bf16[2,128,896]{2,1,0:T(8,128)(2,1)S(1)}, u32[]{:S(2)}, u32[]{:S(2)}) collective-permute-start(bf16[2,128,896]{2,1,0:T(8,128)(2,1)S(1)} %get-tuple-element.119.a0), channel_id=1, source_target_pairs={{0,192},{64,128},{128,64},{192,0},{1,193},{65,129},{129,65},{193,1... | collective-permute-start | bytes 1376264 | tf_op jit(solution)/shard_map/ppermute | solution.py:263
  135.6 13.2 %collective-permute-start.16 = (bf16[7,128,128]{2,1,0:T(8,128)(2,1)S(1)}, bf16[7,128,128]{2,1,0:T(8,128)(2,1)S(1)}, u32[]{:S(2)}, u32[]{:S(2)}) collective-permute-start(bf16[7,128,128]{2,1,0:T(8,128)(2,1)S(1)} %get-tuple-element.117), channel_id=1, source_target_pairs={{0,32},{16,48},{32,0},{48,16},{1,33},{17,49},{33,1},{49,17},{2,34}... | collective-permute-start | bytes 688136 | tf_op jit(solution)/shard_map/ppermute | solution.py:263
  136.7 16.7 %collective-permute-start.17 = (bf16[7,128,128]{2,1,0:T(8,128)(2,1)S(1)}, bf16[7,128,128]{2,1,0:T(8,128)(2,1)S(1)}, u32[]{:S(2)}, u32[]{:S(2)}) collective-permute-start(bf16[7,128,128]{2,1,0:T(8,128)(2,1)S(1)} %get-tuple-element.118), channel_id=1, source_target_pairs={{0,48},{16,32},{32,16},{48,0},{1,49},{17,33},{33,17},{49,1},{2,50}... | collective-permute-start | bytes 688136 | tf_op jit(solution)/shard_map/ppermute | solution.py:263
  157.5 5.1 %collective-permute-start.18 = (bf16[4,2,2,128,256]{4,3,2,1,0:T(8,128)(2,1)S(1)}, bf16[4,2,2,128,256]{4,3,2,1,0:T(8,128)(2,1)S(1)}, u32[]{:S(2)}, u32[]{:S(2)}) collective-permute-start(bf16[4,2,2,128,256]{4,3,2,1,0:T(8,128)(2,1)S(1)} %get-tuple-element.133), channel_id=1, source_target_pairs={{0,1},{1,0},{2,3},{3,2},{4,5},{5,4},{6,7},{7,6},{8,9},{9,8},{10,11... | collective-permute-start | bytes 3145736 | tf_op jit(solution)/shard_map/ppermute | solution.py:263
  163.3 9.5 %collective-permute-start.19 = (bf16[2,2,128,256]{3,2,1,0:T(8,128)(2,1)S(1)}, bf16[2,2,128,256]{3,2,1,0:T(8,128)(2,1)S(1)}, u32[]{:S(2)}, u32[]{:S(2)}) collective-permute-start(bf16[2,2,128,256]{3,2,1,0:T(8,128)(2,1)S(1)} %get-tuple-element.135), channel_id=1, source_target_pairs={{0,4},{4,0},{8,12},{12,8},{1,5},{5,1},{9,13},{13,9},{2,6},{6,2},{1... | collective-permute-start | bytes 786440 | tf_op jit(solution)/shard_map/ppermute | solution.py:263
  165.7 30.1 %collective-permute-start.24 = (bf16[2,7,128,128]{3,2,1,0:T(8,128)(2,1)S(1)}, bf16[2,7,128,128]{3,2,1,0:T(8,128)(2,1)S(1)}, u32[]{:S(2)}, u32[]{:S(2)}) collective-permute-start(bf16[2,7,128,128]{3,2,1,0:T(8,128)(2,1)S(1)} %get-tuple-element.131), channel_id=1, source_target_pairs={{0,16},{16,0},{32,48},{48,32},{1,17},{17,1},{33,49},{49,33},{2,18}... | collective-permute-start | bytes 1376264 | tf_op jit(solution)/shard_map/ppermute | solution.py:263
  165.7 36.6 %collective-permute-start.25 = (bf16[2,7,128,128]{3,2,1,0:T(8,128)(2,1)S(1)}, bf16[2,7,128,128]{3,2,1,0:T(8,128)(2,1)S(1)}, u32[]{:S(2)}, u32[]{:S(2)}) collective-permute-start(bf16[2,7,128,128]{3,2,1,0:T(8,128)(2,1)S(1)} %get-tuple-element.143), channel_id=1, source_target_pairs={{0,32},{16,48},{32,0},{48,16},{1,33},{17,49},{33,1},{49,17},{2,34}... | collective-permute-start | bytes 1376264 | tf_op jit(solution)/shard_map/ppermute | solution.py:263
  168.7 45.9 %collective-permute-start.26 = (bf16[2,7,128,128]{3,2,1,0:T(8,128)(2,1)S(1)}, bf16[2,7,128,128]{3,2,1,0:T(8,128)(2,1)S(1)}, u32[]{:S(2)}, u32[]{:S(2)}) collective-permute-start(bf16[2,7,128,128]{3,2,1,0:T(8,128)(2,1)S(1)} %get-tuple-element.144), channel_id=1, source_target_pairs={{0,48},{16,32},{32,16},{48,0},{1,49},{17,33},{33,17},{49,1},{2,50}... | collective-permute-start | bytes 1376264 | tf_op jit(solution)/shard_map/ppermute | solution.py:263
  169.1 9.4 %collective-permute-start.20 = (bf16[2,2,128,256]{3,2,1,0:T(8,128)(2,1)S(1)}, bf16[2,2,128,256]{3,2,1,0:T(8,128)(2,1)S(1)}, u32[]{:S(2)}, u32[]{:S(2)}) collective-permute-start(bf16[2,2,128,256]{3,2,1,0:T(8,128)(2,1)S(1)} %get-tuple-element.136), channel_id=1, source_target_pairs={{0,8},{4,12},{8,0},{12,4},{1,9},{5,13},{9,1},{13,5},{2,10},{6,14},... | collective-permute-start | bytes 786440 | tf_op jit(solution)/shard_map/ppermute | solution.py:263
  172.8 11.2 %collective-permute-start.21 = (bf16[2,2,128,256]{3,2,1,0:T(8,128)(2,1)S(1)}, bf16[2,2,128,256]{3,2,1,0:T(8,128)(2,1)S(1)}, u32[]{:S(2)}, u32[]{:S(2)}) collective-permute-start(bf16[2,2,128,256]{3,2,1,0:T(8,128)(2,1)S(1)} %get-tuple-element.137), channel_id=1, source_target_pairs={{0,12},{4,8},{8,4},{12,0},{1,13},{5,9},{9,5},{13,1},{2,14},{6,10},... | collective-permute-start | bytes 786440 | tf_op jit(solution)/shard_map/ppermute | solution.py:263
  184.8 31.9 %collective-permute-start.22 = (bf16[2,128,256]{2,1,0:T(8,128)(2,1)S(1)}, bf16[2,128,256]{2,1,0:T(8,128)(2,1)S(1)}, u32[]{:S(2)}, u32[]{:S(2)}) collective-permute-start(bf16[2,128,256]{2,1,0:T(8,128)(2,1)S(1)} %get-tuple-element.138), channel_id=1, source_target_pairs={{0,0},{2,2},{4,64},{6,66},{8,128},{10,130},{12,192},{14,194},{64,4... | collective-permute-start | bytes 393224 | tf_op jit(solution)/shard_map/ppermute | solution.py:281
  187.7 29.0 %collective-permute-start.23 = (bf16[2,128,256]{2,1,0:T(8,128)(2,1)S(1)}, bf16[2,128,256]{2,1,0:T(8,128)(2,1)S(1)}, u32[]{:S(2)}, u32[]{:S(2)}) collective-permute-start(bf16[2,128,256]{2,1,0:T(8,128)(2,1)S(1)} %get-tuple-element.139), channel_id=1, source_target_pairs={{0,2},{2,0},{4,66},{6,64},{8,130},{10,128},{12,194},{14,192},{64,6... | collective-permute-start | bytes 393224 | tf_op jit(solution)/shard_map/ppermute | solution.py:281
